TPU v7x, 256 devices: a whole 4x4x8 slice. The times are simulated.
256 devices in a mesh: row: 16 (over y, z_hi), col: 16 (over z_lo, x, core).
Axes of the slice: x: 4, y: 4, z: 8 (z_hi: 4, z_lo: 2; z = z_hi * 2 + z_lo), core: 2. Of those that a mesh axis runs over, the one named last changes fastest.
Arguments:
- pair: bfloat16 [512, 512, 128], P('row', 'col'), may hold values from -400 to 400, as said below
- cotangent: bfloat16 [512, 512, 128], P('row', 'col'), may hold values from -6 to 6
- in_weight: bfloat16 [128, 512], replicated, may hold values from -0.5 to 0.5
- gate_weight: bfloat16 [128, 128], replicated, may hold values from -0.5 to 0.5
- out_weight: bfloat16 [128, 128], replicated, may hold values from -0.5 to 0.5
Outputs:
- pair_grad: bfloat16 [512, 512, 128], P('row', 'col')
- in_grad: float32 [128, 512], replicated
- gate_grad: float32 [128, 128], replicated
- out_grad: float32 [128, 128], replicated
Inputs may be any that keep to these rules, and one draw needn't show every extreme that they name: Each entry is a bounded noise value times a positive scale of its pair and a positive scale of its channel.
All inputs are finite; a program needn't handle non-finite values.
Results may differ from a plain program's by a relative error of at most 0.0088.
Values may be sent and summed in bfloat16 or wider, within the bound.
No kernel may reach another device: no remote copies, remote signals or barrier semaphores. Data moves between devices by JAX's collectives and lax.ppermute only.
A program may use at most 128 MiB of HBM per device.

v0:
```python
import jax
import jax.numpy as jnp
from jax import lax
from jax.experimental import pallas as pl
from jax.experimental.pallas import tpu as pltpu
from jax.sharding import Mesh, PartitionSpec as P

ROW = ("y", "zh")
CHI = ("zl", "x")
OWNERS = ("y", "zh", "zl", "x")
PLANE = ("y", "x", "core")
LINE = ("zh", "zl")
ALL = ("y", "zh", "zl", "x", "core")
SWAP = [(0, 1), (1, 0)]
BF = jnp.bfloat16
F32 = jnp.float32
EPS = 1e-05


def dot(left, right, contract=((1,), (0,))):
    return lax.dot_general(left, right, (contract, ((), ())), preferred_element_type=F32)


def layer_norm(values, axis=-1):
    center = values - jnp.mean(values, axis=axis, keepdims=True)
    scale = lax.rsqrt(jnp.mean(center * center, axis=axis, keepdims=True) + EPS)
    return center * scale, scale


def layer_norm_backward(grad, normal, scale, axis=-1):
    first = jnp.mean(grad, axis=axis, keepdims=True)
    second = jnp.mean(grad * normal, axis=axis, keepdims=True)
    return scale * (grad - first - normal * second)


def regroup(parts):
    lane = lax.broadcasted_iota(jnp.int32, parts[0].shape, 1)
    low = lane < 64
    even = (lane // 32) % 2 == 0
    p0, p1, p2, p3 = parts
    roll = lambda v, n: pltpu.roll(v, n, 1)
    p0, p2 = jnp.where(low, p0, roll(p2, 64)), jnp.where(low, roll(p0, 64), p2)
    p1, p3 = jnp.where(low, p1, roll(p3, 64)), jnp.where(low, roll(p1, 64), p3)
    p0, p1 = jnp.where(even, p0, roll(p1, 32)), jnp.where(even, roll(p0, 96), p1)
    p2, p3 = jnp.where(even, p2, roll(p3, 32)), jnp.where(even, roll(p2, 96), p3)
    return [p0, p1, p2, p3]


def project_kernel(pair_ref, w_ref, msg_ref, held):
    w = w_ref[...]
    for s in range(8):
        zhat, _ = layer_norm(pair_ref[:, s].astype(F32).reshape(128, 128))
        proj = dot(w, zhat.astype(BF), ((0,), (1,)))
        held[pl.ds(s, 128, stride=16), :] = jax.nn.sigmoid(proj[128:256]) * proj[0:128]
        held[pl.ds(8 + s, 128, stride=16), :] = jax.nn.sigmoid(proj[384:512]) * proj[256:384]
    msg_ref[...] = held[...].reshape(128, 16, 128).astype(BF)


def side_kernel(pair_ref, cot_ref, w_ref, gw_ref, ow_ref, fac_ref, norm_ref, g2_ref, dout_ref, dxn_ref):
    w = w_ref[...]
    gw = gw_ref[...]
    ow = ow_ref[...]
    for s in range(8):
        zhat, _ = layer_norm(pair_ref[:, s].astype(F32).reshape(128, 128))
        normed = zhat.astype(BF)
        norm_ref[s] = normed
        proj = dot(w, normed, ((0,), (1,)))
        for n in range(2):
            val = proj[256 * n : 256 * n + 128]
            sig = jax.nn.sigmoid(proj[256 * n + 128 : 256 * n + 256])
            fac_ref[s, 256 * n : 256 * n + 128] = sig
            fac_ref[s, 256 * n + 128 : 256 * n + 256] = val * sig * (1.0 - sig)
        gate = jax.nn.sigmoid(dot(normed, gw))
        upstream = cot_ref[:, s].astype(F32).reshape(128, 128)
        dout = upstream * gate
        g2_ref[s] = dout * (1.0 - gate)
        dout = dout.astype(BF)
        dout_ref[s] = dout
        dxn_ref[pl.ds(s, 128, stride=8), :] = dot(ow, dout, ((1,), (1,)))


def pack_kernel(core_ref, msg_ref, a_ref, b_ref, give_ref):
    core = core_ref[0]
    for t in range(2):
        parts = [msg_ref[:, :, 4 * t + q].astype(F32)[:, :, 0:8].reshape(128, 128) for q in range(4)]
        for g, part in enumerate(regroup(parts)):
            a_ref[pl.ds(128 * g, 128), pl.ds(128 * t, 128)] = part.astype(BF)
        for half in range(2):
            sel = core if half == 0 else 1 - core
            parts = [msg_ref[:, sel, 4 * t + q].astype(F32)[:, 8:16].reshape(64, 128) for q in range(4)]
            parts = [part.reshape(8, 8, 128) for part in regroup(parts)]
            b_ref[half, :, pl.ds(128 * t, 128)] = jnp.stack(parts, axis=1).reshape(256, 128).astype(BF)
    give_ref[...] = dot(a_ref[...], b_ref[1], ((1,), (1,)))


def x_kernel(a_ref, b_ref, got_ref, msg_ref):
    x = dot(a_ref[...], b_ref[0], ((1,), (1,))) + got_ref[...]
    for t in range(2):
        parts = [x[128 * g : 128 * g + 128, 128 * t : 128 * t + 128] for g in range(4)]
        for q, part in enumerate(regroup(parts)):
            msg_ref[:, 4 * t + q] = part.reshape(16, 8, 128).astype(BF)


def dx_kernel(x_ref, dxn_ref, msg_ref, xhat_ref):
    xhat, xinv = layer_norm(x_ref[...].astype(F32), 0)
    xhat_ref[...] = xhat
    msg_ref[...] = layer_norm_backward(dxn_ref[...], xhat, xinv, 0).astype(BF)


def gate_kernel(xhat_ref, norm_ref, g2_ref, dout_ref, gw_ref, ow_ref, gate_ref, out_ref, dn_ref):
    gw = gw_ref[...]
    ow = ow_ref[...]
    gate_part = jnp.zeros((128, 128), F32)
    out_part = jnp.zeros((128, 128), F32)
    for s in range(8):
        xnorm = xhat_ref[pl.ds(s, 128, stride=8), :].astype(BF)
        dgate = (g2_ref[s] * dot(xnorm, ow, ((0,), (0,)))).astype(BF)
        gate_part += dot(norm_ref[s], dgate, ((0,), (0,)))
        out_part += dot(xnorm, dout_ref[s])
        dn_ref[s] = dot(dgate, gw, ((1,), (1,)))
    gate_ref[...] = gate_part
    out_ref[...] = out_part


def pull_kernel(core_ref, own_ref, other_ref, a_ref, b_ref, msg_ref, dx, held):
    core = core_ref[0]
    for half, ref in enumerate((own_ref, other_ref)):
        for t in range(2):
            parts = [ref[:, 4 * t + q].astype(F32).reshape(128, 128) for q in range(4)]
            for g, part in enumerate(regroup(parts)):
                dx[half, pl.ds(128 * g, 128), pl.ds(128 * t, 128)] = part.astype(BF)
    da = dot(dx[0], b_ref[0]) + dot(dx[1], b_ref[1])
    for t in range(2):
        parts = [da[128 * g : 128 * g + 128, 128 * t : 128 * t + 128] for g in range(4)]
        for q, part in enumerate(regroup(parts)):
            held[:, :, 4 * t + q, 0:8] = part.reshape(8, 2, 8, 128)
    for half in range(2):
        sel = core if half == 0 else 1 - core
        db = dot(dx[half], a_ref[...], ((0,), (0,))).reshape(8, 4, 8, 256)
        for t in range(2):
            parts = [db[:, g, :, 128 * t : 128 * t + 128].reshape(64, 128) for g in range(4)]
            for q, part in enumerate(regroup(parts)):
                held[:, sel, 4 * t + q, 8:16] = part.reshape(8, 8, 128)
    msg_ref[...] = held[...].astype(BF)


def weight_kernel(dab_ref, fac_ref, norm_ref, gate_ref, out_ref, sum_ref, dproj_ref, held):
    held[...] = dab_ref[...].astype(F32).reshape(2048, 128)
    total = jnp.zeros((512, 128), F32)
    for s in range(8):
        da = held[pl.ds(s, 128, stride=16), :]
        db = held[pl.ds(8 + s, 128, stride=16), :]
        fac = fac_ref[s]
        dproj = jnp.concatenate(
            [da * fac[0:128], da * fac[128:256], db * fac[256:384], db * fac[384:512]], axis=0
        ).astype(BF)
        dproj_ref[s] = dproj
        total += dot(dproj, norm_ref[s])
    sum_ref[0:512] = total
    sum_ref[512:640] = gate_ref[...]
    sum_ref[640:768] = out_ref[...]


def pair_kernel(dproj_ref, w_ref, dn_ref, pair_ref, out_ref):
    w = w_ref[...]
    for s in range(8):
        zhat, zinv = layer_norm(pair_ref[:, s].astype(F32).reshape(128, 128))
        dnormed = dot(dproj_ref[s], w, ((0,), (1,))) + dn_ref[s]
        grad = layer_norm_backward(dnormed, zhat, zinv)
        out_ref[:, s] = grad.reshape(4, 32, 128).astype(BF)


def run(kernel, outs, *args, scratch=(), scalars=0, flops=0):
    outs = [jax.ShapeDtypeStruct(shape, dtype) for shape, dtype in outs]
    vmem = pl.BlockSpec(memory_space=pltpu.VMEM)
    smem = pl.BlockSpec(memory_space=pltpu.SMEM)
    size = sum(v.size * v.dtype.itemsize for v in list(args) + outs)
    result = pl.pallas_call(
        kernel,
        out_shape=outs,
        in_specs=[smem] * scalars + [vmem] * (len(args) - scalars),
        out_specs=[vmem] * len(outs),
        scratch_shapes=scratch,
        compiler_params=pltpu.CompilerParams(vmem_limit_bytes=24 * 1024 * 1024),
        cost_estimate=pl.CostEstimate(flops=flops, bytes_accessed=size, transcendentals=0),
    )(*args)
    return result[0] if len(outs) == 1 else result


def exchange(values, axes):
    return lax.all_to_all(values, axes, 0, 0, tiled=True)


def per_device(pair, cotangent, in_weight, gate_weight, out_weight):
    core = jnp.reshape(lax.axis_index("core"), (1,)).astype(jnp.int32)
    total = 512
    pair = pair.reshape(4, 8, 32, 128)
    cotangent = cotangent.reshape(4, 8, 32, 128)

    msg = run(
        project_kernel, [((128, 16, 128), BF)], pair, in_weight,
        scratch=[pltpu.VMEM((2048, 128), F32)], flops=134_000_000,
    )
    msg = exchange(msg, OWNERS).reshape(8, 2, 8, 16, 128)
    factors, normed, g2, dout, dxnorm = run(
        side_kernel,
        [((8, 512, 128), F32), ((8, 128, 128), BF), ((8, 128, 128), F32), ((8, 128, 128), BF), ((1024, 128), F32)],
        pair, cotangent, in_weight, gate_weight, out_weight, flops=200_000_000,
    )
    a_own, b_own, give = run(
        pack_kernel, [((512, 256), BF), ((2, 256, 256), BF), ((512, 256), F32)],
        core, msg, scalars=1, flops=67_000_000,
    )
    got = lax.ppermute(give, "core", SWAP)
    x = run(x_kernel, [((16, 8, 8, 128), BF)], a_own, b_own, got, flops=67_000_000)
    x = exchange(x.reshape(128, 8, 128), OWNERS)
    dx, xhat = run(
        dx_kernel, [((128, 8, 128), BF), ((128, 8, 128), F32)], x, dxnorm.reshape(128, 8, 128), flops=1_000_000
    )
    own = exchange(dx, OWNERS)
    gate_part, out_part, dn_gate = run(
        gate_kernel,
        [((128, 128), F32), ((128, 128), F32), ((8, 128, 128), F32)],
        xhat.reshape(1024, 128), normed, g2, dout, gate_weight, out_weight, flops=134_000_000,
    )
    other = lax.ppermute(own, "core", SWAP)
    dab = run(
        pull_kernel, [((8, 2, 8, 16, 128), BF)],
        core, own.reshape(16, 8, 8, 128), other.reshape(16, 8, 8, 128), a_own, b_own,
        scratch=[pltpu.VMEM((2, 512, 256), BF), pltpu.VMEM((8, 2, 8, 16, 128), F32)], scalars=1, flops=268_000_000,
    )
    dab = exchange(dab.reshape(128, 16, 128), OWNERS)
    parts, dproj = run(
        weight_kernel, [((768, 128), F32), ((8, 512, 128), BF)],
        dab, factors, normed, gate_part, out_part, scratch=[pltpu.VMEM((2048, 128), F32)], flops=134_000_000,
    )
    parts = jnp.sum(exchange(parts.reshape(32, 24, 128), PLANE), axis=0, keepdims=True)
    pair_grad = run(
        pair_kernel, [((4, 8, 32, 128), BF)], dproj, in_weight, dn_gate, pair, flops=134_000_000
    )
    parts = jnp.sum(exchange(jnp.broadcast_to(parts, (8, 24, 128)), LINE), axis=0, keepdims=True) / total
    whole = exchange(jnp.broadcast_to(parts, (32, 24, 128)), PLANE).reshape(768, 128)
    return (pair_grad.reshape(32, 32, 128), whole[0:512].T, whole[512:640], whole[640:768])


def solution(mesh):
    fine = Mesh(mesh.devices.reshape(4, 4, 2, 4, 2), ALL)
    tiles = P(ROW, CHI + ("core",), None)
    return jax.shard_map(
        per_device,
        mesh=fine,
        in_specs=(tiles, tiles, P(), P(), P()),
        out_specs=(tiles, P(), P(), P()),
        check_vma=False,
    )
```

profile of v0, /device:TPU:1, one launch (start us, length us, event | category | flops | bytes accessed | tf_op | source)
XLA Modules:
  0.0 164.1 jit_solution(12083483676448017171)
XLA Ops:
  2.5 1.9 %shard_map.84 = bf16[128,16,128]{2,1,0:T(8,128)(2,1)} custom-call(bf16[4,8,32,128]{3,2,1,0:T(8,128)(2,1)S(1)} %bitcast.16, bf16[128,512]{1,0:T(8,128)(2,1)S(1)} %copy-done.10), custom_call_target="tpu_custom_call" | custom-call | flops 134000000 | bytes 917504 | tf_op jit(solution)/shard_map/pallas_call | solution.py:178
  4.4 16.3 %all-to-all-start = ((bf16[128,16,128]{2,1,0:T(8,128)(2,1)}), bf16[128,16,128]{2,1,0:T(8,128)(2,1)S(1)}, u32[]{:S(2)}, u32[]{:S(2)}) async-start(bf16[128,16,128]{2,1,0:T(8,128)(2,1)} %shard_map.84), calls=%async_computation | async-start | bytes 1048576 | tf_op jit(solution)/shard_map/all_to_all | solution.py:191
  20.8 16.9 %all-to-all-done = bf16[128,16,128]{2,1,0:T(8,128)(2,1)S(1)} async-done(((bf16[128,16,128]{2,1,0:T(8,128)(2,1)}), bf16[128,16,128]{2,1,0:T(8,128)(2,1)S(1)}, u32[]{:S(2)}, u32[]{:S(2)}) %all-to-all-start) | async-done | bytes 524320 | tf_op jit(solution)/shard_map/all_to_all | solution.py:191
  38.4 3.5 %collective-permute-start = (f32[512,256]{1,0:T(8,128)S(1)}, f32[512,256]{1,0:T(8,128)S(1)}, u32[]{:S(2)}, u32[]{:S(2)}) collective-permute-start(f32[512,256]{1,0:T(8,128)S(1)} %get-tuple-element.21), channel_id=1, source_target_pairs={{0,1},{1,0},{2,3},{3,2},{4,5},{5,4},{6,7},{7,6},{8,9},{9,8},{10,11... | collective-permute-start | bytes 1572872 | tf_op jit(solution)/shard_map/ppermute | solution.py:214
  41.9 1.5 collective-permute-done.got_ref
  43.4 1.1 shard_map.86
  44.5 6.7 %all-to-all-start.1 = ((bf16[128,8,128]{2,1,0:T(8,128)(2,1)}), bf16[128,8,128]{2,1,0:T(8,128)(2,1)S(1)}, u32[]{:S(2)}, u32[]{:S(2)}) async-start(bf16[128,8,128]{2,1,0:T(8,128)(2,1)} %bitcast.3), calls=%async_computation.1 | async-start | bytes 524288 | tf_op jit(solution)/shard_map/all_to_all | solution.py:191
  53.7 1.5 shard_map.87
  57.5 6.7 %all-to-all-done.1.x_ref = bf16[128,8,128]{2,1,0:T(8,128)(2,1)S(1)} async-done(((bf16[128,8,128]{2,1,0:T(8,128)(2,1)}), bf16[128,8,128]{2,1,0:T(8,128)(2,1)S(1)}, u32[]{:S(2)}, u32[]{:S(2)}) %all-to-all-start.1) | async-done | bytes 262176 | tf_op jit(solution)/shard_map/all_to_all | solution.py:191
  64.2 1.0 copy-done.13
  65.8 18.7 %all_to_all.35 = bf16[128,8,128]{2,1,0:T(8,128)(2,1)S(1)} all-to-all(bf16[128,8,128]{2,1,0:T(8,128)(2,1)S(1)} %get-tuple-element.23), channel_id=1, replica_groups=mesh['y'=4,'zh'=4,'zl'=2,'x'=4,'core'=2] {'y','zh','zl','x'}, dimensions={0} | all-to-all | bytes 524288 | tf_op jit(solution)/shard_map/all_to_all | solution.py:191
  84.4 3.7 %collective-permute-start.1 = (bf16[128,8,128]{2,1,0:T(8,128)(2,1)S(1)}, bf16[128,8,128]{2,1,0:T(8,128)(2,1)S(1)}, u32[]{:S(2)}, u32[]{:S(2)}) collective-permute-start(bf16[128,8,128]{2,1,0:T(8,128)(2,1)S(1)} %all_to_all.35), channel_id=1, source_target_pairs={{0,1},{1,0},{2,3},{3,2},{4,5},{5,4},{6,7},{7,6},{8,9},{9,8},{10,11... | collective-permute-start | bytes 786440 | tf_op jit(solution)/shard_map/ppermute | solution.py:226
  88.1 1.2 collective-permute-done.1
  89.3 2.5 %shard_map.89 = bf16[8,2,8,16,128]{4,3,2,1,0:T(8,128)(2,1)} custom-call(s32[1]{0:T(128)} %bitcast.core_ref, bf16[16,8,8,128]{3,2,1,0:T(8,128)(2,1)S(1)} %bitcast.19, bf16[16,8,8,128]{3,2,1,0:T(8,128)(2,1)S(1)} %bitcast.23, bf16[512,256]{1,0:T(8,128)(2,1)S(1)} %get-tuple-element.19.a_ref, bf16[2,256,256]{2,1,0:T(8,128)(2,1)S(1)} %get-tuple-element.20.b_ref), custom_call_target="tpu_custom_call" | custom-call | flops 268000000 | bytes 1572868 | tf_op jit(solution)/shard_map/pallas_call | solution.py:178
  91.8 6.3 %all-to-all-start.3 = ((bf16[128,16,128]{2,1,0:T(8,128)(2,1)}), bf16[128,16,128]{2,1,0:T(8,128)(2,1)S(1)}, u32[]{:S(2)}, u32[]{:S(2)}) async-start(bf16[128,16,128]{2,1,0:T(8,128)(2,1)} %bitcast.8), calls=%async_computation.3 | async-start | bytes 1048576 | tf_op jit(solution)/shard_map/all_to_all | solution.py:191
  98.2 1.0 copy-done.7
  99.2 1.0 copy-done.9
  102.7 1.1 shard_map.90
  105.9 10.0 %all-to-all-done.3.dab_ref = bf16[128,16,128]{2,1,0:T(8,128)(2,1)S(1)} async-done(((bf16[128,16,128]{2,1,0:T(8,128)(2,1)}), bf16[128,16,128]{2,1,0:T(8,128)(2,1)S(1)}, u32[]{:S(2)}, u32[]{:S(2)}) %all-to-all-start.3) | async-done | bytes 524320 | tf_op jit(solution)/shard_map/all_to_all | solution.py:191
  119.2 17.0 %all_to_all.36 = f32[32,24,128]{2,1,0:T(8,128)S(1)} all-to-all(f32[32,24,128]{2,1,0:T(8,128)S(1)} %bitcast.22), channel_id=1, replica_groups=mesh['y'=4,'zh'=4,'zl'=2,'x'=4,'core'=2] {'y','x','core'}, dimensions={0} | all-to-all | bytes 786432 | tf_op jit(solution)/shard_map/all_to_all | solution.py:191
  136.3 10.0 %all_to_all.37 = f32[8,24,128]{2,1,0:T(8,128)S(1)} all-to-all(f32[8,24,128]{2,1,0:T(8,128)S(1)} %broadcast_in_dim.4), channel_id=1, replica_groups=mesh['y'=4,'zh'=4,'zl'=2,'x'=4,'core'=2] {'zh','zl'}, dimensions={0} | all-to-all | bytes 196608 | tf_op jit(solution)/shard_map/all_to_all | solution.py:191
  147.1 5.3 %all-to-all-start.6 = ((f32[32,24,128]{2,1,0:T(8,128)}), f32[32,24,128]{2,1,0:T(8,128)S(1)}, u32[]{:S(2)}, u32[]{:S(2)}) async-start(f32[32,24,128]{2,1,0:T(8,128)} %broadcast_in_dim.5), calls=%async_computation.6 | async-start | bytes 786432 | tf_op jit(solution)/shard_map/all_to_all | solution.py:191
  152.4 2.4 %shard_map.92 = bf16[4,8,32,128]{3,2,1,0:T(8,128)(2,1)} custom-call(bf16[8,512,128]{2,1,0:T(8,128)(2,1)S(1)} %copy-done.3, bf16[128,512]{1,0:T(8,128)(2,1)S(1)} %copy-done.11, f32[8,128,128]{2,1,0:T(8,128)S(1)} %copy-done.5, bf16[4,8,32,128]{3,2,1,0:T(8,128)(2,1)S(1)} %bitcast.18), custom_call_target="tpu_custom_call" | custom-call | flops 134000000 | bytes 2228224 | tf_op jit(solution)/shard_map/pallas_call | solution.py:178
  154.8 7.8 %all-to-all-done.6 = f32[32,24,128]{2,1,0:T(8,128)S(1)} async-done(((f32[32,24,128]{2,1,0:T(8,128)}), f32[32,24,128]{2,1,0:T(8,128)S(1)}, u32[]{:S(2)}, u32[]{:S(2)}) %all-to-all-start.6) | async-done | bytes 393248 | tf_op jit(solution)/shard_map/all_to_all | solution.py:191
  (58 shorter events, 18.0 us)
Async XLA Ops:
  0.6 1.0 copy-start
  1.6 0.9 copy-start.10
  2.5 48.7 %copy-start.1 = (bf16[32,32,128]{2,1,0:T(8,128)(2,1)S(1)}, bf16[32,32,128]{2,1,0:T(8,128)(2,1)}, u32[]{:S(2)}) copy-start(bf16[32,32,128]{2,1,0:T(8,128)(2,1)} %param.5) | copy-start | bytes 786436
  2.5 48.8 %copy-start.11 = (bf16[128,512]{1,0:T(8,128)(2,1)S(1)}, bf16[128,512]{1,0:T(8,128)(2,1)}, u32[]{:S(2)}) copy-start(bf16[128,512]{1,0:T(8,128)(2,1)} %w_ref.5) | copy-start | bytes 393220
  4.4 33.2 %all-to-all-start = ((bf16[128,16,128]{2,1,0:T(8,128)(2,1)}), bf16[128,16,128]{2,1,0:T(8,128)(2,1)S(1)}, u32[]{:S(2)}, u32[]{:S(2)}) async-start(bf16[128,16,128]{2,1,0:T(8,128)(2,1)} %shard_map.84), calls=%async_computation | async-start | bytes 1048576 | tf_op jit(solution)/shard_map/all_to_all | solution.py:191
  38.4 5.0 %collective-permute-start = (f32[512,256]{1,0:T(8,128)S(1)}, f32[512,256]{1,0:T(8,128)S(1)}, u32[]{:S(2)}, u32[]{:S(2)}) collective-permute-start(f32[512,256]{1,0:T(8,128)S(1)} %get-tuple-element.21), channel_id=1, source_target_pairs={{0,1},{1,0},{2,3},{3,2},{4,5},{5,4},{6,7},{7,6},{8,9},{9,8},{10,11... | collective-permute-start | bytes 1572872 | tf_op jit(solution)/shard_map/ppermute | solution.py:214
  44.5 19.7 %all-to-all-start.1 = ((bf16[128,8,128]{2,1,0:T(8,128)(2,1)}), bf16[128,8,128]{2,1,0:T(8,128)(2,1)S(1)}, u32[]{:S(2)}, u32[]{:S(2)}) async-start(bf16[128,8,128]{2,1,0:T(8,128)(2,1)} %bitcast.3), calls=%async_computation.1 | async-start | bytes 524288 | tf_op jit(solution)/shard_map/all_to_all | solution.py:191
  52.8 0.9 copy-start.24
  55.2 0.8 copy-start.6
  56.0 0.8 copy-start.12
  64.2 1.0 copy-start.13
  65.8 23.5 %copy-start.8 = (f32[128,8,128]{2,1,0:T(8,128)}, f32[128,8,128]{2,1,0:T(8,128)S(1)}, u32[]{:S(2)}) copy-start(f32[128,8,128]{2,1,0:T(8,128)S(1)} %get-tuple-element.26) | copy-start | bytes 1572868
  84.4 4.8 %collective-permute-start.1 = (bf16[128,8,128]{2,1,0:T(8,128)(2,1)S(1)}, bf16[128,8,128]{2,1,0:T(8,128)(2,1)S(1)}, u32[]{:S(2)}, u32[]{:S(2)}) collective-permute-start(bf16[128,8,128]{2,1,0:T(8,128)(2,1)S(1)} %all_to_all.35), channel_id=1, source_target_pairs={{0,1},{1,0},{2,3},{3,2},{4,5},{5,4},{6,7},{7,6},{8,9},{9,8},{10,11... | collective-permute-start | bytes 786440 | tf_op jit(solution)/shard_map/ppermute | solution.py:226
  91.8 24.1 %all-to-all-start.3 = ((bf16[128,16,128]{2,1,0:T(8,128)(2,1)}), bf16[128,16,128]{2,1,0:T(8,128)(2,1)S(1)}, u32[]{:S(2)}, u32[]{:S(2)}) async-start(bf16[128,16,128]{2,1,0:T(8,128)(2,1)} %bitcast.8), calls=%async_computation.3 | async-start | bytes 1048576 | tf_op jit(solution)/shard_map/all_to_all | solution.py:191
  98.2 1.0 copy-start.7
  99.2 1.0 copy-start.9
  100.3 0.9 copy-start.15
  103.9 0.8 copy-start.4
  115.9 0.8 copy-start.17
  116.7 0.8 copy-start.19
  118.2 1.0 copy-start.2
  119.2 33.1 %copy-start.5 = (f32[8,128,128]{2,1,0:T(8,128)S(1)}, f32[8,128,128]{2,1,0:T(8,128)}, u32[]{:S(2)}) copy-start(f32[8,128,128]{2,1,0:T(8,128)} %copy-done.4) | copy-start | bytes 1572868
  119.2 33.2 %copy-start.3 = (bf16[8,512,128]{2,1,0:T(8,128)(2,1)S(1)}, bf16[8,512,128]{2,1,0:T(8,128)(2,1)}, u32[]{:S(2)}) copy-start(bf16[8,512,128]{2,1,0:T(8,128)(2,1)} %copy-done.2) | copy-start | bytes 3145732
  147.1 15.5 %all-to-all-start.6 = ((f32[32,24,128]{2,1,0:T(8,128)}), f32[32,24,128]{2,1,0:T(8,128)S(1)}, u32[]{:S(2)}, u32[]{:S(2)}) async-start(f32[32,24,128]{2,1,0:T(8,128)} %broadcast_in_dim.5), calls=%async_computation.6 | async-start | bytes 786432 | tf_op jit(solution)/shard_map/all_to_all | solution.py:191
  (7 other events, 5.0 us)
where the time goes:
time: 165 us; the launch traced here: 164 us
  blocking collectives  45.7 us (28%)
  waiting for transfers between devices  44.1 us (27%)
  starting transfers between devices  41.8 us (25%)
  local copies, waits for them, and re-layouts  19.2 us (12%)
  Pallas kernels  12.5 us (8%)
    all_to_all x3, blocking collectives, exchange(): return lax.all_to_all(values, axes, 0, 0, tiled=True)  45.7 us
    all_to_all x4, waiting for transfers between devices, exchange(): return lax.all_to_all(values, axes, 0, 0, tiled=True)  41.4 us
    all_to_all x4, starting transfers between devices, exchange(): return lax.all_to_all(values, axes, 0, 0, tiled=True)  34.7 us
    unnamed x51, local copies, waits for them, and re-layouts  17.7 us
    pallas_call x9, Pallas kernels, run(): pl.pallas_call(kernel, out_shape=outs, in_specs=[smem] * scalars + [vmem]...  12.5 us
    ppermute x1, starting transfers between devices, per_device(): other = lax.ppermute(own, 'core', SWAP)  3.67 us
    ppermute x1, starting transfers between devices, per_device(): got = lax.ppermute(give, 'core', SWAP)  3.49 us
  transfers between devices with their start and end apart: 6, of which 6 were waited for; matrix products, arithmetic and copies ran while one was open for 0% of the time, Pallas kernels for 3%

commit v1 on v0

v1 whole, which is shorter than its diff:
```python
import jax
import jax.numpy as jnp
from jax import lax
from jax.experimental import pallas as pl
from jax.experimental.pallas import tpu as pltpu
from jax.sharding import Mesh, PartitionSpec as P

ROW = ("y", "zh")
CHI = ("zl", "x")
OWNERS = ("zl", "y", "zh", "x")
PLANE = ("core", "y", "x")
LINE = ("zh", "zl")
ALL = ("y", "zh", "zl", "x", "core")
SWAP = [(0, 1), (1, 0)]
BF = jnp.bfloat16
F32 = jnp.float32
EPS = 1e-05


def dot(left, right, contract=((1,), (0,))):
    return lax.dot_general(left, right, (contract, ((), ())), preferred_element_type=F32)


def layer_norm(values, axis=-1):
    center = values - jnp.mean(values, axis=axis, keepdims=True)
    scale = lax.rsqrt(jnp.mean(center * center, axis=axis, keepdims=True) + EPS)
    return center * scale, scale


def layer_norm_backward(grad, normal, scale, axis=-1):
    first = jnp.mean(grad, axis=axis, keepdims=True)
    second = jnp.mean(grad * normal, axis=axis, keepdims=True)
    return scale * (grad - first - normal * second)


def regroup(parts):
    lane = lax.broadcasted_iota(jnp.int32, parts[0].shape, 1)
    low = lane < 64
    even = (lane // 32) % 2 == 0
    p0, p1, p2, p3 = parts
    roll = lambda v, n: pltpu.roll(v, n, 1)
    p0, p2 = jnp.where(low, p0, roll(p2, 64)), jnp.where(low, roll(p0, 64), p2)
    p1, p3 = jnp.where(low, p1, roll(p3, 64)), jnp.where(low, roll(p1, 64), p3)
    p0, p1 = jnp.where(even, p0, roll(p1, 32)), jnp.where(even, roll(p0, 96), p1)
    p2, p3 = jnp.where(even, p2, roll(p3, 32)), jnp.where(even, roll(p2, 96), p3)
    return [p0, p1, p2, p3]


def project_kernel(pair_ref, w_ref, msg_ref, norm_ref, held):
    w = w_ref[...]
    for s in range(8):
        zhat, _ = layer_norm(pair_ref[:, s].astype(F32).reshape(128, 128))
        normed = zhat.astype(BF)
        norm_ref[s] = normed
        proj = dot(w, normed, ((0,), (1,)))
        held[pl.ds(s, 128, stride=16), :] = jax.nn.sigmoid(proj[128:256]) * proj[0:128]
        held[pl.ds(8 + s, 128, stride=16), :] = jax.nn.sigmoid(proj[384:512]) * proj[256:384]
    msg_ref[...] = held[...].reshape(128, 16, 128).astype(BF)


def side_kernel(norm_ref, cot_ref, gw_ref, ow_ref, g2_ref, dout_ref, dxn_ref):
    gw = gw_ref[...]
    ow = ow_ref[...]
    for s in range(8):
        gate = jax.nn.sigmoid(dot(norm_ref[s], gw))
        upstream = cot_ref[:, s].astype(F32).reshape(128, 128)
        dout = upstream * gate
        g2_ref[s] = dout * (1.0 - gate)
        dout = dout.astype(BF)
        dout_ref[s] = dout
        dxn_ref[pl.ds(s, 128, stride=8), :] = dot(ow, dout, ((1,), (1,)))


def pack_kernel(core_ref, msg_ref, a_ref, b_ref, give_ref):
    core = core_ref[0]
    for t in range(2):
        parts = [msg_ref[t, :, :, q].astype(F32)[:, :, 0:8].reshape(128, 128) for q in range(4)]
        for g, part in enumerate(regroup(parts)):
            a_ref[pl.ds(128 * g, 128), pl.ds(128 * t, 128)] = part.astype(BF)
        for half in range(2):
            sel = core if half == 0 else 1 - core
            parts = [msg_ref[t, :, sel, q].astype(F32)[:, 8:16].reshape(64, 128) for q in range(4)]
            parts = [part.reshape(8, 8, 128) for part in regroup(parts)]
            b_ref[half, :, pl.ds(128 * t, 128)] = jnp.stack(parts, axis=1).reshape(256, 128).astype(BF)
    give_ref[...] = dot(a_ref[...], b_ref[1], ((1,), (1,)))


def x_kernel(a_ref, b_ref, got_ref, msg_ref):
    x = dot(a_ref[...], b_ref[0], ((1,), (1,))) + got_ref[...]
    for t in range(2):
        parts = [x[128 * g : 128 * g + 128, 128 * t : 128 * t + 128] for g in range(4)]
        for q, part in enumerate(regroup(parts)):
            msg_ref[t, :, q] = part.reshape(16, 8, 128).astype(BF)


def dx_kernel(x_ref, dxn_ref, msg_ref, xhat_ref):
    xhat, xinv = layer_norm(x_ref[...].astype(F32), 0)
    xhat_ref[...] = xhat
    msg_ref[...] = layer_norm_backward(dxn_ref[...], xhat, xinv, 0).astype(BF)


def late_kernel(xhat_ref, norm_ref, g2_ref, dout_ref, w_ref, gw_ref, ow_ref, sum_ref, dn_ref, fac_ref):
    w = w_ref[...]
    gw = gw_ref[...]
    ow = ow_ref[...]
    gate_part = jnp.zeros((128, 128), F32)
    out_part = jnp.zeros((128, 128), F32)
    for s in range(8):
        normed = norm_ref[s]
        xnorm = xhat_ref[pl.ds(s, 128, stride=8), :].astype(BF)
        dgate = (g2_ref[s] * dot(xnorm, ow, ((0,), (0,)))).astype(BF)
        gate_part += dot(normed, dgate, ((0,), (0,)))
        out_part += dot(xnorm, dout_ref[s])
        dn_ref[s] = dot(dgate, gw, ((1,), (1,)))
        proj = dot(w, normed, ((0,), (1,)))
        for n in range(2):
            val = proj[256 * n : 256 * n + 128]
            sig = jax.nn.sigmoid(proj[256 * n + 128 : 256 * n + 256])
            fac_ref[s, 256 * n : 256 * n + 128] = sig
            fac_ref[s, 256 * n + 128 : 256 * n + 256] = val * sig * (1.0 - sig)
    sum_ref[0:128] = gate_part
    sum_ref[128:256] = out_part


def pull_kernel(core_ref, own_ref, other_ref, a_ref, b_ref, msg_ref, dx, held):
    core = core_ref[0]
    for half, ref in enumerate((own_ref, other_ref)):
        for t in range(2):
            parts = [ref[t, :, q].astype(F32).reshape(128, 128) for q in range(4)]
            for g, part in enumerate(regroup(parts)):
                dx[half, pl.ds(128 * g, 128), pl.ds(128 * t, 128)] = part.astype(BF)
    da = dot(dx[0], b_ref[0]) + dot(dx[1], b_ref[1])
    for t in range(2):
        parts = [da[128 * g : 128 * g + 128, 128 * t : 128 * t + 128] for g in range(4)]
        for q, part in enumerate(regroup(parts)):
            held[t, :, :, q, 0:8] = part.reshape(8, 2, 8, 128)
    for half in range(2):
        sel = core if half == 0 else 1 - core
        db = dot(dx[half], a_ref[...], ((0,), (0,))).reshape(8, 4, 8, 256)
        for t in range(2):
            parts = [db[:, g, :, 128 * t : 128 * t + 128].reshape(64, 128) for g in range(4)]
            for q, part in enumerate(regroup(parts)):
                held[t, :, sel, q, 8:16] = part.reshape(8, 8, 128)
    msg_ref[...] = held[...].astype(BF)


def weight_kernel(dab_ref, fac_ref, norm_ref, gate_out_ref, sum_ref, dproj_ref, held):
    held[...] = dab_ref[...].astype(F32).reshape(2048, 128)
    total = jnp.zeros((512, 128), F32)
    for s in range(8):
        da = held[pl.ds(s, 128, stride=16), :]
        db = held[pl.ds(8 + s, 128, stride=16), :]
        fac = fac_ref[s]
        dproj = jnp.concatenate(
            [da * fac[0:128], da * fac[128:256], db * fac[256:384], db * fac[384:512]], axis=0
        ).astype(BF)
        dproj_ref[s] = dproj
        total += dot(dproj, norm_ref[s])
    sum_ref[0:512] = total.astype(BF)
    sum_ref[512:768] = gate_out_ref[...].astype(BF)


def pair_kernel(dproj_ref, w_ref, dn_ref, pair_ref, out_ref):
    w = w_ref[...]
    for s in range(8):
        zhat, zinv = layer_norm(pair_ref[:, s].astype(F32).reshape(128, 128))
        dnormed = dot(dproj_ref[s], w, ((0,), (1,))) + dn_ref[s]
        grad = layer_norm_backward(dnormed, zhat, zinv)
        out_ref[:, s] = grad.reshape(4, 32, 128).astype(BF)


def collect_kernel(rows_ref, in_ref, gate_ref, out_ref):
    in_ref[...] = rows_ref[0:512].astype(F32).T
    gate_ref[...] = rows_ref[512:640].astype(F32)
    out_ref[...] = rows_ref[640:768].astype(F32)


def run(kernel, outs, *args, scratch=(), scalars=0, flops=0):
    outs = [jax.ShapeDtypeStruct(shape, dtype) for shape, dtype in outs]
    vmem = pl.BlockSpec(memory_space=pltpu.VMEM)
    smem = pl.BlockSpec(memory_space=pltpu.SMEM)
    size = sum(v.size * v.dtype.itemsize for v in list(args) + outs)
    result = pl.pallas_call(
        kernel,
        out_shape=outs,
        in_specs=[smem] * scalars + [vmem] * (len(args) - scalars),
        out_specs=[vmem] * len(outs),
        scratch_shapes=scratch,
        compiler_params=pltpu.CompilerParams(vmem_limit_bytes=16 * 1024 * 1024),
        cost_estimate=pl.CostEstimate(flops=flops, bytes_accessed=size, transcendentals=0),
    )(*args)
    return result[0] if len(outs) == 1 else result


def exchange(values, axes):
    return lax.all_to_all(values, axes, 0, 0, tiled=True)


def per_device(pair, cotangent, in_weight, gate_weight, out_weight):
    core = jnp.reshape(lax.axis_index("core"), (1,)).astype(jnp.int32)
    total = 512
    pair = pair.reshape(4, 8, 32, 128)
    cotangent = cotangent.reshape(4, 8, 32, 128)

    msg, normed = run(
        project_kernel, [((128, 16, 128), BF), ((8, 128, 128), BF)], pair, in_weight,
        scratch=[pltpu.VMEM((2048, 128), F32)], flops=134_000_000,
    )
    msg = exchange(msg, OWNERS).reshape(2, 8, 2, 4, 16, 128)
    g2, dout, dxnorm = run(
        side_kernel, [((8, 128, 128), F32), ((8, 128, 128), BF), ((1024, 128), F32)],
        normed, cotangent, gate_weight, out_weight, flops=67_000_000,
    )
    a_own, b_own, give = run(
        pack_kernel, [((512, 256), BF), ((2, 256, 256), BF), ((512, 256), F32)],
        core, msg, scalars=1, flops=67_000_000,
    )
    got = lax.ppermute(give, "core", SWAP)
    x = run(x_kernel, [((2, 16, 4, 8, 128), BF)], a_own, b_own, got, flops=67_000_000)
    x = exchange(x.reshape(128, 8, 128), OWNERS)
    dx, xhat = run(
        dx_kernel, [((128, 8, 128), BF), ((128, 8, 128), F32)], x, dxnorm.reshape(128, 8, 128), flops=1_000_000
    )
    own = exchange(dx, OWNERS)
    sums, dn_gate, factors = run(
        late_kernel, [((256, 128), F32), ((8, 128, 128), F32), ((8, 512, 128), F32)],
        xhat.reshape(1024, 128), normed, g2, dout, in_weight, gate_weight, out_weight, flops=268_000_000,
    )
    other = lax.ppermute(own, "core", SWAP)
    dab = run(
        pull_kernel, [((2, 8, 2, 4, 16, 128), BF)],
        core, own.reshape(2, 16, 4, 8, 128), other.reshape(2, 16, 4, 8, 128), a_own, b_own,
        scratch=[pltpu.VMEM((2, 512, 256), BF), pltpu.VMEM((2, 8, 2, 4, 16, 128), F32)], scalars=1, flops=268_000_000,
    )
    dab = exchange(dab.reshape(128, 16, 128), OWNERS)
    parts, dproj = run(
        weight_kernel, [((768, 128), BF), ((8, 512, 128), BF)],
        dab, factors, normed, sums, scratch=[pltpu.VMEM((2048, 128), F32)], flops=134_000_000,
    )
    parts = exchange(parts.reshape(32, 24, 128), PLANE).astype(F32)
    parts = jnp.sum(parts, axis=0, keepdims=True).astype(BF)
    parts = exchange(jnp.broadcast_to(parts, (8, 24, 128)), LINE).astype(F32)
    parts = (jnp.sum(parts, axis=0, keepdims=True) / total).astype(BF)
    whole = exchange(jnp.broadcast_to(parts, (32, 24, 128)), PLANE).reshape(768, 128)
    pair_grad = run(
        pair_kernel, [((4, 8, 32, 128), BF)], dproj, in_weight, dn_gate, pair, flops=134_000_000
    )
    in_grad, gate_grad, out_grad = run(
        collect_kernel, [((128, 512), F32), ((128, 128), F32), ((128, 128), F32)], whole
    )
    return (pair_grad.reshape(32, 32, 128), in_grad, gate_grad, out_grad)


def solution(mesh):
    fine = Mesh(mesh.devices.reshape(4, 4, 2, 4, 2), ALL)
    tiles = P(ROW, CHI + ("core",), None)
    return jax.shard_map(
        per_device,
        mesh=fine,
        in_specs=(tiles, tiles, P(), P(), P()),
        out_specs=(tiles, P(), P(), P()),
        check_vma=False,
    )
```

time: 165 us -> 157 us (0.952)
  local copies, waits for them, and re-layouts: 19.2 us -> 12.1 us
  waiting for transfers between devices: 44.1 us -> 42.1 us
    unnamed x51 -> x38, local copies, waits for them, and re-layouts: 17.7 us -> 11.4 us
    all_to_all x4, starting transfers between devices: 34.7 us -> 37.3 us  [exchange(): return lax.all_to_all(values, axes, 0, 0, tiled=True)]
    all_to_all x4, waiting for transfers between devices: 41.4 us -> 39.4 us  [exchange(): return lax.all_to_all(values, axes, 0, 0, tiled=True)]
    pallas_call x9 -> x10, Pallas kernels: 12.5 us -> 13.3 us  [run(): pl.pallas_call(kernel, out_shape=outs, in_specs=[smem] * scalars + [vmem]...]
where the time goes in v1:
time: 157 us; the launch traced here: 156 us
  blocking collectives  44.3 us (28%)
  starting transfers between devices  43.2 us (28%)
  waiting for transfers between devices  42.1 us (27%)
  Pallas kernels  13.3 us (8%)
  local copies, waits for them, and re-layouts  12.1 us (8%)
    all_to_all x3, blocking collectives, exchange(): return lax.all_to_all(values, axes, 0, 0, tiled=True)  44.3 us
    all_to_all x4, waiting for transfers between devices, exchange(): return lax.all_to_all(values, axes, 0, 0, tiled=True)  39.4 us
    all_to_all x4, starting transfers between devices, exchange(): return lax.all_to_all(values, axes, 0, 0, tiled=True)  37.3 us
    pallas_call x10, Pallas kernels, run(): pl.pallas_call(kernel, out_shape=outs, in_specs=[smem] * scalars + [vmem]...  13.3 us
    unnamed x38, local copies, waits for them, and re-layouts  11.4 us
    ppermute x1, starting transfers between devices, per_device(): other = lax.ppermute(own, 'core', SWAP)  3.39 us
  transfers between devices with their start and end apart: 6, of which 6 were waited for; matrix products, arithmetic and copies ran while one was open for 0% of the time, Pallas kernels for 3%

profile of v1, /device:TPU:1, one launch (start us, length us, event | category | flops | bytes accessed | tf_op | source)
XLA Modules:
  0.0 155.9 jit_solution(17751225052928892308)
XLA Ops:
  2.5 1.9 %shard_map.84 = (bf16[128,16,128]{2,1,0:T(8,128)(2,1)}, bf16[8,128,128]{2,1,0:T(8,128)(2,1)S(1)}) custom-call(bf16[4,8,32,128]{3,2,1,0:T(8,128)(2,1)S(1)} %bitcast.18, bf16[128,512]{1,0:T(8,128)(2,1)S(1)} %copy-done.6), custom_call_target="tpu_custom_call" | custom-call | flops 134000000 | bytes 1179648 | tf_op jit(solution)/shard_map/pallas_call | solution.py:183
  4.4 16.3 %all-to-all-start = ((bf16[128,16,128]{2,1,0:T(8,128)(2,1)}), bf16[128,16,128]{2,1,0:T(8,128)(2,1)S(1)}, u32[]{:S(2)}, u32[]{:S(2)}) async-start(bf16[128,16,128]{2,1,0:T(8,128)(2,1)} %get-tuple-element.22), calls=%async_computation | async-start | bytes 1048576 | tf_op jit(solution)/shard_map/all_to_all | solution.py:196
  20.8 16.2 %all-to-all-done = bf16[128,16,128]{2,1,0:T(8,128)(2,1)S(1)} async-done(((bf16[128,16,128]{2,1,0:T(8,128)(2,1)}), bf16[128,16,128]{2,1,0:T(8,128)(2,1)S(1)}, u32[]{:S(2)}, u32[]{:S(2)}) %all-to-all-start) | async-done | bytes 524320 | tf_op jit(solution)/shard_map/all_to_all | solution.py:196
  37.8 2.5 %collective-permute-start = (f32[512,256]{1,0:T(8,128)S(1)}, f32[512,256]{1,0:T(8,128)S(1)}, u32[]{:S(2)}, u32[]{:S(2)}) collective-permute-start(f32[512,256]{1,0:T(8,128)S(1)} %get-tuple-element.25), channel_id=1, source_target_pairs={{0,1},{1,0},{2,3},{3,2},{4,5},{5,4},{6,7},{7,6},{8,9},{9,8},{10,11... | collective-permute-start | bytes 1572872 | tf_op jit(solution)/shard_map/ppermute | solution.py:218
  40.2 1.5 collective-permute-done.got_ref
  41.8 1.1 shard_map.86
  42.9 8.3 %all-to-all-start.1 = ((bf16[128,8,128]{2,1,0:T(8,128)(2,1)}), bf16[128,8,128]{2,1,0:T(8,128)(2,1)S(1)}, u32[]{:S(2)}, u32[]{:S(2)}) async-start(bf16[128,8,128]{2,1,0:T(8,128)(2,1)} %bitcast.3), calls=%async_computation.1 | async-start | bytes 524288 | tf_op jit(solution)/shard_map/all_to_all | solution.py:196
  53.6 8.8 %all-to-all-done.1.x_ref = bf16[128,8,128]{2,1,0:T(8,128)(2,1)S(1)} async-done(((bf16[128,8,128]{2,1,0:T(8,128)(2,1)}), bf16[128,8,128]{2,1,0:T(8,128)(2,1)S(1)}, u32[]{:S(2)}, u32[]{:S(2)}) %all-to-all-start.1) | async-done | bytes 262176 | tf_op jit(solution)/shard_map/all_to_all | solution.py:196
  62.9 19.3 %all_to_all.35 = bf16[128,8,128]{2,1,0:T(8,128)(2,1)S(1)} all-to-all(bf16[128,8,128]{2,1,0:T(8,128)(2,1)S(1)} %get-tuple-element.28), channel_id=1, replica_groups=mesh['y'=4,'zh'=4,'zl'=2,'x'=4,'core'=2] {'zl','y','zh','x'}, dimensions={0} | all-to-all | bytes 524288 | tf_op jit(solution)/shard_map/all_to_all | solution.py:196
  82.2 3.4 %collective-permute-start.1 = (bf16[128,8,128]{2,1,0:T(8,128)(2,1)S(1)}, bf16[128,8,128]{2,1,0:T(8,128)(2,1)S(1)}, u32[]{:S(2)}, u32[]{:S(2)}) collective-permute-start(bf16[128,8,128]{2,1,0:T(8,128)(2,1)S(1)} %all_to_all.35), channel_id=1, source_target_pairs={{0,1},{1,0},{2,3},{3,2},{4,5},{5,4},{6,7},{7,6},{8,9},{9,8},{10,11... | collective-permute-start | bytes 786440 | tf_op jit(solution)/shard_map/ppermute | solution.py:229
  85.6 1.2 collective-permute-done.1
  86.8 2.5 %shard_map.89 = bf16[2,8,2,4,16,128]{5,4,3,2,1,0:T(8,128)(2,1)} custom-call(s32[1]{0:T(128)} %bitcast.core_ref, bf16[2,16,4,8,128]{4,3,2,1,0:T(8,128)(2,1)S(1)} %bitcast.14, bf16[2,16,4,8,128]{4,3,2,1,0:T(8,128)(2,1)S(1)} %bitcast.21, bf16[512,256]{1,0:T(8,128)(2,1)S(1)} %get-tuple-element.23.a_ref, bf16[2,256,256]{2,1,0:T(8,128)(2,1)S(1)} %get-tuple-element.24.b_ref), custom_call_target="tpu_custom_call" | custom-call | flops 268000000 | bytes 1572868 | tf_op jit(solution)/shard_map/pallas_call | solution.py:183
  89.3 7.1 %all-to-all-start.3 = ((bf16[128,16,128]{2,1,0:T(8,128)(2,1)}), bf16[128,16,128]{2,1,0:T(8,128)(2,1)S(1)}, u32[]{:S(2)}, u32[]{:S(2)}) async-start(bf16[128,16,128]{2,1,0:T(8,128)(2,1)} %bitcast.8), calls=%async_computation.3 | async-start | bytes 1048576 | tf_op jit(solution)/shard_map/all_to_all | solution.py:196
  96.5 1.0 copy-done.3
  97.5 1.0 copy-done.5
  98.6 0.9 copy-done.11
  101.0 1.6 %shard_map.90 = (f32[256,128]{1,0:T(8,128)S(1)}, f32[8,128,128]{2,1,0:T(8,128)S(1)}, f32[8,512,128]{2,1,0:T(8,128)S(1)}) custom-call(f32[1024,128]{1,0:T(8,128)S(1)} %bitcast.16, bf16[8,128,128]{2,1,0:T(8,128)(2,1)S(1)} %get-tuple-element.26.norm_ref, f32[8,128,128]{2,1,0:T(8,128)S(1)} %copy-done.3, bf16[8,128,128]{2,1,0:T(8,128)(2,1)S(1)} %copy-done.11, ...), custom_call_target="tpu_custom_call" | custom-call | flops 268000000 | bytes 4521984 | tf_op jit(solution)/shard_map/pallas_call | solution.py:183
  103.3 9.7 %all-to-all-done.3.dab_ref = bf16[128,16,128]{2,1,0:T(8,128)(2,1)S(1)} async-done(((bf16[128,16,128]{2,1,0:T(8,128)(2,1)}), bf16[128,16,128]{2,1,0:T(8,128)(2,1)S(1)}, u32[]{:S(2)}, u32[]{:S(2)}) %all-to-all-start.3) | async-done | bytes 524320 | tf_op jit(solution)/shard_map/all_to_all | solution.py:196
  114.6 1.0 copy-done
  115.6 15.4 %all_to_all.36 = bf16[32,24,128]{2,1,0:T(8,128)(2,1)S(1)} all-to-all(bf16[32,24,128]{2,1,0:T(8,128)(2,1)S(1)} %bitcast.22), channel_id=1, replica_groups=mesh['y'=4,'zh'=4,'zl'=2,'x'=4,'core'=2] {'core','y','x'}, dimensions={0} | all-to-all | bytes 393216 | tf_op jit(solution)/shard_map/all_to_all | solution.py:196
  131.1 9.6 %all_to_all.37 = bf16[8,24,128]{2,1,0:T(8,128)(2,1)S(1)} all-to-all(bf16[8,24,128]{2,1,0:T(8,128)(2,1)S(1)} %broadcast_in_dim.4), channel_id=1, replica_groups=mesh['y'=4,'zh'=4,'zl'=2,'x'=4,'core'=2] {'zh','zl'}, dimensions={0} | all-to-all | bytes 98304 | tf_op jit(solution)/shard_map/all_to_all | solution.py:196
  141.4 5.5 %all-to-all-start.6 = ((bf16[32,24,128]{2,1,0:T(8,128)(2,1)}), bf16[32,24,128]{2,1,0:T(8,128)(2,1)S(1)}, u32[]{:S(2)}, u32[]{:S(2)}) async-start(bf16[32,24,128]{2,1,0:T(8,128)(2,1)} %broadcast_in_dim.5), calls=%async_computation.6 | async-start | bytes 393216 | tf_op jit(solution)/shard_map/all_to_all | solution.py:196
  147.9 2.4 %shard_map.92 = bf16[4,8,32,128]{3,2,1,0:T(8,128)(2,1)} custom-call(bf16[8,512,128]{2,1,0:T(8,128)(2,1)S(1)} %copy-done.1, bf16[128,512]{1,0:T(8,128)(2,1)S(1)} %copy-done.7, f32[8,128,128]{2,1,0:T(8,128)S(1)} %get-tuple-element.35.dn_ref, bf16[4,8,32,128]{3,2,1,0:T(8,128)(2,1)S(1)} %bitcast.19), custom_call_target="tpu_custom_call" | custom-call | flops 134000000 | bytes 2228224 | tf_op jit(solution)/shard_map/pallas_call | solution.py:183
  150.3 4.7 %all-to-all-done.6 = bf16[32,24,128]{2,1,0:T(8,128)(2,1)S(1)} async-done(((bf16[32,24,128]{2,1,0:T(8,128)(2,1)}), bf16[32,24,128]{2,1,0:T(8,128)(2,1)S(1)}, u32[]{:S(2)}, u32[]{:S(2)}) %all-to-all-start.6) | async-done | bytes 196640 | tf_op jit(solution)/shard_map/all_to_all | solution.py:196
  (44 shorter events, 11.8 us)
Async XLA Ops:
  0.6 0.9 copy-start.6
  1.5 0.9 copy-start.8
  2.5 48.7 %copy-start.12 = (bf16[32,32,128]{2,1,0:T(8,128)(2,1)S(1)}, bf16[32,32,128]{2,1,0:T(8,128)(2,1)}, u32[]{:S(2)}) copy-start(bf16[32,32,128]{2,1,0:T(8,128)(2,1)} %param.6) | copy-start | bytes 786436
  2.5 48.7 %copy-start.13 = (bf16[128,128]{1,0:T(8,128)(2,1)S(1)}, bf16[128,128]{1,0:T(8,128)(2,1)}, u32[]{:S(2)}) copy-start(bf16[128,128]{1,0:T(8,128)(2,1)} %gw_ref.3) | copy-start | bytes 98308
  2.5 48.7 %copy-start.15 = (bf16[128,128]{1,0:T(8,128)(2,1)S(1)}, bf16[128,128]{1,0:T(8,128)(2,1)}, u32[]{:S(2)}) copy-start(bf16[128,128]{1,0:T(8,128)(2,1)} %ow_ref.3) | copy-start | bytes 98308
  4.4 32.6 %all-to-all-start = ((bf16[128,16,128]{2,1,0:T(8,128)(2,1)}), bf16[128,16,128]{2,1,0:T(8,128)(2,1)S(1)}, u32[]{:S(2)}, u32[]{:S(2)}) async-start(bf16[128,16,128]{2,1,0:T(8,128)(2,1)} %get-tuple-element.22), calls=%async_computation | async-start | bytes 1048576 | tf_op jit(solution)/shard_map/all_to_all | solution.py:196
  37.8 4.0 %collective-permute-start = (f32[512,256]{1,0:T(8,128)S(1)}, f32[512,256]{1,0:T(8,128)S(1)}, u32[]{:S(2)}, u32[]{:S(2)}) collective-permute-start(f32[512,256]{1,0:T(8,128)S(1)} %get-tuple-element.25), channel_id=1, source_target_pairs={{0,1},{1,0},{2,3},{3,2},{4,5},{5,4},{6,7},{7,6},{8,9},{9,8},{10,11... | collective-permute-start | bytes 1572872 | tf_op jit(solution)/shard_map/ppermute | solution.py:218
  42.9 19.5 %all-to-all-start.1 = ((bf16[128,8,128]{2,1,0:T(8,128)(2,1)}), bf16[128,8,128]{2,1,0:T(8,128)(2,1)S(1)}, u32[]{:S(2)}, u32[]{:S(2)}) async-start(bf16[128,8,128]{2,1,0:T(8,128)(2,1)} %bitcast.3), calls=%async_computation.1 | async-start | bytes 524288 | tf_op jit(solution)/shard_map/all_to_all | solution.py:196
  52.1 0.8 copy-start.2
  52.9 0.7 copy-start.10
  53.6 42.8 %copy-start.7 = (bf16[128,512]{1,0:T(8,128)(2,1)S(1)}, bf16[128,512]{1,0:T(8,128)(2,1)}, u32[]{:S(2)}) copy-start(bf16[128,512]{1,0:T(8,128)(2,1)} %w_ref.5) | copy-start | bytes 393220
  62.9 23.8 %copy-start.4 = (f32[128,8,128]{2,1,0:T(8,128)}, f32[128,8,128]{2,1,0:T(8,128)S(1)}, u32[]{:S(2)}) copy-start(f32[128,8,128]{2,1,0:T(8,128)S(1)} %get-tuple-element.29) | copy-start | bytes 1572868
  82.2 4.6 %collective-permute-start.1 = (bf16[128,8,128]{2,1,0:T(8,128)(2,1)S(1)}, bf16[128,8,128]{2,1,0:T(8,128)(2,1)S(1)}, u32[]{:S(2)}, u32[]{:S(2)}) collective-permute-start(bf16[128,8,128]{2,1,0:T(8,128)(2,1)S(1)} %all_to_all.35), channel_id=1, source_target_pairs={{0,1},{1,0},{2,3},{3,2},{4,5},{5,4},{6,7},{7,6},{8,9},{9,8},{10,11... | collective-permute-start | bytes 786440 | tf_op jit(solution)/shard_map/ppermute | solution.py:229
  89.3 23.7 %all-to-all-start.3 = ((bf16[128,16,128]{2,1,0:T(8,128)(2,1)}), bf16[128,16,128]{2,1,0:T(8,128)(2,1)S(1)}, u32[]{:S(2)}, u32[]{:S(2)}) async-start(bf16[128,16,128]{2,1,0:T(8,128)(2,1)} %bitcast.8), calls=%async_computation.3 | async-start | bytes 1048576 | tf_op jit(solution)/shard_map/all_to_all | solution.py:196
  96.5 1.0 copy-start.3
  97.5 1.0 copy-start.5
  98.6 0.9 copy-start.11
  99.5 0.8 copy-start.14
  100.3 0.8 copy-start.16
  113.0 0.9 copy-start.18
  114.6 1.0 copy-start
  115.6 31.4 %copy-start.1 = (bf16[8,512,128]{2,1,0:T(8,128)(2,1)S(1)}, bf16[8,512,128]{2,1,0:T(8,128)(2,1)}, u32[]{:S(2)}) copy-start(bf16[8,512,128]{2,1,0:T(8,128)(2,1)} %copy-done) | copy-start | bytes 3145732
  141.4 13.6 %all-to-all-start.6 = ((bf16[32,24,128]{2,1,0:T(8,128)(2,1)}), bf16[32,24,128]{2,1,0:T(8,128)(2,1)S(1)}, u32[]{:S(2)}, u32[]{:S(2)}) async-start(bf16[32,24,128]{2,1,0:T(8,128)(2,1)} %broadcast_in_dim.5), calls=%async_computation.6 | async-start | bytes 393216 | tf_op jit(solution)/shard_map/all_to_all | solution.py:196
  147.0 1.0 copy-start.9
  (1 other events, 0.7 us)

commit v2 on v1

--- a/solution.py
+++ b/solution.py
@@ -1,3 +1,5 @@
+import functools
+
 import jax
 import jax.numpy as jnp
 from jax import lax
@@ -46,7 +48,15 @@
     return [p0, p1, p2, p3]
 
 
-def project_kernel(pair_ref, w_ref, msg_ref, norm_ref, held):
+def project_kernel(pair_hbm, w_hbm, msg_ref, norm_ref, pair_ref, w_ref, held, sems):
+    copies = [
+        pltpu.make_async_copy(pair_hbm, pair_ref, sems.at[0]),
+        pltpu.make_async_copy(w_hbm, w_ref, sems.at[1]),
+    ]
+    for copy in copies:
+        copy.start()
+    for copy in copies:
+        copy.wait()
     w = w_ref[...]
     for s in range(8):
         zhat, _ = layer_norm(pair_ref[:, s].astype(F32).reshape(128, 128))
@@ -78,19 +88,25 @@
         for g, part in enumerate(regroup(parts)):
             a_ref[pl.ds(128 * g, 128), pl.ds(128 * t, 128)] = part.astype(BF)
         for half in range(2):
-            sel = core if half == 0 else 1 - core
-            parts = [msg_ref[t, :, sel, q].astype(F32)[:, 8:16].reshape(64, 128) for q in range(4)]
+            parts = [msg_ref[t, :, half, q].astype(F32)[:, 8:16].reshape(64, 128) for q in range(4)]
             parts = [part.reshape(8, 8, 128) for part in regroup(parts)]
             b_ref[half, :, pl.ds(128 * t, 128)] = jnp.stack(parts, axis=1).reshape(256, 128).astype(BF)
-    give_ref[...] = dot(a_ref[...], b_ref[1], ((1,), (1,)))
-
-
-def x_kernel(a_ref, b_ref, got_ref, msg_ref):
-    x = dot(a_ref[...], b_ref[0], ((1,), (1,))) + got_ref[...]
+    to_message(dot(a_ref[...], b_ref[1 - core], ((1,), (1,))), give_ref)
+
+
+def to_message(x, out_ref):
     for t in range(2):
         parts = [x[128 * g : 128 * g + 128, 128 * t : 128 * t + 128] for g in range(4)]
         for q, part in enumerate(regroup(parts)):
-            msg_ref[t, :, q] = part.reshape(16, 8, 128).astype(BF)
+            out_ref[t, :, q] = part.reshape(16, 8, 128)
+
+
+def keep_kernel(core_ref, a_ref, b_ref, keep_ref):
+    to_message(dot(a_ref[...], b_ref[core_ref[0]], ((1,), (1,))), keep_ref)
+
+
+def add_kernel(keep_ref, got_ref, msg_ref):
+    msg_ref[...] = (keep_ref[...] + got_ref[...]).astype(BF)
 
 
 def dx_kernel(x_ref, dxn_ref, msg_ref, xhat_ref):
@@ -118,13 +134,13 @@
             sig = jax.nn.sigmoid(proj[256 * n + 128 : 256 * n + 256])
             fac_ref[s, 256 * n : 256 * n + 128] = sig
             fac_ref[s, 256 * n + 128 : 256 * n + 256] = val * sig * (1.0 - sig)
-    sum_ref[0:128] = gate_part
-    sum_ref[128:256] = out_part
+    sum_ref[0:128] = gate_part.astype(BF)
+    sum_ref[128:256] = out_part.astype(BF)
 
 
 def pull_kernel(core_ref, own_ref, other_ref, a_ref, b_ref, msg_ref, dx, held):
-    core = core_ref[0]
-    for half, ref in enumerate((own_ref, other_ref)):
+    for n, ref in enumerate((own_ref, other_ref)):
+        half = core_ref[0] if n == 0 else 1 - core_ref[0]
         for t in range(2):
             parts = [ref[t, :, q].astype(F32).reshape(128, 128) for q in range(4)]
             for g, part in enumerate(regroup(parts)):
@@ -135,16 +151,17 @@
         for q, part in enumerate(regroup(parts)):
             held[t, :, :, q, 0:8] = part.reshape(8, 2, 8, 128)
     for half in range(2):
-        sel = core if half == 0 else 1 - core
         db = dot(dx[half], a_ref[...], ((0,), (0,))).reshape(8, 4, 8, 256)
         for t in range(2):
             parts = [db[:, g, :, 128 * t : 128 * t + 128].reshape(64, 128) for g in range(4)]
             for q, part in enumerate(regroup(parts)):
-                held[t, :, sel, q, 8:16] = part.reshape(8, 8, 128)
+                held[t, :, half, q, 8:16] = part.reshape(8, 8, 128)
     msg_ref[...] = held[...].astype(BF)
 
 
-def weight_kernel(dab_ref, fac_ref, norm_ref, gate_out_ref, sum_ref, dproj_ref, held):
+def weight_kernel(go_hbm, dab_ref, fac_ref, norm_ref, sum_hbm, dproj_ref, held, sums, sems):
+    first = pltpu.make_async_copy(go_hbm, sum_hbm.at[pl.ds(512, 256)], sems.at[0])
+    first.start()
     held[...] = dab_ref[...].astype(F32).reshape(2048, 128)
     total = jnp.zeros((512, 128), F32)
     for s in range(8):
@@ -156,8 +173,11 @@
         ).astype(BF)
         dproj_ref[s] = dproj
         total += dot(dproj, norm_ref[s])
-    sum_ref[0:512] = total.astype(BF)
-    sum_ref[512:768] = gate_out_ref[...].astype(BF)
+    sums[...] = total.astype(BF)
+    last = pltpu.make_async_copy(sums, sum_hbm.at[pl.ds(0, 512)], sems.at[1])
+    last.start()
+    first.wait()
+    last.wait()
 
 
 def pair_kernel(dproj_ref, w_ref, dn_ref, pair_ref, out_ref):
@@ -169,26 +189,33 @@
         out_ref[:, s] = grad.reshape(4, 32, 128).astype(BF)
 
 
+def sum_kernel(scale, parts_ref, out_ref):
+    total = jnp.sum(parts_ref[...].astype(F32), axis=0, keepdims=True) * scale
+    out_ref[...] = jnp.broadcast_to(total, out_ref.shape).astype(BF)
+
+
 def collect_kernel(rows_ref, in_ref, gate_ref, out_ref):
     in_ref[...] = rows_ref[0:512].astype(F32).T
     gate_ref[...] = rows_ref[512:640].astype(F32)
     out_ref[...] = rows_ref[640:768].astype(F32)
 
 
-def run(kernel, outs, *args, scratch=(), scalars=0, flops=0):
+def run(kernel, outs, *args, scratch=(), scalars=0, hbm=0, hbm_out=0, flops=0, after=(), grant=16):
     outs = [jax.ShapeDtypeStruct(shape, dtype) for shape, dtype in outs]
     vmem = pl.BlockSpec(memory_space=pltpu.VMEM)
     smem = pl.BlockSpec(memory_space=pltpu.SMEM)
+    anywhere = pl.BlockSpec(memory_space=pltpu.HBM)
+    skip = len(after)
     size = sum(v.size * v.dtype.itemsize for v in list(args) + outs)
     result = pl.pallas_call(
-        kernel,
+        lambda *refs: kernel(*refs[skip:]),
         out_shape=outs,
-        in_specs=[smem] * scalars + [vmem] * (len(args) - scalars),
-        out_specs=[vmem] * len(outs),
+        in_specs=[anywhere] * (skip + hbm) + [smem] * scalars + [vmem] * (len(args) - scalars - hbm),
+        out_specs=[anywhere] * hbm_out + [vmem] * (len(outs) - hbm_out),
         scratch_shapes=scratch,
-        compiler_params=pltpu.CompilerParams(vmem_limit_bytes=16 * 1024 * 1024),
+        compiler_params=pltpu.CompilerParams(vmem_limit_bytes=grant * 1024 * 1024),
         cost_estimate=pl.CostEstimate(flops=flops, bytes_accessed=size, transcendentals=0),
-    )(*args)
+    )(*after, *args)
     return result[0] if len(outs) == 1 else result
 
 
@@ -198,53 +225,62 @@
 
 def per_device(pair, cotangent, in_weight, gate_weight, out_weight):
     core = jnp.reshape(lax.axis_index("core"), (1,)).astype(jnp.int32)
-    total = 512
     pair = pair.reshape(4, 8, 32, 128)
     cotangent = cotangent.reshape(4, 8, 32, 128)
 
     msg, normed = run(
-        project_kernel, [((128, 16, 128), BF), ((8, 128, 128), BF)], pair, in_weight,
-        scratch=[pltpu.VMEM((2048, 128), F32)], flops=134_000_000,
+        project_kernel, [((128, 16, 128), BF), ((8, 128, 128), BF)], pair, in_weight, hbm=2, grant=56,
+        scratch=[
+            pltpu.VMEM((4, 8, 32, 128), BF), pltpu.VMEM((128, 512), BF),
+            pltpu.VMEM((2048, 128), F32), pltpu.SemaphoreType.DMA((2,)),
+        ],
+        flops=134_000_000,
     )
     msg = exchange(msg, OWNERS).reshape(2, 8, 2, 4, 16, 128)
     g2, dout, dxnorm = run(
         side_kernel, [((8, 128, 128), F32), ((8, 128, 128), BF), ((1024, 128), F32)],
         normed, cotangent, gate_weight, out_weight, flops=67_000_000,
     )
+    half = (2, 16, 4, 8, 128)
     a_own, b_own, give = run(
-        pack_kernel, [((512, 256), BF), ((2, 256, 256), BF), ((512, 256), F32)],
+        pack_kernel, [((512, 256), BF), ((2, 256, 256), BF), (half, F32)],
         core, msg, scalars=1, flops=67_000_000,
     )
     got = lax.ppermute(give, "core", SWAP)
-    x = run(x_kernel, [((2, 16, 4, 8, 128), BF)], a_own, b_own, got, flops=67_000_000)
+    keep = run(keep_kernel, [(half, F32)], core, a_own, b_own, scalars=1, flops=67_000_000)
+    x = run(add_kernel, [(half, BF)], keep, got)
     x = exchange(x.reshape(128, 8, 128), OWNERS)
     dx, xhat = run(
         dx_kernel, [((128, 8, 128), BF), ((128, 8, 128), F32)], x, dxnorm.reshape(128, 8, 128), flops=1_000_000
     )
-    own = exchange(dx, OWNERS)
+    dx = exchange(dx, OWNERS)
+    dx = dx.reshape(2, 16, 4, 8, 128)
+    other = lax.ppermute(dx, "core", SWAP)
     sums, dn_gate, factors = run(
-        late_kernel, [((256, 128), F32), ((8, 128, 128), F32), ((8, 512, 128), F32)],
+        late_kernel, [((256, 128), BF), ((8, 128, 128), F32), ((8, 512, 128), F32)],
         xhat.reshape(1024, 128), normed, g2, dout, in_weight, gate_weight, out_weight, flops=268_000_000,
     )
-    other = lax.ppermute(own, "core", SWAP)
     dab = run(
-        pull_kernel, [((2, 8, 2, 4, 16, 128), BF)],
-        core, own.reshape(2, 16, 4, 8, 128), other.reshape(2, 16, 4, 8, 128), a_own, b_own,
-        scratch=[pltpu.VMEM((2, 512, 256), BF), pltpu.VMEM((2, 8, 2, 4, 16, 128), F32)], scalars=1, flops=268_000_000,
+        pull_kernel, [((2, 8, 2, 4, 16, 128), BF)], core, dx, other, a_own, b_own, scalars=1, after=(dn_gate,),
+        scratch=[pltpu.VMEM((2, 512, 256), BF), pltpu.VMEM((2, 8, 2, 4, 16, 128), F32)], flops=268_000_000,
     )
     dab = exchange(dab.reshape(128, 16, 128), OWNERS)
     parts, dproj = run(
         weight_kernel, [((768, 128), BF), ((8, 512, 128), BF)],
-        dab, factors, normed, sums, scratch=[pltpu.VMEM((2048, 128), F32)], flops=134_000_000,
-    )
-    parts = exchange(parts.reshape(32, 24, 128), PLANE).astype(F32)
-    parts = jnp.sum(parts, axis=0, keepdims=True).astype(BF)
-    parts = exchange(jnp.broadcast_to(parts, (8, 24, 128)), LINE).astype(F32)
-    parts = (jnp.sum(parts, axis=0, keepdims=True) / total).astype(BF)
-    whole = exchange(jnp.broadcast_to(parts, (32, 24, 128)), PLANE).reshape(768, 128)
+        sums, dab, factors, normed, hbm=1, hbm_out=1,
+        scratch=[
+            pltpu.VMEM((2048, 128), F32), pltpu.VMEM((512, 128), BF), pltpu.SemaphoreType.DMA((2,)),
+        ],
+        flops=134_000_000,
+    )
+    parts = exchange(parts.reshape(32, 24, 128), PLANE)
     pair_grad = run(
         pair_kernel, [((4, 8, 32, 128), BF)], dproj, in_weight, dn_gate, pair, flops=134_000_000
     )
+    parts = run(functools.partial(sum_kernel, 1.0), [((8, 24, 128), BF)], parts, after=(pair_grad,))
+    parts = exchange(parts, LINE)
+    parts = run(functools.partial(sum_kernel, 1.0 / 512), [((32, 24, 128), BF)], parts)
+    whole = exchange(parts, PLANE).reshape(768, 128)
     in_grad, gate_grad, out_grad = run(
         collect_kernel, [((128, 512), F32), ((128, 128), F32), ((128, 128), F32)], whole
     )

time: 157 us -> 154 us (0.981)
  blocking collectives: 44.3 us -> 66.2 us
  local copies, waits for them, and re-layouts: 12.1 us -> 0.99 us
  waiting for transfers between devices: 42.1 us -> 33.1 us
  starting transfers between devices: 43.2 us -> 37.6 us
    all_to_all x3 -> x4, blocking collectives: 44.3 us -> 66.2 us  [exchange(): return lax.all_to_all(values, axes, 0, 0, tiled=True)]
    unnamed x38 -> x14, local copies, waits for them, and re-layouts: 11.4 us -> 0.99 us
    all_to_all x4 -> x3, waiting for transfers between devices: 39.4 us -> 32.1 us  [exchange(): return lax.all_to_all(values, axes, 0, 0, tiled=True)]
    all_to_all x4 -> x3, starting transfers between devices: 37.3 us -> 31.7 us  [exchange(): return lax.all_to_all(values, axes, 0, 0, tiled=True)]
    pallas_call x10 -> x13, Pallas kernels: 13.3 us -> 14.6 us  [run(): pl.pallas_call(lambda *refs: kernel(*refs[skip:]), out_shape=outs, in_spe...]
  transfers between devices with their start and end apart: 6 -> 5, of which waited for: 6 -> 4; matrix products, arithmetic and copies ran while one was open for 0% -> 0% of each run, Pallas kernels for 3% -> 4%
where the time goes in v2:
time: 154 us; the launch traced here: 153 us
  blocking collectives  66.2 us (43%)
  starting transfers between devices  37.6 us (24%)
  waiting for transfers between devices  33.1 us (21%)
  Pallas kernels  14.6 us (9%)
    all_to_all x4, blocking collectives, exchange(): return lax.all_to_all(values, axes, 0, 0, tiled=True)  66.2 us
    all_to_all x3, waiting for transfers between devices, exchange(): return lax.all_to_all(values, axes, 0, 0, tiled=True)  32.1 us
    all_to_all x3, starting transfers between devices, exchange(): return lax.all_to_all(values, axes, 0, 0, tiled=True)  31.7 us
    pallas_call x13, Pallas kernels, run(): pl.pallas_call(lambda *refs: kernel(*refs[skip:]), out_shape=outs, in_spe...  14.6 us
    ppermute x1, starting transfers between devices, per_device(): other = lax.ppermute(dx, 'core', SWAP)  3.4 us
  transfers between devices with their start and end apart: 5, of which 4 were waited for; matrix products, arithmetic and copies ran while one was open for 0% of the time, Pallas kernels for 4%

profile of v2, /device:TPU:1, one launch (start us, length us, event | category | flops | bytes accessed | tf_op | source)
XLA Modules:
  0.0 153.3 jit_solution(1782934792004413750)
XLA Ops:
  0.6 2.9 %shard_map.84 = (bf16[128,16,128]{2,1,0:T(8,128)(2,1)}, bf16[8,128,128]{2,1,0:T(8,128)(2,1)}) custom-call(bf16[4,8,32,128]{3,2,1,0:T(8,128)(2,1)} %bitcast.20, bf16[128,512]{1,0:T(8,128)(2,1)} %refs_1_.3), custom_call_target="tpu_custom_call" | custom-call | flops 134000000 | bytes 1179648 | tf_op jit(solution)/shard_map/pallas_call | solution.py:210
  3.6 16.5 %all-to-all-start = ((bf16[128,16,128]{2,1,0:T(8,128)(2,1)}), bf16[128,16,128]{2,1,0:T(8,128)(2,1)S(1)}, u32[]{:S(2)}, u32[]{:S(2)}) async-start(bf16[128,16,128]{2,1,0:T(8,128)(2,1)} %get-tuple-element.22), calls=%async_computation | async-start | bytes 1048576 | tf_op jit(solution)/shard_map/all_to_all | solution.py:223
  20.1 16.2 %all-to-all-done = bf16[128,16,128]{2,1,0:T(8,128)(2,1)S(1)} async-done(((bf16[128,16,128]{2,1,0:T(8,128)(2,1)}), bf16[128,16,128]{2,1,0:T(8,128)(2,1)S(1)}, u32[]{:S(2)}, u32[]{:S(2)}) %all-to-all-start) | async-done | bytes 524320 | tf_op jit(solution)/shard_map/all_to_all | solution.py:223
  36.3 1.2 shard_map.85
  37.5 2.5 %collective-permute-start = (f32[2,16,4,8,128]{4,3,2,1,0:T(8,128)S(1)}, f32[2,16,4,8,128]{4,3,2,1,0:T(8,128)S(1)}, u32[]{:S(2)}, u32[]{:S(2)}) collective-permute-start(f32[2,16,4,8,128]{4,3,2,1,0:T(8,128)S(1)} %get-tuple-element.25), channel_id=1, source_target_pairs={{0,1},{1,0},{2,3},{3,2},{4,5},{5,4},{6,7},{7,6},{8,9},{9,8},{10,11... | collective-permute-start | bytes 1572872 | tf_op jit(solution)/shard_map/ppermute | solution.py:249
  40.0 0.5 shard_map.86.refs_0_
  40.5 1.0 collective-permute-done.refs_1_
  41.5 0.7 shard_map.87
  42.3 8.3 %all-to-all-start.1 = ((bf16[128,8,128]{2,1,0:T(8,128)(2,1)}), bf16[128,8,128]{2,1,0:T(8,128)(2,1)S(1)}, u32[]{:S(2)}, u32[]{:S(2)}) async-start(bf16[128,8,128]{2,1,0:T(8,128)(2,1)} %bitcast.3), calls=%async_computation.1 | async-start | bytes 524288 | tf_op jit(solution)/shard_map/all_to_all | solution.py:223
  50.6 0.9 shard_map.88
  51.5 10.2 %all-to-all-done.1.refs_0_ = bf16[128,8,128]{2,1,0:T(8,128)(2,1)S(1)} async-done(((bf16[128,8,128]{2,1,0:T(8,128)(2,1)}), bf16[128,8,128]{2,1,0:T(8,128)(2,1)S(1)}, u32[]{:S(2)}, u32[]{:S(2)}) %all-to-all-start.1) | async-done | bytes 262176 | tf_op jit(solution)/shard_map/all_to_all | solution.py:223
  62.3 19.3 %all_to_all.35 = bf16[128,8,128]{2,1,0:T(8,128)(2,1)S(1)} all-to-all(bf16[128,8,128]{2,1,0:T(8,128)(2,1)S(1)} %get-tuple-element.33), channel_id=1, replica_groups=mesh['y'=4,'zh'=4,'zl'=2,'x'=4,'core'=2] {'zl','y','zh','x'}, dimensions={0} | all-to-all | bytes 524288 | tf_op jit(solution)/shard_map/all_to_all | solution.py:223
  81.6 3.4 %collective-permute-start.1 = (bf16[2,16,4,8,128]{4,3,2,1,0:T(8,128)(2,1)S(1)}, bf16[2,16,4,8,128]{4,3,2,1,0:T(8,128)(2,1)S(1)}, u32[]{:S(2)}, u32[]{:S(2)}) collective-permute-start(bf16[2,16,4,8,128]{4,3,2,1,0:T(8,128)(2,1)S(1)} %bitcast.15), channel_id=1, source_target_pairs={{0,1},{1,0},{2,3},{3,2},{4,5},{5,4},{6,7},{7,6},{8,9},{9,8},{10,11... | collective-permute-start | bytes 786440 | tf_op jit(solution)/shard_map/ppermute | solution.py:258
  85.0 1.6 %shard_map.90 = (bf16[256,128]{1,0:T(8,128)(2,1)S(1)}, f32[8,128,128]{2,1,0:T(8,128)S(1)}, f32[8,512,128]{2,1,0:T(8,128)S(1)}) custom-call(f32[1024,128]{1,0:T(8,128)S(1)} %bitcast.18, bf16[8,128,128]{2,1,0:T(8,128)(2,1)S(1)} %copy-done, f32[8,128,128]{2,1,0:T(8,128)S(1)} %get-tuple-element.29.refs_2_, bf16[8,128,128]{2,1,0:T(8,128)(2,1)S(1)} %get-tuple-element.30.refs_3_, ...), custom_call_target="tpu_custom_call" | custom-call | flops 268000000 | bytes 4456448 | tf_op jit(solution)/shard_map/pallas_call | solution.py:210
  86.6 1.5 %shard_map.91 = bf16[2,8,2,4,16,128]{5,4,3,2,1,0:T(8,128)(2,1)S(1)} custom-call(f32[8,128,128]{2,1,0:T(8,128)S(1)} %get-tuple-element.32.refs_0_.refs_2_, s32[1]{0:T(128)} %bitcast.refs_0_.refs_1_, bf16[2,16,4,8,128]{4,3,2,1,0:T(8,128)(2,1)S(1)} %bitcast.16, bf16[2,16,4,8,128]{4,3,2,1,0:T(8,128)(2,1)S(1)} %collective-permute-done.1.refs_3_, ...), custom_call_target="tpu_custom_call" | custom-call | flops 268000000 | bytes 1572868 | tf_op jit(solution)/shard_map/pallas_call | solution.py:210
  88.2 24.1 %all_to_all.36.refs_1_ = bf16[128,16,128]{2,1,0:T(8,128)(2,1)S(1)} all-to-all(bf16[128,16,128]{2,1,0:T(8,128)(2,1)S(1)} %bitcast.12), channel_id=1, replica_groups=mesh['y'=4,'zh'=4,'zl'=2,'x'=4,'core'=2] {'zl','y','zh','x'}, dimensions={0} | all-to-all | bytes 1048576 | tf_op jit(solution)/shard_map/all_to_all | solution.py:223
  112.3 1.3 shard_map.92
  113.7 6.9 %all-to-all-start.4 = ((bf16[32,24,128]{2,1,0:T(8,128)(2,1)}), bf16[32,24,128]{2,1,0:T(8,128)(2,1)S(1)}, u32[]{:S(2)}, u32[]{:S(2)}) async-start(bf16[32,24,128]{2,1,0:T(8,128)(2,1)} %bitcast.10), calls=%async_computation.4 | async-start | bytes 393216 | tf_op jit(solution)/shard_map/all_to_all | solution.py:223
  120.6 2.4 %shard_map.93.refs_0_ = bf16[4,8,32,128]{3,2,1,0:T(8,128)(2,1)} custom-call(bf16[8,512,128]{2,1,0:T(8,128)(2,1)S(1)} %get-tuple-element.35.refs_0_, bf16[128,512]{1,0:T(8,128)(2,1)S(1)} %copy-done.2, f32[8,128,128]{2,1,0:T(8,128)S(1)} %get-tuple-element.32.refs_0_.refs_2_, bf16[4,8,32,128]{3,2,1,0:T(8,128)(2,1)S(1)} %bitcast.21), custom_call_target="tpu_custom_call" | custom-call | flops 134000000 | bytes 2228224 | tf_op jit(solution)/shard_map/pallas_call | solution.py:210
  123.0 5.7 %all-to-all-done.4.refs_1_ = bf16[32,24,128]{2,1,0:T(8,128)(2,1)S(1)} async-done(((bf16[32,24,128]{2,1,0:T(8,128)(2,1)}), bf16[32,24,128]{2,1,0:T(8,128)(2,1)S(1)}, u32[]{:S(2)}, u32[]{:S(2)}) %all-to-all-start.4) | async-done | bytes 196640 | tf_op jit(solution)/shard_map/all_to_all | solution.py:223
  128.7 0.9 copy-done.1
  129.7 9.6 %all_to_all.37.refs_0_ = bf16[8,24,128]{2,1,0:T(8,128)(2,1)S(1)} all-to-all(bf16[8,24,128]{2,1,0:T(8,128)(2,1)S(1)} %shard_map.94), channel_id=1, replica_groups=mesh['y'=4,'zh'=4,'zl'=2,'x'=4,'core'=2] {'zh','zl'}, dimensions={0} | all-to-all | bytes 98304 | tf_op jit(solution)/shard_map/all_to_all | solution.py:223
  139.3 13.1 %all_to_all.38 = bf16[32,24,128]{2,1,0:T(8,128)(2,1)S(1)} all-to-all(bf16[32,24,128]{2,1,0:T(8,128)(2,1)S(1)} %shard_map.95), channel_id=1, replica_groups=mesh['y'=4,'zh'=4,'zl'=2,'x'=4,'core'=2] {'core','y','x'}, dimensions={0} | all-to-all | bytes 393216 | tf_op jit(solution)/shard_map/all_to_all | solution.py:223
  152.5 0.8 shard_map.96
  (17 shorter events, 0.6 us)
Async XLA Ops:
  3.6 47.0 %copy-start = (bf16[8,128,128]{2,1,0:T(8,128)(2,1)S(1)}, bf16[8,128,128]{2,1,0:T(8,128)(2,1)}, u32[]{:S(2)}) copy-start(bf16[8,128,128]{2,1,0:T(8,128)(2,1)} %get-tuple-element.26.refs_0_.refs_1_.refs_3_) | copy-start | bytes 786436
  3.6 47.0 %copy-start.4 = (bf16[32,32,128]{2,1,0:T(8,128)(2,1)S(1)}, bf16[32,32,128]{2,1,0:T(8,128)(2,1)}, u32[]{:S(2)}) copy-start(bf16[32,32,128]{2,1,0:T(8,128)(2,1)} %param.6) | copy-start | bytes 786436
  3.6 47.0 %copy-start.5 = (bf16[128,128]{1,0:T(8,128)(2,1)S(1)}, bf16[128,128]{1,0:T(8,128)(2,1)}, u32[]{:S(2)}) copy-start(bf16[128,128]{1,0:T(8,128)(2,1)} %refs_5_.1) | copy-start | bytes 98308
  3.6 47.0 %copy-start.6 = (bf16[128,128]{1,0:T(8,128)(2,1)S(1)}, bf16[128,128]{1,0:T(8,128)(2,1)}, u32[]{:S(2)}) copy-start(bf16[128,128]{1,0:T(8,128)(2,1)} %refs_6_.1) | copy-start | bytes 98308
  3.6 32.7 %all-to-all-start = ((bf16[128,16,128]{2,1,0:T(8,128)(2,1)}), bf16[128,16,128]{2,1,0:T(8,128)(2,1)S(1)}, u32[]{:S(2)}, u32[]{:S(2)}) async-start(bf16[128,16,128]{2,1,0:T(8,128)(2,1)} %get-tuple-element.22), calls=%async_computation | async-start | bytes 1048576 | tf_op jit(solution)/shard_map/all_to_all | solution.py:223
  37.5 4.0 %collective-permute-start = (f32[2,16,4,8,128]{4,3,2,1,0:T(8,128)S(1)}, f32[2,16,4,8,128]{4,3,2,1,0:T(8,128)S(1)}, u32[]{:S(2)}, u32[]{:S(2)}) collective-permute-start(f32[2,16,4,8,128]{4,3,2,1,0:T(8,128)S(1)} %get-tuple-element.25), channel_id=1, source_target_pairs={{0,1},{1,0},{2,3},{3,2},{4,5},{5,4},{6,7},{7,6},{8,9},{9,8},{10,11... | collective-permute-start | bytes 1572872 | tf_op jit(solution)/shard_map/ppermute | solution.py:249
  40.5 44.5 %copy-start.2 = (bf16[128,512]{1,0:T(8,128)(2,1)S(1)}, bf16[128,512]{1,0:T(8,128)(2,1)}, u32[]{:S(2)}) copy-start(bf16[128,512]{1,0:T(8,128)(2,1)} %refs_1_.3) | copy-start | bytes 393220
  42.3 19.5 %all-to-all-start.1 = ((bf16[128,8,128]{2,1,0:T(8,128)(2,1)}), bf16[128,8,128]{2,1,0:T(8,128)(2,1)S(1)}, u32[]{:S(2)}, u32[]{:S(2)}) async-start(bf16[128,8,128]{2,1,0:T(8,128)(2,1)} %bitcast.3), calls=%async_computation.1 | async-start | bytes 524288 | tf_op jit(solution)/shard_map/all_to_all | solution.py:223
  81.6 5.1 %collective-permute-start.1 = (bf16[2,16,4,8,128]{4,3,2,1,0:T(8,128)(2,1)S(1)}, bf16[2,16,4,8,128]{4,3,2,1,0:T(8,128)(2,1)S(1)}, u32[]{:S(2)}, u32[]{:S(2)}) collective-permute-start(bf16[2,16,4,8,128]{4,3,2,1,0:T(8,128)(2,1)S(1)} %bitcast.15), channel_id=1, source_target_pairs={{0,1},{1,0},{2,3},{3,2},{4,5},{5,4},{6,7},{7,6},{8,9},{9,8},{10,11... | collective-permute-start | bytes 786440 | tf_op jit(solution)/shard_map/ppermute | solution.py:258
  88.2 32.4 %copy-start.3 = (bf16[32,32,128]{2,1,0:T(8,128)(2,1)S(1)}, bf16[32,32,128]{2,1,0:T(8,128)(2,1)}, u32[]{:S(2)}) copy-start(bf16[32,32,128]{2,1,0:T(8,128)(2,1)} %param.5) | copy-start | bytes 786436
  113.7 15.0 %all-to-all-start.4 = ((bf16[32,24,128]{2,1,0:T(8,128)(2,1)}), bf16[32,24,128]{2,1,0:T(8,128)(2,1)S(1)}, u32[]{:S(2)}, u32[]{:S(2)}) async-start(bf16[32,24,128]{2,1,0:T(8,128)(2,1)} %bitcast.10), calls=%async_computation.4 | async-start | bytes 393216 | tf_op jit(solution)/shard_map/all_to_all | solution.py:223
  128.7 1.0 copy-start.1

commit v3 on v2

--- a/solution.py
+++ b/solution.py
@@ -58,13 +58,15 @@
     for copy in copies:
         copy.wait()
     w = w_ref[...]
-    for s in range(8):
-        zhat, _ = layer_norm(pair_ref[:, s].astype(F32).reshape(128, 128))
-        normed = zhat.astype(BF)
-        norm_ref[s] = normed
-        proj = dot(w, normed, ((0,), (1,)))
-        held[pl.ds(s, 128, stride=16), :] = jax.nn.sigmoid(proj[128:256]) * proj[0:128]
-        held[pl.ds(8 + s, 128, stride=16), :] = jax.nn.sigmoid(proj[384:512]) * proj[256:384]
+    pair = jnp.concatenate([pair_ref[:, s].astype(F32).reshape(128, 128) for s in range(8)], axis=0)
+    normed = layer_norm(pair)[0].astype(BF)
+    norm_ref[...] = normed.reshape(8, 128, 128)
+    for n in range(2):
+        val = dot(w[:, 256 * n : 256 * n + 128], normed, ((0,), (1,)))
+        sig = jax.nn.sigmoid(dot(w[:, 256 * n + 128 : 256 * n + 256], normed, ((0,), (1,))))
+        val = val * sig
+        for s in range(8):
+            held[pl.ds(8 * n + s, 128, stride=16), :] = val[:, 128 * s : 128 * s + 128]
     msg_ref[...] = held[...].reshape(128, 16, 128).astype(BF)
 
 
@@ -115,9 +117,8 @@
     msg_ref[...] = layer_norm_backward(dxn_ref[...], xhat, xinv, 0).astype(BF)
 
 
-def late_kernel(xhat_ref, norm_ref, g2_ref, dout_ref, w_ref, gw_ref, ow_ref, sum_ref, dn_ref, fac_ref):
+def late_kernel(xhat_ref, norm_ref, g2_ref, dout_ref, w_ref, ow_ref, sum_ref, dgate_ref, fac_ref):
     w = w_ref[...]
-    gw = gw_ref[...]
     ow = ow_ref[...]
     gate_part = jnp.zeros((128, 128), F32)
     out_part = jnp.zeros((128, 128), F32)
@@ -127,7 +128,7 @@
         dgate = (g2_ref[s] * dot(xnorm, ow, ((0,), (0,)))).astype(BF)
         gate_part += dot(normed, dgate, ((0,), (0,)))
         out_part += dot(xnorm, dout_ref[s])
-        dn_ref[s] = dot(dgate, gw, ((1,), (1,)))
+        dgate_ref[s] = dgate
         proj = dot(w, normed, ((0,), (1,)))
         for n in range(2):
             val = proj[256 * n : 256 * n + 128]
@@ -180,11 +181,13 @@
     last.wait()
 
 
-def pair_kernel(dproj_ref, w_ref, dn_ref, pair_ref, out_ref):
+def pair_kernel(dproj_ref, w_ref, dgate_ref, gw_ref, pair_ref, out_ref, token_ref):
+    token_ref[...] = jnp.zeros((8, 128), F32)
     w = w_ref[...]
+    gw = gw_ref[...]
     for s in range(8):
         zhat, zinv = layer_norm(pair_ref[:, s].astype(F32).reshape(128, 128))
-        dnormed = dot(dproj_ref[s], w, ((0,), (1,))) + dn_ref[s]
+        dnormed = dot(dproj_ref[s], w, ((0,), (1,))) + dot(dgate_ref[s], gw, ((1,), (1,)))
         grad = layer_norm_backward(dnormed, zhat, zinv)
         out_ref[:, s] = grad.reshape(4, 32, 128).astype(BF)
 
@@ -256,12 +259,12 @@
     dx = exchange(dx, OWNERS)
     dx = dx.reshape(2, 16, 4, 8, 128)
     other = lax.ppermute(dx, "core", SWAP)
-    sums, dn_gate, factors = run(
-        late_kernel, [((256, 128), BF), ((8, 128, 128), F32), ((8, 512, 128), F32)],
-        xhat.reshape(1024, 128), normed, g2, dout, in_weight, gate_weight, out_weight, flops=268_000_000,
+    sums, dgate, factors = run(
+        late_kernel, [((256, 128), BF), ((8, 128, 128), BF), ((8, 512, 128), F32)],
+        xhat.reshape(1024, 128), normed, g2, dout, in_weight, out_weight, flops=268_000_000,
     )
     dab = run(
-        pull_kernel, [((2, 8, 2, 4, 16, 128), BF)], core, dx, other, a_own, b_own, scalars=1, after=(dn_gate,),
+        pull_kernel, [((2, 8, 2, 4, 16, 128), BF)], core, dx, other, a_own, b_own, scalars=1, after=(sums,),
         scratch=[pltpu.VMEM((2, 512, 256), BF), pltpu.VMEM((2, 8, 2, 4, 16, 128), F32)], flops=268_000_000,
     )
     dab = exchange(dab.reshape(128, 16, 128), OWNERS)
@@ -274,10 +277,11 @@
         flops=134_000_000,
     )
     parts = exchange(parts.reshape(32, 24, 128), PLANE)
-    pair_grad = run(
-        pair_kernel, [((4, 8, 32, 128), BF)], dproj, in_weight, dn_gate, pair, flops=134_000_000
-    )
-    parts = run(functools.partial(sum_kernel, 1.0), [((8, 24, 128), BF)], parts, after=(pair_grad,))
+    pair_grad, token = run(
+        pair_kernel, [((4, 8, 32, 128), BF), ((8, 128), F32)], dproj, in_weight, dgate, gate_weight, pair,
+        flops=134_000_000,
+    )
+    parts = run(functools.partial(sum_kernel, 1.0), [((8, 24, 128), BF)], parts, after=(token,))
     parts = exchange(parts, LINE)
     parts = run(functools.partial(sum_kernel, 1.0 / 512), [((32, 24, 128), BF)], parts)
     whole = exchange(parts, PLANE).reshape(768, 128)

time: 154 us -> 153 us (level)
  no operation moved by 1% of the time
where the time goes in v3:
time: 153 us; the launch traced here: 152 us
  blocking collectives  66.2 us (43%)
  starting transfers between devices  37.6 us (25%)
  waiting for transfers between devices  33.1 us (22%)
  Pallas kernels  14.3 us (9%)
    all_to_all x4, blocking collectives, exchange(): return lax.all_to_all(values, axes, 0, 0, tiled=True)  66.2 us
    all_to_all x3, waiting for transfers between devices, exchange(): return lax.all_to_all(values, axes, 0, 0, tiled=True)  32.1 us
    all_to_all x3, starting transfers between devices, exchange(): return lax.all_to_all(values, axes, 0, 0, tiled=True)  31.7 us
    pallas_call x13, Pallas kernels, run(): pl.pallas_call(lambda *refs: kernel(*refs[skip:]), out_shape=outs, in_spe...  14.3 us
    ppermute x1, starting transfers between devices, per_device(): other = lax.ppermute(dx, 'core', SWAP)  3.4 us
  transfers between devices with their start and end apart: 5, of which 4 were waited for; matrix products, arithmetic and copies ran while one was open for 0% of the time, Pallas kernels for 4%

profile of v3, /device:TPU:1, one launch (start us, length us, event | category | flops | bytes accessed | tf_op | source)
XLA Modules:
  0.0 152.0 jit_solution(7541480309023562900)
XLA Ops:
  0.6 2.8 %shard_map.84 = (bf16[128,16,128]{2,1,0:T(8,128)(2,1)}, bf16[8,128,128]{2,1,0:T(8,128)(2,1)}) custom-call(bf16[4,8,32,128]{3,2,1,0:T(8,128)(2,1)} %bitcast.20, bf16[128,512]{1,0:T(8,128)(2,1)} %refs_1_.3), custom_call_target="tpu_custom_call" | custom-call | flops 134000000 | bytes 1179648 | tf_op jit(solution)/shard_map/pallas_call | solution.py:213
  3.5 16.5 %all-to-all-start = ((bf16[128,16,128]{2,1,0:T(8,128)(2,1)}), bf16[128,16,128]{2,1,0:T(8,128)(2,1)S(1)}, u32[]{:S(2)}, u32[]{:S(2)}) async-start(bf16[128,16,128]{2,1,0:T(8,128)(2,1)} %get-tuple-element.24), calls=%async_computation | async-start | bytes 1048576 | tf_op jit(solution)/shard_map/all_to_all | solution.py:226
  20.0 16.2 %all-to-all-done = bf16[128,16,128]{2,1,0:T(8,128)(2,1)S(1)} async-done(((bf16[128,16,128]{2,1,0:T(8,128)(2,1)}), bf16[128,16,128]{2,1,0:T(8,128)(2,1)S(1)}, u32[]{:S(2)}, u32[]{:S(2)}) %all-to-all-start) | async-done | bytes 524320 | tf_op jit(solution)/shard_map/all_to_all | solution.py:226
  36.2 1.2 shard_map.85
  37.3 2.5 %collective-permute-start = (f32[2,16,4,8,128]{4,3,2,1,0:T(8,128)S(1)}, f32[2,16,4,8,128]{4,3,2,1,0:T(8,128)S(1)}, u32[]{:S(2)}, u32[]{:S(2)}) collective-permute-start(f32[2,16,4,8,128]{4,3,2,1,0:T(8,128)S(1)} %get-tuple-element.27), channel_id=1, source_target_pairs={{0,1},{1,0},{2,3},{3,2},{4,5},{5,4},{6,7},{7,6},{8,9},{9,8},{10,11... | collective-permute-start | bytes 1572872 | tf_op jit(solution)/shard_map/ppermute | solution.py:252
  39.8 0.5 shard_map.86.refs_0_
  40.4 1.0 collective-permute-done.refs_1_
  41.4 0.7 shard_map.87
  42.1 8.3 %all-to-all-start.1 = ((bf16[128,8,128]{2,1,0:T(8,128)(2,1)}), bf16[128,8,128]{2,1,0:T(8,128)(2,1)S(1)}, u32[]{:S(2)}, u32[]{:S(2)}) async-start(bf16[128,8,128]{2,1,0:T(8,128)(2,1)} %bitcast.3), calls=%async_computation.1 | async-start | bytes 524288 | tf_op jit(solution)/shard_map/all_to_all | solution.py:226
  50.4 0.9 shard_map.88
  51.3 10.2 %all-to-all-done.1.refs_0_ = bf16[128,8,128]{2,1,0:T(8,128)(2,1)S(1)} async-done(((bf16[128,8,128]{2,1,0:T(8,128)(2,1)}), bf16[128,8,128]{2,1,0:T(8,128)(2,1)S(1)}, u32[]{:S(2)}, u32[]{:S(2)}) %all-to-all-start.1) | async-done | bytes 262176 | tf_op jit(solution)/shard_map/all_to_all | solution.py:226
  61.6 0.5 shard_map.89
  62.1 19.3 %all_to_all.35 = bf16[128,8,128]{2,1,0:T(8,128)(2,1)S(1)} all-to-all(bf16[128,8,128]{2,1,0:T(8,128)(2,1)S(1)} %get-tuple-element.34), channel_id=1, replica_groups=mesh['y'=4,'zh'=4,'zl'=2,'x'=4,'core'=2] {'zl','y','zh','x'}, dimensions={0} | all-to-all | bytes 524288 | tf_op jit(solution)/shard_map/all_to_all | solution.py:226
  81.4 3.4 %collective-permute-start.1 = (bf16[2,16,4,8,128]{4,3,2,1,0:T(8,128)(2,1)S(1)}, bf16[2,16,4,8,128]{4,3,2,1,0:T(8,128)(2,1)S(1)}, u32[]{:S(2)}, u32[]{:S(2)}) collective-permute-start(bf16[2,16,4,8,128]{4,3,2,1,0:T(8,128)(2,1)S(1)} %bitcast.14), channel_id=1, source_target_pairs={{0,1},{1,0},{2,3},{3,2},{4,5},{5,4},{6,7},{7,6},{8,9},{9,8},{10,11... | collective-permute-start | bytes 786440 | tf_op jit(solution)/shard_map/ppermute | solution.py:261
  84.8 1.5 shard_map.90
  86.3 1.5 %shard_map.91 = bf16[2,8,2,4,16,128]{5,4,3,2,1,0:T(8,128)(2,1)S(1)} custom-call(bf16[256,128]{1,0:T(8,128)(2,1)S(1)} %get-tuple-element.33.refs_0_, s32[1]{0:T(128)} %bitcast.refs_0_.refs_1_, bf16[2,16,4,8,128]{4,3,2,1,0:T(8,128)(2,1)S(1)} %bitcast.15, bf16[2,16,4,8,128]{4,3,2,1,0:T(8,128)(2,1)S(1)} %collective-permute-done.1.refs_3_, ...), custom_call_target="tpu_custom_call" | custom-call | flops 268000000 | bytes 1572868 | tf_op jit(solution)/shard_map/pallas_call | solution.py:213
  87.9 24.1 %all_to_all.36.refs_1_ = bf16[128,16,128]{2,1,0:T(8,128)(2,1)S(1)} all-to-all(bf16[128,16,128]{2,1,0:T(8,128)(2,1)S(1)} %bitcast.13), channel_id=1, replica_groups=mesh['y'=4,'zh'=4,'zl'=2,'x'=4,'core'=2] {'zl','y','zh','x'}, dimensions={0} | all-to-all | bytes 1048576 | tf_op jit(solution)/shard_map/all_to_all | solution.py:226
  112.0 1.3 shard_map.92
  113.4 6.9 %all-to-all-start.4 = ((bf16[32,24,128]{2,1,0:T(8,128)(2,1)}), bf16[32,24,128]{2,1,0:T(8,128)(2,1)S(1)}, u32[]{:S(2)}, u32[]{:S(2)}) async-start(bf16[32,24,128]{2,1,0:T(8,128)(2,1)} %bitcast.10), calls=%async_computation.4 | async-start | bytes 393216 | tf_op jit(solution)/shard_map/all_to_all | solution.py:226
  120.3 2.4 %shard_map.93 = (bf16[4,8,32,128]{3,2,1,0:T(8,128)(2,1)}, f32[8,128]{1,0:T(8,128)S(1)}) custom-call(bf16[8,512,128]{2,1,0:T(8,128)(2,1)S(1)} %get-tuple-element.36.refs_0_, bf16[128,512]{1,0:T(8,128)(2,1)S(1)} %copy-done.1, bf16[8,128,128]{2,1,0:T(8,128)(2,1)S(1)} %get-tuple-element.37.refs_2_, bf16[128,128]{1,0:T(8,128)(2,1)S(1)} %copy-done.5, ...), custom_call_target="tpu_custom_call" | custom-call | flops 134000000 | bytes 2002944 | tf_op jit(solution)/shard_map/pallas_call | solution.py:213
  122.7 5.7 %all-to-all-done.4.refs_1_ = bf16[32,24,128]{2,1,0:T(8,128)(2,1)S(1)} async-done(((bf16[32,24,128]{2,1,0:T(8,128)(2,1)}), bf16[32,24,128]{2,1,0:T(8,128)(2,1)S(1)}, u32[]{:S(2)}, u32[]{:S(2)}) %all-to-all-start.4) | async-done | bytes 196640 | tf_op jit(solution)/shard_map/all_to_all | solution.py:226
  128.4 9.6 %all_to_all.37.refs_0_ = bf16[8,24,128]{2,1,0:T(8,128)(2,1)S(1)} all-to-all(bf16[8,24,128]{2,1,0:T(8,128)(2,1)S(1)} %shard_map.94), channel_id=1, replica_groups=mesh['y'=4,'zh'=4,'zl'=2,'x'=4,'core'=2] {'zh','zl'}, dimensions={0} | all-to-all | bytes 98304 | tf_op jit(solution)/shard_map/all_to_all | solution.py:226
  138.1 13.1 %all_to_all.38 = bf16[32,24,128]{2,1,0:T(8,128)(2,1)S(1)} all-to-all(bf16[32,24,128]{2,1,0:T(8,128)(2,1)S(1)} %shard_map.95), channel_id=1, replica_groups=mesh['y'=4,'zh'=4,'zl'=2,'x'=4,'core'=2] {'core','y','x'}, dimensions={0} | all-to-all | bytes 393216 | tf_op jit(solution)/shard_map/all_to_all | solution.py:226
  151.2 0.8 shard_map.96
  (15 shorter events, 0.1 us)
Async XLA Ops:
  3.4 47.0 %copy-start = (bf16[8,128,128]{2,1,0:T(8,128)(2,1)S(1)}, bf16[8,128,128]{2,1,0:T(8,128)(2,1)}, u32[]{:S(2)}) copy-start(bf16[8,128,128]{2,1,0:T(8,128)(2,1)} %get-tuple-element.28.refs_0_.refs_1_.refs_3_) | copy-start | bytes 786436
  3.4 47.0 %copy-start.2 = (bf16[32,32,128]{2,1,0:T(8,128)(2,1)S(1)}, bf16[32,32,128]{2,1,0:T(8,128)(2,1)}, u32[]{:S(2)}) copy-start(bf16[32,32,128]{2,1,0:T(8,128)(2,1)} %param.6) | copy-start | bytes 786436
  3.4 47.0 %copy-start.4 = (bf16[128,128]{1,0:T(8,128)(2,1)S(1)}, bf16[128,128]{1,0:T(8,128)(2,1)}, u32[]{:S(2)}) copy-start(bf16[128,128]{1,0:T(8,128)(2,1)} %refs_5_.1) | copy-start | bytes 98308
  3.5 47.0 %copy-start.5 = (bf16[128,128]{1,0:T(8,128)(2,1)S(1)}, bf16[128,128]{1,0:T(8,128)(2,1)}, u32[]{:S(2)}) copy-start(bf16[128,128]{1,0:T(8,128)(2,1)} %refs_3_.3) | copy-start | bytes 98308
  3.5 32.7 %all-to-all-start = ((bf16[128,16,128]{2,1,0:T(8,128)(2,1)}), bf16[128,16,128]{2,1,0:T(8,128)(2,1)S(1)}, u32[]{:S(2)}, u32[]{:S(2)}) async-start(bf16[128,16,128]{2,1,0:T(8,128)(2,1)} %get-tuple-element.24), calls=%async_computation | async-start | bytes 1048576 | tf_op jit(solution)/shard_map/all_to_all | solution.py:226
  37.3 4.0 %collective-permute-start = (f32[2,16,4,8,128]{4,3,2,1,0:T(8,128)S(1)}, f32[2,16,4,8,128]{4,3,2,1,0:T(8,128)S(1)}, u32[]{:S(2)}, u32[]{:S(2)}) collective-permute-start(f32[2,16,4,8,128]{4,3,2,1,0:T(8,128)S(1)} %get-tuple-element.27), channel_id=1, source_target_pairs={{0,1},{1,0},{2,3},{3,2},{4,5},{5,4},{6,7},{7,6},{8,9},{9,8},{10,11... | collective-permute-start | bytes 1572872 | tf_op jit(solution)/shard_map/ppermute | solution.py:252
  40.4 44.5 %copy-start.1 = (bf16[128,512]{1,0:T(8,128)(2,1)S(1)}, bf16[128,512]{1,0:T(8,128)(2,1)}, u32[]{:S(2)}) copy-start(bf16[128,512]{1,0:T(8,128)(2,1)} %refs_1_.3) | copy-start | bytes 393220
  42.1 19.5 %all-to-all-start.1 = ((bf16[128,8,128]{2,1,0:T(8,128)(2,1)}), bf16[128,8,128]{2,1,0:T(8,128)(2,1)S(1)}, u32[]{:S(2)}, u32[]{:S(2)}) async-start(bf16[128,8,128]{2,1,0:T(8,128)(2,1)} %bitcast.3), calls=%async_computation.1 | async-start | bytes 524288 | tf_op jit(solution)/shard_map/all_to_all | solution.py:226
  81.4 4.9 %collective-permute-start.1 = (bf16[2,16,4,8,128]{4,3,2,1,0:T(8,128)(2,1)S(1)}, bf16[2,16,4,8,128]{4,3,2,1,0:T(8,128)(2,1)S(1)}, u32[]{:S(2)}, u32[]{:S(2)}) collective-permute-start(bf16[2,16,4,8,128]{4,3,2,1,0:T(8,128)(2,1)S(1)} %bitcast.14), channel_id=1, source_target_pairs={{0,1},{1,0},{2,3},{3,2},{4,5},{5,4},{6,7},{7,6},{8,9},{9,8},{10,11... | collective-permute-start | bytes 786440 | tf_op jit(solution)/shard_map/ppermute | solution.py:261
  87.9 32.4 %copy-start.3 = (bf16[32,32,128]{2,1,0:T(8,128)(2,1)S(1)}, bf16[32,32,128]{2,1,0:T(8,128)(2,1)}, u32[]{:S(2)}) copy-start(bf16[32,32,128]{2,1,0:T(8,128)(2,1)} %param.5) | copy-start | bytes 786436
  113.4 15.0 %all-to-all-start.4 = ((bf16[32,24,128]{2,1,0:T(8,128)(2,1)}), bf16[32,24,128]{2,1,0:T(8,128)(2,1)S(1)}, u32[]{:S(2)}, u32[]{:S(2)}) async-start(bf16[32,24,128]{2,1,0:T(8,128)(2,1)} %bitcast.10), calls=%async_computation.4 | async-start | bytes 393216 | tf_op jit(solution)/shard_map/all_to_all | solution.py:226

commit v4 on v3

--- a/solution.py
+++ b/solution.py
@@ -83,32 +83,35 @@
         dxn_ref[pl.ds(s, 128, stride=8), :] = dot(ow, dout, ((1,), (1,)))
 
 
-def pack_kernel(core_ref, msg_ref, a_ref, b_ref, give_ref):
+def pack_a(msg_ref, a_ref):
+    for t in range(2):
+        parts = [msg_ref[t, :, :, q][:, :, 0:8].reshape(128, 128) for q in range(4)]
+        for g, part in enumerate(regroup(parts)):
+            a_ref[pl.ds(128 * g, 128), pl.ds(128 * t, 128)] = part
+
+
+def pack_b(msg_ref, half, b_ref):
+    for t in range(2):
+        parts = [msg_ref[t, :, half, q][:, 8:16].reshape(64, 128) for q in range(4)]
+        parts = [part.reshape(8, 8, 128) for part in regroup(parts)]
+        b_ref[:, pl.ds(128 * t, 128)] = jnp.stack(parts, axis=1).reshape(256, 128)
+
+
+def pack_kernel(msg_ref, a_ref, b_ref):
+    pack_a(msg_ref, a_ref)
+    for half in range(2):
+        pack_b(msg_ref, half, b_ref.at[half])
+
+
+def x_kernel(core_ref, a_ref, b_ref, other_ref, msg_ref, oa_ref, ob_ref):
     core = core_ref[0]
-    for t in range(2):
-        parts = [msg_ref[t, :, :, q].astype(F32)[:, :, 0:8].reshape(128, 128) for q in range(4)]
-        for g, part in enumerate(regroup(parts)):
-            a_ref[pl.ds(128 * g, 128), pl.ds(128 * t, 128)] = part.astype(BF)
-        for half in range(2):
-            parts = [msg_ref[t, :, half, q].astype(F32)[:, 8:16].reshape(64, 128) for q in range(4)]
-            parts = [part.reshape(8, 8, 128) for part in regroup(parts)]
-            b_ref[half, :, pl.ds(128 * t, 128)] = jnp.stack(parts, axis=1).reshape(256, 128).astype(BF)
-    to_message(dot(a_ref[...], b_ref[1 - core], ((1,), (1,))), give_ref)
-
-
-def to_message(x, out_ref):
+    pack_a(other_ref, oa_ref)
+    pack_b(other_ref, core, ob_ref)
+    x = dot(a_ref[...], b_ref[core], ((1,), (1,))) + dot(oa_ref[...], ob_ref[...], ((1,), (1,)))
     for t in range(2):
         parts = [x[128 * g : 128 * g + 128, 128 * t : 128 * t + 128] for g in range(4)]
         for q, part in enumerate(regroup(parts)):
-            out_ref[t, :, q] = part.reshape(16, 8, 128)
-
-
-def keep_kernel(core_ref, a_ref, b_ref, keep_ref):
-    to_message(dot(a_ref[...], b_ref[core_ref[0]], ((1,), (1,))), keep_ref)
-
-
-def add_kernel(keep_ref, got_ref, msg_ref):
-    msg_ref[...] = (keep_ref[...] + got_ref[...]).astype(BF)
+            msg_ref[t, :, q] = part.reshape(16, 8, 128).astype(BF)
 
 
 def dx_kernel(x_ref, dxn_ref, msg_ref, xhat_ref):
@@ -143,9 +146,9 @@
     for n, ref in enumerate((own_ref, other_ref)):
         half = core_ref[0] if n == 0 else 1 - core_ref[0]
         for t in range(2):
-            parts = [ref[t, :, q].astype(F32).reshape(128, 128) for q in range(4)]
+            parts = [ref[t, :, q].reshape(128, 128) for q in range(4)]
             for g, part in enumerate(regroup(parts)):
-                dx[half, pl.ds(128 * g, 128), pl.ds(128 * t, 128)] = part.astype(BF)
+                dx[half, pl.ds(128 * g, 128), pl.ds(128 * t, 128)] = part
     da = dot(dx[0], b_ref[0]) + dot(dx[1], b_ref[1])
     for t in range(2):
         parts = [da[128 * g : 128 * g + 128, 128 * t : 128 * t + 128] for g in range(4)]
@@ -244,14 +247,12 @@
         side_kernel, [((8, 128, 128), F32), ((8, 128, 128), BF), ((1024, 128), F32)],
         normed, cotangent, gate_weight, out_weight, flops=67_000_000,
     )
-    half = (2, 16, 4, 8, 128)
-    a_own, b_own, give = run(
-        pack_kernel, [((512, 256), BF), ((2, 256, 256), BF), (half, F32)],
-        core, msg, scalars=1, flops=67_000_000,
-    )
-    got = lax.ppermute(give, "core", SWAP)
-    keep = run(keep_kernel, [(half, F32)], core, a_own, b_own, scalars=1, flops=67_000_000)
-    x = run(add_kernel, [(half, BF)], keep, got)
+    other = lax.ppermute(msg, "core", SWAP)
+    a_own, b_own = run(pack_kernel, [((512, 256), BF), ((2, 256, 256), BF)], msg, flops=1_000_000)
+    x = run(
+        x_kernel, [((2, 16, 4, 8, 128), BF)], core, a_own, b_own, other, scalars=1, flops=134_000_000,
+        scratch=[pltpu.VMEM((512, 256), BF), pltpu.VMEM((256, 256), BF)],
+    )
     x = exchange(x.reshape(128, 8, 128), OWNERS)
     dx, xhat = run(
         dx_kernel, [((128, 8, 128), BF), ((128, 8, 128), F32)], x, dxnorm.reshape(128, 8, 128), flops=1_000_000

time: 153 us -> 152 us (level)
  blocking collectives: 66.2 us -> 99.1 us
  starting transfers between devices: 37.6 us -> 21 us
  waiting for transfers between devices: 33.1 us -> 16.8 us
    all_to_all x4 -> x5, blocking collectives: 66.2 us -> 99.1 us  [exchange(): return lax.all_to_all(values, axes, 0, 0, tiled=True)]
    all_to_all x3 -> x2, starting transfers between devices: 31.7 us -> 15.2 us  [exchange(): return lax.all_to_all(values, axes, 0, 0, tiled=True)]
    all_to_all x3 -> x2, waiting for transfers between devices: 32.1 us -> 15.9 us  [exchange(): return lax.all_to_all(values, axes, 0, 0, tiled=True)]
    pallas_call x13 -> x12, Pallas kernels: 14.3 us -> 14 us  [run(): pl.pallas_call(lambda *refs: kernel(*refs[skip:]), out_shape=outs, in_spe...]
  transfers between devices with their start and end apart: 5 -> 4, of which waited for: 4 -> 3; matrix products, arithmetic and copies ran while one was open for 0% -> 0% of each run, Pallas kernels for 4% -> 4%
where the time goes in v4:
time: 152 us
  blocking collectives  99.1 us (65%)
  starting transfers between devices  21 us (14%)
  waiting for transfers between devices  16.8 us (11%)
  Pallas kernels  14 us (9%)
    all_to_all x5, blocking collectives, exchange(): return lax.all_to_all(values, axes, 0, 0, tiled=True)  99.1 us
    all_to_all x2, waiting for transfers between devices, exchange(): return lax.all_to_all(values, axes, 0, 0, tiled=True)  15.9 us
    all_to_all x2, starting transfers between devices, exchange(): return lax.all_to_all(values, axes, 0, 0, tiled=True)  15.2 us
    pallas_call x12, Pallas kernels, run(): pl.pallas_call(lambda *refs: kernel(*refs[skip:]), out_shape=outs, in_spe...  14 us
    ppermute x1, starting transfers between devices, per_device(): other = lax.ppermute(dx, 'core', SWAP)  3.4 us
  transfers between devices with their start and end apart: 4, of which 3 were waited for; matrix products, arithmetic and copies ran while one was open for 0% of the time, Pallas kernels for 4%

profile of v4, /device:TPU:1, one launch (start us, length us, event | category | flops | bytes accessed | tf_op | source)
XLA Modules:
  0.0 151.7 jit_solution(7583852089211703594)
XLA Ops:
  0.7 2.8 %shard_map.84 = (bf16[128,16,128]{2,1,0:T(8,128)(2,1)}, bf16[8,128,128]{2,1,0:T(8,128)(2,1)}) custom-call(bf16[4,8,32,128]{3,2,1,0:T(8,128)(2,1)} %bitcast.21, bf16[128,512]{1,0:T(8,128)(2,1)} %refs_1_.3), custom_call_target="tpu_custom_call" | custom-call | flops 134000000 | bytes 1179648 | tf_op jit(solution)/shard_map/pallas_call | solution.py:216
  3.5 0.0 copy-start
  3.5 32.7 %all_to_all.35 = bf16[128,16,128]{2,1,0:T(8,128)(2,1)S(1)} all-to-all(bf16[128,16,128]{2,1,0:T(8,128)(2,1)} %get-tuple-element.23), channel_id=1, replica_groups=mesh['y'=4,'zh'=4,'zl'=2,'x'=4,'core'=2] {'zl','y','zh','x'}, dimensions={0} | all-to-all | bytes 1048576 | tf_op jit(solution)/shard_map/all_to_all | solution.py:229
  36.2 2.4 %collective-permute-start = (bf16[2,8,2,4,16,128]{5,4,3,2,1,0:T(8,128)(2,1)S(1)}, bf16[2,8,2,4,16,128]{5,4,3,2,1,0:T(8,128)(2,1)S(1)}, u32[]{:S(2)}, u32[]{:S(2)}) collective-permute-start(bf16[2,8,2,4,16,128]{5,4,3,2,1,0:T(8,128)(2,1)S(1)} %bitcast.12), channel_id=1, source_target_pairs={{0,1},{1,0},{2,3},{3,2},{4,5},{5,4},{6,7},{7,6},{8,9},{9,8},{10,11... | collective-permute-start | bytes 1572872 | tf_op jit(solution)/shard_map/ppermute | solution.py:250
  38.6 0.6 shard_map.85
  39.2 0.9 collective-permute-done.refs_3_
  40.1 1.5 shard_map.86
  41.6 8.3 %all-to-all-start.1 = ((bf16[128,8,128]{2,1,0:T(8,128)(2,1)}), bf16[128,8,128]{2,1,0:T(8,128)(2,1)S(1)}, u32[]{:S(2)}, u32[]{:S(2)}) async-start(bf16[128,8,128]{2,1,0:T(8,128)(2,1)} %bitcast.3), calls=%async_computation.1 | async-start | bytes 524288 | tf_op jit(solution)/shard_map/all_to_all | solution.py:229
  49.9 0.9 shard_map.87
  50.8 10.2 %all-to-all-done.1.refs_0_ = bf16[128,8,128]{2,1,0:T(8,128)(2,1)S(1)} async-done(((bf16[128,8,128]{2,1,0:T(8,128)(2,1)}), bf16[128,8,128]{2,1,0:T(8,128)(2,1)S(1)}, u32[]{:S(2)}, u32[]{:S(2)}) %all-to-all-start.1) | async-done | bytes 262176 | tf_op jit(solution)/shard_map/all_to_all | solution.py:229
  61.0 0.5 shard_map.88
  61.6 19.3 %all_to_all.36 = bf16[128,8,128]{2,1,0:T(8,128)(2,1)S(1)} all-to-all(bf16[128,8,128]{2,1,0:T(8,128)(2,1)S(1)} %get-tuple-element.32), channel_id=1, replica_groups=mesh['y'=4,'zh'=4,'zl'=2,'x'=4,'core'=2] {'zl','y','zh','x'}, dimensions={0} | all-to-all | bytes 524288 | tf_op jit(solution)/shard_map/all_to_all | solution.py:229
  80.9 3.4 %collective-permute-start.1 = (bf16[2,16,4,8,128]{4,3,2,1,0:T(8,128)(2,1)S(1)}, bf16[2,16,4,8,128]{4,3,2,1,0:T(8,128)(2,1)S(1)}, u32[]{:S(2)}, u32[]{:S(2)}) collective-permute-start(bf16[2,16,4,8,128]{4,3,2,1,0:T(8,128)(2,1)S(1)} %bitcast.15), channel_id=1, source_target_pairs={{0,1},{1,0},{2,3},{3,2},{4,5},{5,4},{6,7},{7,6},{8,9},{9,8},{10,11... | collective-permute-start | bytes 786440 | tf_op jit(solution)/shard_map/ppermute | solution.py:262
  84.3 1.5 shard_map.89
  85.8 1.5 %shard_map.90 = bf16[2,8,2,4,16,128]{5,4,3,2,1,0:T(8,128)(2,1)S(1)} custom-call(bf16[256,128]{1,0:T(8,128)(2,1)S(1)} %get-tuple-element.31.refs_0_, s32[1]{0:T(128)} %bitcast.refs_0_.refs_1_, bf16[2,16,4,8,128]{4,3,2,1,0:T(8,128)(2,1)S(1)} %bitcast.16, bf16[2,16,4,8,128]{4,3,2,1,0:T(8,128)(2,1)S(1)} %collective-permute-done.1.refs_3_, ...), custom_call_target="tpu_custom_call" | custom-call | flops 268000000 | bytes 1572868 | tf_op jit(solution)/shard_map/pallas_call | solution.py:216
  87.4 0.0 copy-start.3
  87.4 24.3 %all_to_all.37.refs_1_ = bf16[128,16,128]{2,1,0:T(8,128)(2,1)S(1)} all-to-all(bf16[128,16,128]{2,1,0:T(8,128)(2,1)S(1)} %bitcast.14), channel_id=1, replica_groups=mesh['y'=4,'zh'=4,'zl'=2,'x'=4,'core'=2] {'zl','y','zh','x'}, dimensions={0} | all-to-all | bytes 1048576 | tf_op jit(solution)/shard_map/all_to_all | solution.py:229
  111.7 1.3 shard_map.91
  113.0 6.9 %all-to-all-start.4 = ((bf16[32,24,128]{2,1,0:T(8,128)(2,1)}), bf16[32,24,128]{2,1,0:T(8,128)(2,1)S(1)}, u32[]{:S(2)}, u32[]{:S(2)}) async-start(bf16[32,24,128]{2,1,0:T(8,128)(2,1)} %bitcast.10), calls=%async_computation.4 | async-start | bytes 393216 | tf_op jit(solution)/shard_map/all_to_all | solution.py:229
  120.0 2.4 %shard_map.92 = (bf16[4,8,32,128]{3,2,1,0:T(8,128)(2,1)}, f32[8,128]{1,0:T(8,128)S(1)}) custom-call(bf16[8,512,128]{2,1,0:T(8,128)(2,1)S(1)} %get-tuple-element.34.refs_0_, bf16[128,512]{1,0:T(8,128)(2,1)S(1)} %copy-done.1, bf16[8,128,128]{2,1,0:T(8,128)(2,1)S(1)} %get-tuple-element.35.refs_2_, bf16[128,128]{1,0:T(8,128)(2,1)S(1)} %copy-done.5, ...), custom_call_target="tpu_custom_call" | custom-call | flops 134000000 | bytes 2002944 | tf_op jit(solution)/shard_map/pallas_call | solution.py:216
  122.4 5.7 %all-to-all-done.4.refs_1_ = bf16[32,24,128]{2,1,0:T(8,128)(2,1)S(1)} async-done(((bf16[32,24,128]{2,1,0:T(8,128)(2,1)}), bf16[32,24,128]{2,1,0:T(8,128)(2,1)S(1)}, u32[]{:S(2)}, u32[]{:S(2)}) %all-to-all-start.4) | async-done | bytes 196640 | tf_op jit(solution)/shard_map/all_to_all | solution.py:229
  128.1 9.6 %all_to_all.38.refs_0_ = bf16[8,24,128]{2,1,0:T(8,128)(2,1)S(1)} all-to-all(bf16[8,24,128]{2,1,0:T(8,128)(2,1)S(1)} %shard_map.93), channel_id=1, replica_groups=mesh['y'=4,'zh'=4,'zl'=2,'x'=4,'core'=2] {'zh','zl'}, dimensions={0} | all-to-all | bytes 98304 | tf_op jit(solution)/shard_map/all_to_all | solution.py:229
  137.7 13.1 %all_to_all.39 = bf16[32,24,128]{2,1,0:T(8,128)(2,1)S(1)} all-to-all(bf16[32,24,128]{2,1,0:T(8,128)(2,1)S(1)} %shard_map.94), channel_id=1, replica_groups=mesh['y'=4,'zh'=4,'zl'=2,'x'=4,'core'=2] {'core','y','x'}, dimensions={0} | all-to-all | bytes 393216 | tf_op jit(solution)/shard_map/all_to_all | solution.py:229
  150.9 0.8 shard_map.95
  (13 shorter events, 0.1 us)
Async XLA Ops:
  0.6 49.2 %copy-start.2 = (bf16[32,32,128]{2,1,0:T(8,128)(2,1)S(1)}, bf16[32,32,128]{2,1,0:T(8,128)(2,1)}, u32[]{:S(2)}) copy-start(bf16[32,32,128]{2,1,0:T(8,128)(2,1)} %param.6) | copy-start | bytes 786436
  0.6 49.2 %copy-start.5 = (bf16[128,128]{1,0:T(8,128)(2,1)S(1)}, bf16[128,128]{1,0:T(8,128)(2,1)}, u32[]{:S(2)}) copy-start(bf16[128,128]{1,0:T(8,128)(2,1)} %refs_3_.3) | copy-start | bytes 98308
  0.7 49.2 %copy-start.4 = (bf16[128,128]{1,0:T(8,128)(2,1)S(1)}, bf16[128,128]{1,0:T(8,128)(2,1)}, u32[]{:S(2)}) copy-start(bf16[128,128]{1,0:T(8,128)(2,1)} %refs_5_.1) | copy-start | bytes 98308
  3.5 46.4 %copy-start = (bf16[8,128,128]{2,1,0:T(8,128)(2,1)S(1)}, bf16[8,128,128]{2,1,0:T(8,128)(2,1)}, u32[]{:S(2)}) copy-start(bf16[8,128,128]{2,1,0:T(8,128)(2,1)} %get-tuple-element.26.refs_0_.refs_1_.refs_3_) | copy-start | bytes 786436
  36.2 3.9 %collective-permute-start = (bf16[2,8,2,4,16,128]{5,4,3,2,1,0:T(8,128)(2,1)S(1)}, bf16[2,8,2,4,16,128]{5,4,3,2,1,0:T(8,128)(2,1)S(1)}, u32[]{:S(2)}, u32[]{:S(2)}) collective-permute-start(bf16[2,8,2,4,16,128]{5,4,3,2,1,0:T(8,128)(2,1)S(1)} %bitcast.12), channel_id=1, source_target_pairs={{0,1},{1,0},{2,3},{3,2},{4,5},{5,4},{6,7},{7,6},{8,9},{9,8},{10,11... | collective-permute-start | bytes 1572872 | tf_op jit(solution)/shard_map/ppermute | solution.py:250
  38.6 45.7 %copy-start.1 = (bf16[128,512]{1,0:T(8,128)(2,1)S(1)}, bf16[128,512]{1,0:T(8,128)(2,1)}, u32[]{:S(2)}) copy-start(bf16[128,512]{1,0:T(8,128)(2,1)} %refs_1_.3) | copy-start | bytes 393220
  41.6 19.5 %all-to-all-start.1 = ((bf16[128,8,128]{2,1,0:T(8,128)(2,1)}), bf16[128,8,128]{2,1,0:T(8,128)(2,1)S(1)}, u32[]{:S(2)}, u32[]{:S(2)}) async-start(bf16[128,8,128]{2,1,0:T(8,128)(2,1)} %bitcast.3), calls=%async_computation.1 | async-start | bytes 524288 | tf_op jit(solution)/shard_map/all_to_all | solution.py:229
  80.9 4.9 %collective-permute-start.1 = (bf16[2,16,4,8,128]{4,3,2,1,0:T(8,128)(2,1)S(1)}, bf16[2,16,4,8,128]{4,3,2,1,0:T(8,128)(2,1)S(1)}, u32[]{:S(2)}, u32[]{:S(2)}) collective-permute-start(bf16[2,16,4,8,128]{4,3,2,1,0:T(8,128)(2,1)S(1)} %bitcast.15), channel_id=1, source_target_pairs={{0,1},{1,0},{2,3},{3,2},{4,5},{5,4},{6,7},{7,6},{8,9},{9,8},{10,11... | collective-permute-start | bytes 786440 | tf_op jit(solution)/shard_map/ppermute | solution.py:262
  87.4 32.6 %copy-start.3 = (bf16[32,32,128]{2,1,0:T(8,128)(2,1)S(1)}, bf16[32,32,128]{2,1,0:T(8,128)(2,1)}, u32[]{:S(2)}) copy-start(bf16[32,32,128]{2,1,0:T(8,128)(2,1)} %param.5) | copy-start | bytes 786436
  113.0 15.0 %all-to-all-start.4 = ((bf16[32,24,128]{2,1,0:T(8,128)(2,1)}), bf16[32,24,128]{2,1,0:T(8,128)(2,1)S(1)}, u32[]{:S(2)}, u32[]{:S(2)}) async-start(bf16[32,24,128]{2,1,0:T(8,128)(2,1)} %bitcast.10), calls=%async_computation.4 | async-start | bytes 393216 | tf_op jit(solution)/shard_map/all_to_all | solution.py:229

commit v5 on v4

--- a/solution.py
+++ b/solution.py
@@ -85,16 +85,16 @@
 
 def pack_a(msg_ref, a_ref):
     for t in range(2):
-        parts = [msg_ref[t, :, :, q][:, :, 0:8].reshape(128, 128) for q in range(4)]
+        parts = [msg_ref[t, :, :, q].astype(F32)[:, :, 0:8].reshape(128, 128) for q in range(4)]
         for g, part in enumerate(regroup(parts)):
-            a_ref[pl.ds(128 * g, 128), pl.ds(128 * t, 128)] = part
+            a_ref[pl.ds(128 * g, 128), pl.ds(128 * t, 128)] = part.astype(BF)
 
 
 def pack_b(msg_ref, half, b_ref):
     for t in range(2):
-        parts = [msg_ref[t, :, half, q][:, 8:16].reshape(64, 128) for q in range(4)]
+        parts = [msg_ref[t, :, half, q].astype(F32)[:, 8:16].reshape(64, 128) for q in range(4)]
         parts = [part.reshape(8, 8, 128) for part in regroup(parts)]
-        b_ref[:, pl.ds(128 * t, 128)] = jnp.stack(parts, axis=1).reshape(256, 128)
+        b_ref[:, pl.ds(128 * t, 128)] = jnp.stack(parts, axis=1).reshape(256, 128).astype(BF)
 
 
 def pack_kernel(msg_ref, a_ref, b_ref):
@@ -146,9 +146,9 @@
     for n, ref in enumerate((own_ref, other_ref)):
         half = core_ref[0] if n == 0 else 1 - core_ref[0]
         for t in range(2):
-            parts = [ref[t, :, q].reshape(128, 128) for q in range(4)]
+            parts = [ref[t, :, q].astype(F32).reshape(128, 128) for q in range(4)]
             for g, part in enumerate(regroup(parts)):
-                dx[half, pl.ds(128 * g, 128), pl.ds(128 * t, 128)] = part
+                dx[half, pl.ds(128 * g, 128), pl.ds(128 * t, 128)] = part.astype(BF)
     da = dot(dx[0], b_ref[0]) + dot(dx[1], b_ref[1])
     for t in range(2):
         parts = [da[128 * g : 128 * g + 128, 128 * t : 128 * t + 128] for g in range(4)]

time: 152 us -> 152 us (level)
  no operation moved by 1% of the time
where the time goes in v5:
time: 152 us
  blocking collectives  98.9 us (65%)
  starting transfers between devices  21 us (14%)
  waiting for transfers between devices  16.7 us (11%)
  Pallas kernels  14.2 us (9%)
    all_to_all x5, blocking collectives, exchange(): return lax.all_to_all(values, axes, 0, 0, tiled=True)  98.9 us
    all_to_all x2, waiting for transfers between devices, exchange(): return lax.all_to_all(values, axes, 0, 0, tiled=True)  15.9 us
    all_to_all x2, starting transfers between devices, exchange(): return lax.all_to_all(values, axes, 0, 0, tiled=True)  15.2 us
    pallas_call x12, Pallas kernels, run(): pl.pallas_call(lambda *refs: kernel(*refs[skip:]), out_shape=outs, in_spe...  14.2 us
    ppermute x1, starting transfers between devices, per_device(): other = lax.ppermute(dx, 'core', SWAP)  3.4 us
  transfers between devices with their start and end apart: 4, of which 3 were waited for; matrix products, arithmetic and copies ran while one was open for 0% of the time, Pallas kernels for 4%

profile of v5, /device:TPU:1, one launch (start us, length us, event | category | flops | bytes accessed | tf_op | source)
XLA Modules:
  0.0 151.7 jit_solution(10360833314228185364)
XLA Ops:
  0.7 2.8 %shard_map.84 = (bf16[128,16,128]{2,1,0:T(8,128)(2,1)}, bf16[8,128,128]{2,1,0:T(8,128)(2,1)}) custom-call(bf16[4,8,32,128]{3,2,1,0:T(8,128)(2,1)} %bitcast.21, bf16[128,512]{1,0:T(8,128)(2,1)} %refs_1_.3), custom_call_target="tpu_custom_call" | custom-call | flops 134000000 | bytes 1179648 | tf_op jit(solution)/shard_map/pallas_call | solution.py:216
  3.5 0.0 copy-start
  3.5 32.7 %all_to_all.35 = bf16[128,16,128]{2,1,0:T(8,128)(2,1)S(1)} all-to-all(bf16[128,16,128]{2,1,0:T(8,128)(2,1)} %get-tuple-element.23), channel_id=1, replica_groups=mesh['y'=4,'zh'=4,'zl'=2,'x'=4,'core'=2] {'zl','y','zh','x'}, dimensions={0} | all-to-all | bytes 1048576 | tf_op jit(solution)/shard_map/all_to_all | solution.py:229
  36.2 2.4 %collective-permute-start = (bf16[2,8,2,4,16,128]{5,4,3,2,1,0:T(8,128)(2,1)S(1)}, bf16[2,8,2,4,16,128]{5,4,3,2,1,0:T(8,128)(2,1)S(1)}, u32[]{:S(2)}, u32[]{:S(2)}) collective-permute-start(bf16[2,8,2,4,16,128]{5,4,3,2,1,0:T(8,128)(2,1)S(1)} %bitcast.12), channel_id=1, source_target_pairs={{0,1},{1,0},{2,3},{3,2},{4,5},{5,4},{6,7},{7,6},{8,9},{9,8},{10,11... | collective-permute-start | bytes 1572872 | tf_op jit(solution)/shard_map/ppermute | solution.py:250
  38.6 0.7 shard_map.85
  39.3 0.8 collective-permute-done.refs_3_
  40.1 1.6 %shard_map.86 = bf16[2,16,4,8,128]{4,3,2,1,0:T(8,128)(2,1)} custom-call(s32[1]{0:T(128)} %bitcast.refs_0_.refs_1_, bf16[512,256]{1,0:T(8,128)(2,1)S(1)} %get-tuple-element.24.refs_1_.refs_4_, bf16[2,256,256]{2,1,0:T(8,128)(2,1)S(1)} %get-tuple-element.25.refs_2_.refs_5_, bf16[2,8,2,4,16,128]{5,4,3,2,1,0:T(8,128)(2,1)S(1)} %collective-permute-done.refs_3_), custom_call_target="tpu_custom_call" | custom-call | flops 134000000 | bytes 1310724 | tf_op jit(solution)/shard_map/pallas_call | solution.py:216
  41.7 8.3 %all-to-all-start.1 = ((bf16[128,8,128]{2,1,0:T(8,128)(2,1)}), bf16[128,8,128]{2,1,0:T(8,128)(2,1)S(1)}, u32[]{:S(2)}, u32[]{:S(2)}) async-start(bf16[128,8,128]{2,1,0:T(8,128)(2,1)} %bitcast.3), calls=%async_computation.1 | async-start | bytes 524288 | tf_op jit(solution)/shard_map/all_to_all | solution.py:229
  50.0 0.9 shard_map.87
  51.0 10.2 %all-to-all-done.1.refs_0_ = bf16[128,8,128]{2,1,0:T(8,128)(2,1)S(1)} async-done(((bf16[128,8,128]{2,1,0:T(8,128)(2,1)}), bf16[128,8,128]{2,1,0:T(8,128)(2,1)S(1)}, u32[]{:S(2)}, u32[]{:S(2)}) %all-to-all-start.1) | async-done | bytes 262176 | tf_op jit(solution)/shard_map/all_to_all | solution.py:229
  61.2 0.5 shard_map.88
  61.7 19.3 %all_to_all.36 = bf16[128,8,128]{2,1,0:T(8,128)(2,1)S(1)} all-to-all(bf16[128,8,128]{2,1,0:T(8,128)(2,1)S(1)} %get-tuple-element.32), channel_id=1, replica_groups=mesh['y'=4,'zh'=4,'zl'=2,'x'=4,'core'=2] {'zl','y','zh','x'}, dimensions={0} | all-to-all | bytes 524288 | tf_op jit(solution)/shard_map/all_to_all | solution.py:229
  81.0 3.4 %collective-permute-start.1 = (bf16[2,16,4,8,128]{4,3,2,1,0:T(8,128)(2,1)S(1)}, bf16[2,16,4,8,128]{4,3,2,1,0:T(8,128)(2,1)S(1)}, u32[]{:S(2)}, u32[]{:S(2)}) collective-permute-start(bf16[2,16,4,8,128]{4,3,2,1,0:T(8,128)(2,1)S(1)} %bitcast.15), channel_id=1, source_target_pairs={{0,1},{1,0},{2,3},{3,2},{4,5},{5,4},{6,7},{7,6},{8,9},{9,8},{10,11... | collective-permute-start | bytes 786440 | tf_op jit(solution)/shard_map/ppermute | solution.py:262
  84.4 1.5 shard_map.89
  86.0 1.5 %shard_map.90 = bf16[2,8,2,4,16,128]{5,4,3,2,1,0:T(8,128)(2,1)S(1)} custom-call(bf16[256,128]{1,0:T(8,128)(2,1)S(1)} %get-tuple-element.31.refs_0_, s32[1]{0:T(128)} %bitcast.refs_0_.refs_1_, bf16[2,16,4,8,128]{4,3,2,1,0:T(8,128)(2,1)S(1)} %bitcast.16, bf16[2,16,4,8,128]{4,3,2,1,0:T(8,128)(2,1)S(1)} %collective-permute-done.1.refs_3_, ...), custom_call_target="tpu_custom_call" | custom-call | flops 268000000 | bytes 1572868 | tf_op jit(solution)/shard_map/pallas_call | solution.py:216
  87.5 0.0 copy-start.3
  87.5 24.1 %all_to_all.37.refs_1_ = bf16[128,16,128]{2,1,0:T(8,128)(2,1)S(1)} all-to-all(bf16[128,16,128]{2,1,0:T(8,128)(2,1)S(1)} %bitcast.14), channel_id=1, replica_groups=mesh['y'=4,'zh'=4,'zl'=2,'x'=4,'core'=2] {'zl','y','zh','x'}, dimensions={0} | all-to-all | bytes 1048576 | tf_op jit(solution)/shard_map/all_to_all | solution.py:229
  111.6 1.3 shard_map.91
  113.0 6.9 %all-to-all-start.4 = ((bf16[32,24,128]{2,1,0:T(8,128)(2,1)}), bf16[32,24,128]{2,1,0:T(8,128)(2,1)S(1)}, u32[]{:S(2)}, u32[]{:S(2)}) async-start(bf16[32,24,128]{2,1,0:T(8,128)(2,1)} %bitcast.10), calls=%async_computation.4 | async-start | bytes 393216 | tf_op jit(solution)/shard_map/all_to_all | solution.py:229
  119.9 2.4 %shard_map.92 = (bf16[4,8,32,128]{3,2,1,0:T(8,128)(2,1)}, f32[8,128]{1,0:T(8,128)S(1)}) custom-call(bf16[8,512,128]{2,1,0:T(8,128)(2,1)S(1)} %get-tuple-element.34.refs_0_, bf16[128,512]{1,0:T(8,128)(2,1)S(1)} %copy-done.1, bf16[8,128,128]{2,1,0:T(8,128)(2,1)S(1)} %get-tuple-element.35.refs_2_, bf16[128,128]{1,0:T(8,128)(2,1)S(1)} %copy-done.5, ...), custom_call_target="tpu_custom_call" | custom-call | flops 134000000 | bytes 2002944 | tf_op jit(solution)/shard_map/pallas_call | solution.py:216
  122.3 5.7 %all-to-all-done.4.refs_1_ = bf16[32,24,128]{2,1,0:T(8,128)(2,1)S(1)} async-done(((bf16[32,24,128]{2,1,0:T(8,128)(2,1)}), bf16[32,24,128]{2,1,0:T(8,128)(2,1)S(1)}, u32[]{:S(2)}, u32[]{:S(2)}) %all-to-all-start.4) | async-done | bytes 196640 | tf_op jit(solution)/shard_map/all_to_all | solution.py:229
  128.0 9.6 %all_to_all.38.refs_0_ = bf16[8,24,128]{2,1,0:T(8,128)(2,1)S(1)} all-to-all(bf16[8,24,128]{2,1,0:T(8,128)(2,1)S(1)} %shard_map.93), channel_id=1, replica_groups=mesh['y'=4,'zh'=4,'zl'=2,'x'=4,'core'=2] {'zh','zl'}, dimensions={0} | all-to-all | bytes 98304 | tf_op jit(solution)/shard_map/all_to_all | solution.py:229
  137.7 13.1 %all_to_all.39 = bf16[32,24,128]{2,1,0:T(8,128)(2,1)S(1)} all-to-all(bf16[32,24,128]{2,1,0:T(8,128)(2,1)S(1)} %shard_map.94), channel_id=1, replica_groups=mesh['y'=4,'zh'=4,'zl'=2,'x'=4,'core'=2] {'core','y','x'}, dimensions={0} | all-to-all | bytes 393216 | tf_op jit(solution)/shard_map/all_to_all | solution.py:229
  150.8 0.8 shard_map.95
  (13 shorter events, 0.1 us)
Async XLA Ops:
  0.6 49.4 %copy-start.2 = (bf16[32,32,128]{2,1,0:T(8,128)(2,1)S(1)}, bf16[32,32,128]{2,1,0:T(8,128)(2,1)}, u32[]{:S(2)}) copy-start(bf16[32,32,128]{2,1,0:T(8,128)(2,1)} %param.6) | copy-start | bytes 786436
  0.6 49.4 %copy-start.5 = (bf16[128,128]{1,0:T(8,128)(2,1)S(1)}, bf16[128,128]{1,0:T(8,128)(2,1)}, u32[]{:S(2)}) copy-start(bf16[128,128]{1,0:T(8,128)(2,1)} %refs_3_.3) | copy-start | bytes 98308
  0.7 49.4 %copy-start.4 = (bf16[128,128]{1,0:T(8,128)(2,1)S(1)}, bf16[128,128]{1,0:T(8,128)(2,1)}, u32[]{:S(2)}) copy-start(bf16[128,128]{1,0:T(8,128)(2,1)} %refs_5_.1) | copy-start | bytes 98308
  3.5 46.6 %copy-start = (bf16[8,128,128]{2,1,0:T(8,128)(2,1)S(1)}, bf16[8,128,128]{2,1,0:T(8,128)(2,1)}, u32[]{:S(2)}) copy-start(bf16[8,128,128]{2,1,0:T(8,128)(2,1)} %get-tuple-element.26.refs_0_.refs_1_.refs_3_) | copy-start | bytes 786436
  36.2 3.9 %collective-permute-start = (bf16[2,8,2,4,16,128]{5,4,3,2,1,0:T(8,128)(2,1)S(1)}, bf16[2,8,2,4,16,128]{5,4,3,2,1,0:T(8,128)(2,1)S(1)}, u32[]{:S(2)}, u32[]{:S(2)}) collective-permute-start(bf16[2,8,2,4,16,128]{5,4,3,2,1,0:T(8,128)(2,1)S(1)} %bitcast.12), channel_id=1, source_target_pairs={{0,1},{1,0},{2,3},{3,2},{4,5},{5,4},{6,7},{7,6},{8,9},{9,8},{10,11... | collective-permute-start | bytes 1572872 | tf_op jit(solution)/shard_map/ppermute | solution.py:250
  38.6 45.9 %copy-start.1 = (bf16[128,512]{1,0:T(8,128)(2,1)S(1)}, bf16[128,512]{1,0:T(8,128)(2,1)}, u32[]{:S(2)}) copy-start(bf16[128,512]{1,0:T(8,128)(2,1)} %refs_1_.3) | copy-start | bytes 393220
  41.7 19.5 %all-to-all-start.1 = ((bf16[128,8,128]{2,1,0:T(8,128)(2,1)}), bf16[128,8,128]{2,1,0:T(8,128)(2,1)S(1)}, u32[]{:S(2)}, u32[]{:S(2)}) async-start(bf16[128,8,128]{2,1,0:T(8,128)(2,1)} %bitcast.3), calls=%async_computation.1 | async-start | bytes 524288 | tf_op jit(solution)/shard_map/all_to_all | solution.py:229
  81.0 4.9 %collective-permute-start.1 = (bf16[2,16,4,8,128]{4,3,2,1,0:T(8,128)(2,1)S(1)}, bf16[2,16,4,8,128]{4,3,2,1,0:T(8,128)(2,1)S(1)}, u32[]{:S(2)}, u32[]{:S(2)}) collective-permute-start(bf16[2,16,4,8,128]{4,3,2,1,0:T(8,128)(2,1)S(1)} %bitcast.15), channel_id=1, source_target_pairs={{0,1},{1,0},{2,3},{3,2},{4,5},{5,4},{6,7},{7,6},{8,9},{9,8},{10,11... | collective-permute-start | bytes 786440 | tf_op jit(solution)/shard_map/ppermute | solution.py:262
  87.5 32.4 %copy-start.3 = (bf16[32,32,128]{2,1,0:T(8,128)(2,1)S(1)}, bf16[32,32,128]{2,1,0:T(8,128)(2,1)}, u32[]{:S(2)}) copy-start(bf16[32,32,128]{2,1,0:T(8,128)(2,1)} %param.5) | copy-start | bytes 786436
  113.0 15.0 %all-to-all-start.4 = ((bf16[32,24,128]{2,1,0:T(8,128)(2,1)}), bf16[32,24,128]{2,1,0:T(8,128)(2,1)S(1)}, u32[]{:S(2)}, u32[]{:S(2)}) async-start(bf16[32,24,128]{2,1,0:T(8,128)(2,1)} %bitcast.10), calls=%async_computation.4 | async-start | bytes 393216 | tf_op jit(solution)/shard_map/all_to_all | solution.py:229

commit v6 on v5

--- a/solution.py
+++ b/solution.py
@@ -77,7 +77,7 @@
         gate = jax.nn.sigmoid(dot(norm_ref[s], gw))
         upstream = cot_ref[:, s].astype(F32).reshape(128, 128)
         dout = upstream * gate
-        g2_ref[s] = dout * (1.0 - gate)
+        g2_ref[s] = (dout * (1.0 - gate)).T
         dout = dout.astype(BF)
         dout_ref[s] = dout
         dxn_ref[pl.ds(s, 128, stride=8), :] = dot(ow, dout, ((1,), (1,)))
@@ -97,17 +97,20 @@
         b_ref[:, pl.ds(128 * t, 128)] = jnp.stack(parts, axis=1).reshape(256, 128).astype(BF)
 
 
-def pack_kernel(msg_ref, a_ref, b_ref):
+def pack_kernel(core_ref, msg_ref, a_ref, b_ref, send_ref):
     pack_a(msg_ref, a_ref)
     for half in range(2):
         pack_b(msg_ref, half, b_ref.at[half])
-
-
-def x_kernel(core_ref, a_ref, b_ref, other_ref, msg_ref, oa_ref, ob_ref):
-    core = core_ref[0]
-    pack_a(other_ref, oa_ref)
-    pack_b(other_ref, core, ob_ref)
-    x = dot(a_ref[...], b_ref[core], ((1,), (1,))) + dot(oa_ref[...], ob_ref[...], ((1,), (1,)))
+    send_ref[0:512] = a_ref[...]
+    send_ref[512:768] = b_ref[1 - core_ref[0]]
+
+
+def keep_kernel(core_ref, a_ref, b_ref, keep_ref):
+    keep_ref[...] = dot(a_ref[...], b_ref[core_ref[0]], ((1,), (1,)))
+
+
+def x_kernel(keep_ref, got_ref, msg_ref):
+    x = keep_ref[...] + dot(got_ref[0:512], got_ref[512:768], ((1,), (1,)))
     for t in range(2):
         parts = [x[128 * g : 128 * g + 128, 128 * t : 128 * t + 128] for g in range(4)]
         for q, part in enumerate(regroup(parts)):
@@ -122,14 +125,14 @@
 
 def late_kernel(xhat_ref, norm_ref, g2_ref, dout_ref, w_ref, ow_ref, sum_ref, dgate_ref, fac_ref):
     w = w_ref[...]
-    ow = ow_ref[...]
+    ow = ow_ref[...].T
     gate_part = jnp.zeros((128, 128), F32)
     out_part = jnp.zeros((128, 128), F32)
     for s in range(8):
         normed = norm_ref[s]
         xnorm = xhat_ref[pl.ds(s, 128, stride=8), :].astype(BF)
-        dgate = (g2_ref[s] * dot(xnorm, ow, ((0,), (0,)))).astype(BF)
-        gate_part += dot(normed, dgate, ((0,), (0,)))
+        dgate = (g2_ref[s] * dot(ow, xnorm)).astype(BF)
+        gate_part += dot(dgate, normed)
         out_part += dot(xnorm, dout_ref[s])
         dgate_ref[s] = dgate
         proj = dot(w, normed, ((0,), (1,)))
@@ -138,7 +141,7 @@
             sig = jax.nn.sigmoid(proj[256 * n + 128 : 256 * n + 256])
             fac_ref[s, 256 * n : 256 * n + 128] = sig
             fac_ref[s, 256 * n + 128 : 256 * n + 256] = val * sig * (1.0 - sig)
-    sum_ref[0:128] = gate_part.astype(BF)
+    sum_ref[0:128] = gate_part.T.astype(BF)
     sum_ref[128:256] = out_part.astype(BF)
 
 
@@ -190,7 +193,7 @@
     gw = gw_ref[...]
     for s in range(8):
         zhat, zinv = layer_norm(pair_ref[:, s].astype(F32).reshape(128, 128))
-        dnormed = dot(dproj_ref[s], w, ((0,), (1,))) + dot(dgate_ref[s], gw, ((1,), (1,)))
+        dnormed = dot(dproj_ref[s], w, ((0,), (1,))) + dot(dgate_ref[s], gw, ((0,), (1,)))
         grad = layer_norm_backward(dnormed, zhat, zinv)
         out_ref[:, s] = grad.reshape(4, 32, 128).astype(BF)
 
@@ -247,12 +250,13 @@
         side_kernel, [((8, 128, 128), F32), ((8, 128, 128), BF), ((1024, 128), F32)],
         normed, cotangent, gate_weight, out_weight, flops=67_000_000,
     )
-    other = lax.ppermute(msg, "core", SWAP)
-    a_own, b_own = run(pack_kernel, [((512, 256), BF), ((2, 256, 256), BF)], msg, flops=1_000_000)
-    x = run(
-        x_kernel, [((2, 16, 4, 8, 128), BF)], core, a_own, b_own, other, scalars=1, flops=134_000_000,
-        scratch=[pltpu.VMEM((512, 256), BF), pltpu.VMEM((256, 256), BF)],
-    )
+    a_own, b_own, send = run(
+        pack_kernel, [((512, 256), BF), ((2, 256, 256), BF), ((768, 256), BF)], core, msg, scalars=1,
+        flops=1_000_000,
+    )
+    got = lax.ppermute(send, "core", SWAP)
+    keep = run(keep_kernel, [((512, 256), F32)], core, a_own, b_own, scalars=1, flops=67_000_000)
+    x = run(x_kernel, [((2, 16, 4, 8, 128), BF)], keep, got, flops=67_000_000)
     x = exchange(x.reshape(128, 8, 128), OWNERS)
     dx, xhat = run(
         dx_kernel, [((128, 8, 128), BF), ((128, 8, 128), F32)], x, dxnorm.reshape(128, 8, 128), flops=1_000_000

time: 152 us -> 152 us (level)
  blocking collectives: 98.9 us -> 66.4 us
  starting transfers between devices: 21 us -> 37.6 us
  waiting for transfers between devices: 16.7 us -> 33.1 us
    all_to_all x5 -> x4, blocking collectives: 98.9 us -> 66.4 us  [exchange(): return lax.all_to_all(values, axes, 0, 0, tiled=True)]
    all_to_all x2 -> x3, starting transfers between devices: 15.2 us -> 31.7 us  [exchange(): return lax.all_to_all(values, axes, 0, 0, tiled=True)]
    all_to_all x2 -> x3, waiting for transfers between devices: 15.9 us -> 32 us  [exchange(): return lax.all_to_all(values, axes, 0, 0, tiled=True)]
    pallas_call x12 -> x13, Pallas kernels: 14.2 us -> 14 us  [run(): pl.pallas_call(lambda *refs: kernel(*refs[skip:]), out_shape=outs, in_spe...]
  transfers between devices with their start and end apart: 4 -> 5, of which waited for: 3 -> 4; matrix products, arithmetic and copies ran while one was open for 0% -> 0% of each run, Pallas kernels for 4% -> 3%
where the time goes in v6:
time: 152 us
  blocking collectives  66.4 us (44%)
  starting transfers between devices  37.6 us (25%)
  waiting for transfers between devices  33.1 us (22%)
  Pallas kernels  14 us (9%)
    all_to_all x4, blocking collectives, exchange(): return lax.all_to_all(values, axes, 0, 0, tiled=True)  66.4 us
    all_to_all x3, waiting for transfers between devices, exchange(): return lax.all_to_all(values, axes, 0, 0, tiled=True)  32 us
    all_to_all x3, starting transfers between devices, exchange(): return lax.all_to_all(values, axes, 0, 0, tiled=True)  31.7 us
    pallas_call x13, Pallas kernels, run(): pl.pallas_call(lambda *refs: kernel(*refs[skip:]), out_shape=outs, in_spe...  14 us
    ppermute x1, starting transfers between devices, per_device(): other = lax.ppermute(dx, 'core', SWAP)  3.4 us
  transfers between devices with their start and end apart: 5, of which 4 were waited for; matrix products, arithmetic and copies ran while one was open for 0% of the time, Pallas kernels for 3%

profile of v6, /device:TPU:1, one launch (start us, length us, event | category | flops | bytes accessed | tf_op | source)
XLA Modules:
  0.0 151.9 jit_solution(18103283371922744408)
XLA Ops:
  0.6 2.8 %shard_map.84 = (bf16[128,16,128]{2,1,0:T(8,128)(2,1)}, bf16[8,128,128]{2,1,0:T(8,128)(2,1)}) custom-call(bf16[4,8,32,128]{3,2,1,0:T(8,128)(2,1)} %bitcast.20, bf16[128,512]{1,0:T(8,128)(2,1)} %refs_1_.3), custom_call_target="tpu_custom_call" | custom-call | flops 134000000 | bytes 1179648 | tf_op jit(solution)/shard_map/pallas_call | solution.py:219
  3.5 16.5 %all-to-all-start = ((bf16[128,16,128]{2,1,0:T(8,128)(2,1)}), bf16[128,16,128]{2,1,0:T(8,128)(2,1)S(1)}, u32[]{:S(2)}, u32[]{:S(2)}) async-start(bf16[128,16,128]{2,1,0:T(8,128)(2,1)} %get-tuple-element.24), calls=%async_computation | async-start | bytes 1048576 | tf_op jit(solution)/shard_map/all_to_all | solution.py:232
  20.0 16.2 %all-to-all-done = bf16[128,16,128]{2,1,0:T(8,128)(2,1)S(1)} async-done(((bf16[128,16,128]{2,1,0:T(8,128)(2,1)}), bf16[128,16,128]{2,1,0:T(8,128)(2,1)S(1)}, u32[]{:S(2)}, u32[]{:S(2)}) %all-to-all-start) | async-done | bytes 524320 | tf_op jit(solution)/shard_map/all_to_all | solution.py:232
  36.2 0.7 shard_map.85
  36.9 2.5 %collective-permute-start = (bf16[768,256]{1,0:T(8,128)(2,1)S(1)}, bf16[768,256]{1,0:T(8,128)(2,1)S(1)}, u32[]{:S(2)}, u32[]{:S(2)}) collective-permute-start(bf16[768,256]{1,0:T(8,128)(2,1)S(1)} %get-tuple-element.27), channel_id=1, source_target_pairs={{0,1},{1,0},{2,3},{3,2},{4,5},{5,4},{6,7},{7,6},{8,9},{9,8},{10,11... | collective-permute-start | bytes 1179656 | tf_op jit(solution)/shard_map/ppermute | solution.py:257
  39.4 0.2 shard_map.86.refs_0_
  39.6 1.1 collective-permute-done.refs_1_
  40.7 1.1 shard_map.87
  41.8 8.3 %all-to-all-start.1 = ((bf16[128,8,128]{2,1,0:T(8,128)(2,1)}), bf16[128,8,128]{2,1,0:T(8,128)(2,1)S(1)}, u32[]{:S(2)}, u32[]{:S(2)}) async-start(bf16[128,8,128]{2,1,0:T(8,128)(2,1)} %bitcast.3), calls=%async_computation.1 | async-start | bytes 524288 | tf_op jit(solution)/shard_map/all_to_all | solution.py:232
  50.2 0.9 shard_map.88
  51.1 10.2 %all-to-all-done.1.refs_0_ = bf16[128,8,128]{2,1,0:T(8,128)(2,1)S(1)} async-done(((bf16[128,8,128]{2,1,0:T(8,128)(2,1)}), bf16[128,8,128]{2,1,0:T(8,128)(2,1)S(1)}, u32[]{:S(2)}, u32[]{:S(2)}) %all-to-all-start.1) | async-done | bytes 262176 | tf_op jit(solution)/shard_map/all_to_all | solution.py:232
  61.3 0.5 shard_map.89
  61.8 19.3 %all_to_all.35 = bf16[128,8,128]{2,1,0:T(8,128)(2,1)S(1)} all-to-all(bf16[128,8,128]{2,1,0:T(8,128)(2,1)S(1)} %get-tuple-element.34), channel_id=1, replica_groups=mesh['y'=4,'zh'=4,'zl'=2,'x'=4,'core'=2] {'zl','y','zh','x'}, dimensions={0} | all-to-all | bytes 524288 | tf_op jit(solution)/shard_map/all_to_all | solution.py:232
  81.1 3.4 %collective-permute-start.1 = (bf16[2,16,4,8,128]{4,3,2,1,0:T(8,128)(2,1)S(1)}, bf16[2,16,4,8,128]{4,3,2,1,0:T(8,128)(2,1)S(1)}, u32[]{:S(2)}, u32[]{:S(2)}) collective-permute-start(bf16[2,16,4,8,128]{4,3,2,1,0:T(8,128)(2,1)S(1)} %bitcast.14), channel_id=1, source_target_pairs={{0,1},{1,0},{2,3},{3,2},{4,5},{5,4},{6,7},{7,6},{8,9},{9,8},{10,11... | collective-permute-start | bytes 786440 | tf_op jit(solution)/shard_map/ppermute | solution.py:266
  84.5 1.5 shard_map.90
  86.0 1.5 %shard_map.91 = bf16[2,8,2,4,16,128]{5,4,3,2,1,0:T(8,128)(2,1)S(1)} custom-call(bf16[256,128]{1,0:T(8,128)(2,1)S(1)} %get-tuple-element.33.refs_0_, s32[1]{0:T(128)} %bitcast.refs_0_.refs_1_, bf16[2,16,4,8,128]{4,3,2,1,0:T(8,128)(2,1)S(1)} %bitcast.15, bf16[2,16,4,8,128]{4,3,2,1,0:T(8,128)(2,1)S(1)} %collective-permute-done.1.refs_3_, ...), custom_call_target="tpu_custom_call" | custom-call | flops 268000000 | bytes 1572868 | tf_op jit(solution)/shard_map/pallas_call | solution.py:219
  87.6 24.3 %all_to_all.36.refs_1_ = bf16[128,16,128]{2,1,0:T(8,128)(2,1)S(1)} all-to-all(bf16[128,16,128]{2,1,0:T(8,128)(2,1)S(1)} %bitcast.13), channel_id=1, replica_groups=mesh['y'=4,'zh'=4,'zl'=2,'x'=4,'core'=2] {'zl','y','zh','x'}, dimensions={0} | all-to-all | bytes 1048576 | tf_op jit(solution)/shard_map/all_to_all | solution.py:232
  111.8 1.3 shard_map.92
  113.2 7.0 %all-to-all-start.4 = ((bf16[32,24,128]{2,1,0:T(8,128)(2,1)}), bf16[32,24,128]{2,1,0:T(8,128)(2,1)S(1)}, u32[]{:S(2)}, u32[]{:S(2)}) async-start(bf16[32,24,128]{2,1,0:T(8,128)(2,1)} %bitcast.10), calls=%async_computation.4 | async-start | bytes 393216 | tf_op jit(solution)/shard_map/all_to_all | solution.py:232
  120.1 2.5 %shard_map.93 = (bf16[4,8,32,128]{3,2,1,0:T(8,128)(2,1)}, f32[8,128]{1,0:T(8,128)S(1)}) custom-call(bf16[8,512,128]{2,1,0:T(8,128)(2,1)S(1)} %get-tuple-element.36.refs_0_, bf16[128,512]{1,0:T(8,128)(2,1)S(1)} %copy-done.1, bf16[8,128,128]{2,1,0:T(8,128)(2,1)S(1)} %get-tuple-element.37.refs_2_, bf16[128,128]{1,0:T(8,128)(2,1)S(1)} %copy-done.5, ...), custom_call_target="tpu_custom_call" | custom-call | flops 134000000 | bytes 2002944 | tf_op jit(solution)/shard_map/pallas_call | solution.py:219
  122.7 5.5 %all-to-all-done.4.refs_1_ = bf16[32,24,128]{2,1,0:T(8,128)(2,1)S(1)} async-done(((bf16[32,24,128]{2,1,0:T(8,128)(2,1)}), bf16[32,24,128]{2,1,0:T(8,128)(2,1)S(1)}, u32[]{:S(2)}, u32[]{:S(2)}) %all-to-all-start.4) | async-done | bytes 196640 | tf_op jit(solution)/shard_map/all_to_all | solution.py:232
  128.3 9.6 %all_to_all.37.refs_0_ = bf16[8,24,128]{2,1,0:T(8,128)(2,1)S(1)} all-to-all(bf16[8,24,128]{2,1,0:T(8,128)(2,1)S(1)} %shard_map.94), channel_id=1, replica_groups=mesh['y'=4,'zh'=4,'zl'=2,'x'=4,'core'=2] {'zh','zl'}, dimensions={0} | all-to-all | bytes 98304 | tf_op jit(solution)/shard_map/all_to_all | solution.py:232
  137.9 13.1 %all_to_all.38 = bf16[32,24,128]{2,1,0:T(8,128)(2,1)S(1)} all-to-all(bf16[32,24,128]{2,1,0:T(8,128)(2,1)S(1)} %shard_map.95), channel_id=1, replica_groups=mesh['y'=4,'zh'=4,'zl'=2,'x'=4,'core'=2] {'core','y','x'}, dimensions={0} | all-to-all | bytes 393216 | tf_op jit(solution)/shard_map/all_to_all | solution.py:232
  151.1 0.8 shard_map.96
  (15 shorter events, 0.1 us)
Async XLA Ops:
  3.4 46.7 %copy-start = (bf16[8,128,128]{2,1,0:T(8,128)(2,1)S(1)}, bf16[8,128,128]{2,1,0:T(8,128)(2,1)}, u32[]{:S(2)}) copy-start(bf16[8,128,128]{2,1,0:T(8,128)(2,1)} %get-tuple-element.28.refs_0_.refs_1_.refs_3_) | copy-start | bytes 786436
  3.4 46.7 %copy-start.2 = (bf16[32,32,128]{2,1,0:T(8,128)(2,1)S(1)}, bf16[32,32,128]{2,1,0:T(8,128)(2,1)}, u32[]{:S(2)}) copy-start(bf16[32,32,128]{2,1,0:T(8,128)(2,1)} %param.6) | copy-start | bytes 786436
  3.4 46.7 %copy-start.4 = (bf16[128,128]{1,0:T(8,128)(2,1)S(1)}, bf16[128,128]{1,0:T(8,128)(2,1)}, u32[]{:S(2)}) copy-start(bf16[128,128]{1,0:T(8,128)(2,1)} %refs_5_.1) | copy-start | bytes 98308
  3.5 46.7 %copy-start.5 = (bf16[128,128]{1,0:T(8,128)(2,1)S(1)}, bf16[128,128]{1,0:T(8,128)(2,1)}, u32[]{:S(2)}) copy-start(bf16[128,128]{1,0:T(8,128)(2,1)} %refs_3_.3) | copy-start | bytes 98308
  3.5 32.7 %all-to-all-start = ((bf16[128,16,128]{2,1,0:T(8,128)(2,1)}), bf16[128,16,128]{2,1,0:T(8,128)(2,1)S(1)}, u32[]{:S(2)}, u32[]{:S(2)}) async-start(bf16[128,16,128]{2,1,0:T(8,128)(2,1)} %get-tuple-element.24), calls=%async_computation | async-start | bytes 1048576 | tf_op jit(solution)/shard_map/all_to_all | solution.py:232
  36.9 3.8 %collective-permute-start = (bf16[768,256]{1,0:T(8,128)(2,1)S(1)}, bf16[768,256]{1,0:T(8,128)(2,1)S(1)}, u32[]{:S(2)}, u32[]{:S(2)}) collective-permute-start(bf16[768,256]{1,0:T(8,128)(2,1)S(1)} %get-tuple-element.27), channel_id=1, source_target_pairs={{0,1},{1,0},{2,3},{3,2},{4,5},{5,4},{6,7},{7,6},{8,9},{9,8},{10,11... | collective-permute-start | bytes 1179656 | tf_op jit(solution)/shard_map/ppermute | solution.py:257
  39.4 45.2 %copy-start.1 = (bf16[128,512]{1,0:T(8,128)(2,1)S(1)}, bf16[128,512]{1,0:T(8,128)(2,1)}, u32[]{:S(2)}) copy-start(bf16[128,512]{1,0:T(8,128)(2,1)} %refs_1_.3) | copy-start | bytes 393220
  41.8 19.5 %all-to-all-start.1 = ((bf16[128,8,128]{2,1,0:T(8,128)(2,1)}), bf16[128,8,128]{2,1,0:T(8,128)(2,1)S(1)}, u32[]{:S(2)}, u32[]{:S(2)}) async-start(bf16[128,8,128]{2,1,0:T(8,128)(2,1)} %bitcast.3), calls=%async_computation.1 | async-start | bytes 524288 | tf_op jit(solution)/shard_map/all_to_all | solution.py:232
  81.1 4.9 %collective-permute-start.1 = (bf16[2,16,4,8,128]{4,3,2,1,0:T(8,128)(2,1)S(1)}, bf16[2,16,4,8,128]{4,3,2,1,0:T(8,128)(2,1)S(1)}, u32[]{:S(2)}, u32[]{:S(2)}) collective-permute-start(bf16[2,16,4,8,128]{4,3,2,1,0:T(8,128)(2,1)S(1)} %bitcast.14), channel_id=1, source_target_pairs={{0,1},{1,0},{2,3},{3,2},{4,5},{5,4},{6,7},{7,6},{8,9},{9,8},{10,11... | collective-permute-start | bytes 786440 | tf_op jit(solution)/shard_map/ppermute | solution.py:266
  87.6 32.6 %copy-start.3 = (bf16[32,32,128]{2,1,0:T(8,128)(2,1)S(1)}, bf16[32,32,128]{2,1,0:T(8,128)(2,1)}, u32[]{:S(2)}) copy-start(bf16[32,32,128]{2,1,0:T(8,128)(2,1)} %param.5) | copy-start | bytes 786436
  113.2 15.1 %all-to-all-start.4 = ((bf16[32,24,128]{2,1,0:T(8,128)(2,1)}), bf16[32,24,128]{2,1,0:T(8,128)(2,1)S(1)}, u32[]{:S(2)}, u32[]{:S(2)}) async-start(bf16[32,24,128]{2,1,0:T(8,128)(2,1)} %bitcast.10), calls=%async_computation.4 | async-start | bytes 393216 | tf_op jit(solution)/shard_map/all_to_all | solution.py:232

commit v7 on v6

--- a/solution.py
+++ b/solution.py
@@ -123,46 +123,58 @@
     msg_ref[...] = layer_norm_backward(dxn_ref[...], xhat, xinv, 0).astype(BF)
 
 
-def late_kernel(xhat_ref, norm_ref, g2_ref, dout_ref, w_ref, ow_ref, sum_ref, dgate_ref, fac_ref):
+def pack_dx(ref, dx):
+    for t in range(2):
+        parts = [ref[t, :, q].astype(F32).reshape(128, 128) for q in range(4)]
+        for g, part in enumerate(regroup(parts)):
+            dx[pl.ds(128 * g, 128), pl.ds(128 * t, 128)] = part.astype(BF)
+
+
+def late_kernel(
+    own_ref, xhat_ref, norm_ref, g2_ref, dout_ref, w_ref, ow_ref, sum_ref, dgate_ref, fac_ref, dx_ref
+):
+    pack_dx(own_ref, dx_ref)
     w = w_ref[...]
     ow = ow_ref[...].T
     gate_part = jnp.zeros((128, 128), F32)
     out_part = jnp.zeros((128, 128), F32)
-    for s in range(8):
-        normed = norm_ref[s]
-        xnorm = xhat_ref[pl.ds(s, 128, stride=8), :].astype(BF)
-        dgate = (g2_ref[s] * dot(ow, xnorm)).astype(BF)
+    for s in range(0, 8, 2):
+        pair = (s, s + 1)
+        normed = norm_ref[s : s + 2].reshape(256, 128)
+        xnorm = jnp.concatenate([xhat_ref[pl.ds(n, 128, stride=8), :] for n in pair], axis=1).astype(BF)
+        dgate = jnp.concatenate([g2_ref[n] for n in pair], axis=1) * dot(ow, xnorm)
+        dgate = dgate.astype(BF)
         gate_part += dot(dgate, normed)
-        out_part += dot(xnorm, dout_ref[s])
-        dgate_ref[s] = dgate
+        out_part += dot(xnorm, dout_ref[s : s + 2].reshape(256, 128))
         proj = dot(w, normed, ((0,), (1,)))
-        for n in range(2):
-            val = proj[256 * n : 256 * n + 128]
-            sig = jax.nn.sigmoid(proj[256 * n + 128 : 256 * n + 256])
-            fac_ref[s, 256 * n : 256 * n + 128] = sig
-            fac_ref[s, 256 * n + 128 : 256 * n + 256] = val * sig * (1.0 - sig)
+        for m, n in enumerate(pair):
+            lanes = slice(128 * m, 128 * m + 128)
+            dgate_ref[n] = dgate[:, lanes]
+            for k in range(2):
+                val = proj[256 * k : 256 * k + 128, lanes]
+                sig = jax.nn.sigmoid(proj[256 * k + 128 : 256 * k + 256, lanes])
+                fac_ref[n, 256 * k : 256 * k + 128] = sig
+                fac_ref[n, 256 * k + 128 : 256 * k + 256] = val * sig * (1.0 - sig)
     sum_ref[0:128] = gate_part.T.astype(BF)
     sum_ref[128:256] = out_part.astype(BF)
 
 
 def pull_kernel(core_ref, own_ref, other_ref, a_ref, b_ref, msg_ref, dx, held):
-    for n, ref in enumerate((own_ref, other_ref)):
-        half = core_ref[0] if n == 0 else 1 - core_ref[0]
-        for t in range(2):
-            parts = [ref[t, :, q].astype(F32).reshape(128, 128) for q in range(4)]
-            for g, part in enumerate(regroup(parts)):
-                dx[half, pl.ds(128 * g, 128), pl.ds(128 * t, 128)] = part.astype(BF)
-    da = dot(dx[0], b_ref[0]) + dot(dx[1], b_ref[1])
+    core = core_ref[0]
+    pack_dx(other_ref, dx)
+    da = dot(own_ref[...], b_ref[core]) + dot(dx[...], b_ref[1 - core])
     for t in range(2):
         parts = [da[128 * g : 128 * g + 128, 128 * t : 128 * t + 128] for g in range(4)]
         for q, part in enumerate(regroup(parts)):
             held[t, :, :, q, 0:8] = part.reshape(8, 2, 8, 128)
     for half in range(2):
-        db = dot(dx[half], a_ref[...], ((0,), (0,))).reshape(8, 4, 8, 256)
+        place = core if half == 0 else 1 - core
+        part = own_ref[...] if half == 0 else dx[...]
+        db = dot(part, a_ref[...], ((0,), (0,))).reshape(8, 4, 8, 256)
         for t in range(2):
             parts = [db[:, g, :, 128 * t : 128 * t + 128].reshape(64, 128) for g in range(4)]
             for q, part in enumerate(regroup(parts)):
-                held[t, :, half, q, 8:16] = part.reshape(8, 8, 128)
+                held[t, :, place, q, 8:16] = part.reshape(8, 8, 128)
     msg_ref[...] = held[...].astype(BF)
 
 
@@ -264,13 +276,14 @@
     dx = exchange(dx, OWNERS)
     dx = dx.reshape(2, 16, 4, 8, 128)
     other = lax.ppermute(dx, "core", SWAP)
-    sums, dgate, factors = run(
-        late_kernel, [((256, 128), BF), ((8, 128, 128), BF), ((8, 512, 128), F32)],
-        xhat.reshape(1024, 128), normed, g2, dout, in_weight, out_weight, flops=268_000_000,
+    sums, dgate, factors, own = run(
+        late_kernel,
+        [((256, 128), BF), ((8, 128, 128), BF), ((8, 512, 128), F32), ((512, 256), BF)],
+        dx, xhat.reshape(1024, 128), normed, g2, dout, in_weight, out_weight, flops=268_000_000,
     )
     dab = run(
-        pull_kernel, [((2, 8, 2, 4, 16, 128), BF)], core, dx, other, a_own, b_own, scalars=1, after=(sums,),
-        scratch=[pltpu.VMEM((2, 512, 256), BF), pltpu.VMEM((2, 8, 2, 4, 16, 128), F32)], flops=268_000_000,
+        pull_kernel, [((2, 8, 2, 4, 16, 128), BF)], core, own, other, a_own, b_own, scalars=1,
+        scratch=[pltpu.VMEM((512, 256), BF), pltpu.VMEM((2, 8, 2, 4, 16, 128), F32)], flops=268_000_000,
     )
     dab = exchange(dab.reshape(128, 16, 128), OWNERS)
     parts, dproj = run(

time: 152 us -> 152 us (level)
  transfers between devices with their start and end apart: 5 -> 5, of which waited for: 4 -> 5; matrix products, arithmetic and copies ran while one was open for 0% -> 0% of each run, Pallas kernels for 3% -> 3%
where the time goes in v7:
time: 152 us
  blocking collectives  65.9 us (43%)
  starting transfers between devices  38.1 us (25%)
  waiting for transfers between devices  33.4 us (22%)
  Pallas kernels  13.3 us (9%)
    all_to_all x4, blocking collectives, exchange(): return lax.all_to_all(values, axes, 0, 0, tiled=True)  65.9 us
    all_to_all x3, starting transfers between devices, exchange(): return lax.all_to_all(values, axes, 0, 0, tiled=True)  32.2 us
    all_to_all x3, waiting for transfers between devices, exchange(): return lax.all_to_all(values, axes, 0, 0, tiled=True)  32 us
    pallas_call x13, Pallas kernels, run(): pl.pallas_call(lambda *refs: kernel(*refs[skip:]), out_shape=outs, in_spe...  13.3 us
    ppermute x1, starting transfers between devices, per_device(): other = lax.ppermute(dx, 'core', SWAP)  3.4 us
  transfers between devices with their start and end apart: 5, of which 5 were waited for; matrix products, arithmetic and copies ran while one was open for 0% of the time, Pallas kernels for 3%

profile of v7, /device:TPU:1, one launch (start us, length us, event | category | flops | bytes accessed | tf_op | source)
XLA Modules:
  0.0 151.5 jit_solution(11679807121170550555)
XLA Ops:
  0.6 2.8 %shard_map.84 = (bf16[128,16,128]{2,1,0:T(8,128)(2,1)}, bf16[8,128,128]{2,1,0:T(8,128)(2,1)}) custom-call(bf16[4,8,32,128]{3,2,1,0:T(8,128)(2,1)} %bitcast.20, bf16[128,512]{1,0:T(8,128)(2,1)} %refs_1_.3), custom_call_target="tpu_custom_call" | custom-call | flops 134000000 | bytes 1179648 | tf_op jit(solution)/shard_map/pallas_call | solution.py:231
  3.5 16.5 %all-to-all-start = ((bf16[128,16,128]{2,1,0:T(8,128)(2,1)}), bf16[128,16,128]{2,1,0:T(8,128)(2,1)S(1)}, u32[]{:S(2)}, u32[]{:S(2)}) async-start(bf16[128,16,128]{2,1,0:T(8,128)(2,1)} %get-tuple-element.25), calls=%async_computation | async-start | bytes 1048576 | tf_op jit(solution)/shard_map/all_to_all | solution.py:244
  20.0 16.2 %all-to-all-done = bf16[128,16,128]{2,1,0:T(8,128)(2,1)S(1)} async-done(((bf16[128,16,128]{2,1,0:T(8,128)(2,1)}), bf16[128,16,128]{2,1,0:T(8,128)(2,1)S(1)}, u32[]{:S(2)}, u32[]{:S(2)}) %all-to-all-start) | async-done | bytes 524320 | tf_op jit(solution)/shard_map/all_to_all | solution.py:244
  36.2 0.7 shard_map.85
  36.9 2.5 %collective-permute-start = (bf16[768,256]{1,0:T(8,128)(2,1)S(1)}, bf16[768,256]{1,0:T(8,128)(2,1)S(1)}, u32[]{:S(2)}, u32[]{:S(2)}) collective-permute-start(bf16[768,256]{1,0:T(8,128)(2,1)S(1)} %get-tuple-element.28), channel_id=1, source_target_pairs={{0,1},{1,0},{2,3},{3,2},{4,5},{5,4},{6,7},{7,6},{8,9},{9,8},{10,11... | collective-permute-start | bytes 1179656 | tf_op jit(solution)/shard_map/ppermute | solution.py:269
  39.6 1.1 collective-permute-done.refs_1_
  40.7 1.1 shard_map.87
  41.8 8.3 %all-to-all-start.1 = ((bf16[128,8,128]{2,1,0:T(8,128)(2,1)}), bf16[128,8,128]{2,1,0:T(8,128)(2,1)S(1)}, u32[]{:S(2)}, u32[]{:S(2)}) async-start(bf16[128,8,128]{2,1,0:T(8,128)(2,1)} %bitcast.3), calls=%async_computation.1 | async-start | bytes 524288 | tf_op jit(solution)/shard_map/all_to_all | solution.py:244
  50.2 0.9 shard_map.88
  51.1 10.2 %all-to-all-done.1.refs_0_ = bf16[128,8,128]{2,1,0:T(8,128)(2,1)S(1)} async-done(((bf16[128,8,128]{2,1,0:T(8,128)(2,1)}), bf16[128,8,128]{2,1,0:T(8,128)(2,1)S(1)}, u32[]{:S(2)}, u32[]{:S(2)}) %all-to-all-start.1) | async-done | bytes 262176 | tf_op jit(solution)/shard_map/all_to_all | solution.py:244
  61.3 0.5 shard_map.89
  61.8 19.3 %all_to_all.35 = bf16[128,8,128]{2,1,0:T(8,128)(2,1)S(1)} all-to-all(bf16[128,8,128]{2,1,0:T(8,128)(2,1)S(1)} %get-tuple-element.31), channel_id=1, replica_groups=mesh['y'=4,'zh'=4,'zl'=2,'x'=4,'core'=2] {'zl','y','zh','x'}, dimensions={0} | all-to-all | bytes 524288 | tf_op jit(solution)/shard_map/all_to_all | solution.py:244
  81.1 3.4 %collective-permute-start.1 = (bf16[2,16,4,8,128]{4,3,2,1,0:T(8,128)(2,1)S(1)}, bf16[2,16,4,8,128]{4,3,2,1,0:T(8,128)(2,1)S(1)}, u32[]{:S(2)}, u32[]{:S(2)}) collective-permute-start(bf16[2,16,4,8,128]{4,3,2,1,0:T(8,128)(2,1)S(1)} %bitcast.14), channel_id=1, source_target_pairs={{0,1},{1,0},{2,3},{3,2},{4,5},{5,4},{6,7},{7,6},{8,9},{9,8},{10,11... | collective-permute-start | bytes 786440 | tf_op jit(solution)/shard_map/ppermute | solution.py:278
  84.5 0.9 shard_map.90
  85.4 0.3 collective-permute-done.1.refs_2_
  85.7 1.5 shard_map.91
  87.2 23.8 %all_to_all.36.refs_1_ = bf16[128,16,128]{2,1,0:T(8,128)(2,1)S(1)} all-to-all(bf16[128,16,128]{2,1,0:T(8,128)(2,1)S(1)} %bitcast.13), channel_id=1, replica_groups=mesh['y'=4,'zh'=4,'zl'=2,'x'=4,'core'=2] {'zl','y','zh','x'}, dimensions={0} | all-to-all | bytes 1048576 | tf_op jit(solution)/shard_map/all_to_all | solution.py:244
  111.0 1.3 shard_map.92
  112.3 7.4 %all-to-all-start.4 = ((bf16[32,24,128]{2,1,0:T(8,128)(2,1)}), bf16[32,24,128]{2,1,0:T(8,128)(2,1)S(1)}, u32[]{:S(2)}, u32[]{:S(2)}) async-start(bf16[32,24,128]{2,1,0:T(8,128)(2,1)} %bitcast.10), calls=%async_computation.4 | async-start | bytes 393216 | tf_op jit(solution)/shard_map/all_to_all | solution.py:244
  119.8 2.5 %shard_map.93 = (bf16[4,8,32,128]{3,2,1,0:T(8,128)(2,1)}, f32[8,128]{1,0:T(8,128)S(1)}) custom-call(bf16[8,512,128]{2,1,0:T(8,128)(2,1)S(1)} %get-tuple-element.38.refs_0_, bf16[128,512]{1,0:T(8,128)(2,1)S(1)} %copy-done.1, bf16[8,128,128]{2,1,0:T(8,128)(2,1)S(1)} %get-tuple-element.39.refs_2_, bf16[128,128]{1,0:T(8,128)(2,1)S(1)} %copy-done.5, ...), custom_call_target="tpu_custom_call" | custom-call | flops 134000000 | bytes 2002944 | tf_op jit(solution)/shard_map/pallas_call | solution.py:231
  122.3 5.5 %all-to-all-done.4.refs_1_ = bf16[32,24,128]{2,1,0:T(8,128)(2,1)S(1)} async-done(((bf16[32,24,128]{2,1,0:T(8,128)(2,1)}), bf16[32,24,128]{2,1,0:T(8,128)(2,1)S(1)}, u32[]{:S(2)}, u32[]{:S(2)}) %all-to-all-start.4) | async-done | bytes 196640 | tf_op jit(solution)/shard_map/all_to_all | solution.py:244
  127.9 9.7 %all_to_all.37.refs_0_ = bf16[8,24,128]{2,1,0:T(8,128)(2,1)S(1)} all-to-all(bf16[8,24,128]{2,1,0:T(8,128)(2,1)S(1)} %shard_map.94), channel_id=1, replica_groups=mesh['y'=4,'zh'=4,'zl'=2,'x'=4,'core'=2] {'zh','zl'}, dimensions={0} | all-to-all | bytes 98304 | tf_op jit(solution)/shard_map/all_to_all | solution.py:244
  137.6 13.1 %all_to_all.38 = bf16[32,24,128]{2,1,0:T(8,128)(2,1)S(1)} all-to-all(bf16[32,24,128]{2,1,0:T(8,128)(2,1)S(1)} %shard_map.95), channel_id=1, replica_groups=mesh['y'=4,'zh'=4,'zl'=2,'x'=4,'core'=2] {'core','y','x'}, dimensions={0} | all-to-all | bytes 393216 | tf_op jit(solution)/shard_map/all_to_all | solution.py:244
  150.7 0.8 shard_map.96
  (15 shorter events, 0.3 us)
Async XLA Ops:
  3.4 46.7 %copy-start = (bf16[8,128,128]{2,1,0:T(8,128)(2,1)S(1)}, bf16[8,128,128]{2,1,0:T(8,128)(2,1)}, u32[]{:S(2)}) copy-start(bf16[8,128,128]{2,1,0:T(8,128)(2,1)} %get-tuple-element.29.refs_0_.refs_2_.refs_3_) | copy-start | bytes 786436
  3.4 46.7 %copy-start.2 = (bf16[32,32,128]{2,1,0:T(8,128)(2,1)S(1)}, bf16[32,32,128]{2,1,0:T(8,128)(2,1)}, u32[]{:S(2)}) copy-start(bf16[32,32,128]{2,1,0:T(8,128)(2,1)} %param.6) | copy-start | bytes 786436
  3.4 46.7 %copy-start.4 = (bf16[128,128]{1,0:T(8,128)(2,1)S(1)}, bf16[128,128]{1,0:T(8,128)(2,1)}, u32[]{:S(2)}) copy-start(bf16[128,128]{1,0:T(8,128)(2,1)} %refs_6_.1) | copy-start | bytes 98308
  3.5 46.7 %copy-start.5 = (bf16[128,128]{1,0:T(8,128)(2,1)S(1)}, bf16[128,128]{1,0:T(8,128)(2,1)}, u32[]{:S(2)}) copy-start(bf16[128,128]{1,0:T(8,128)(2,1)} %refs_3_.3) | copy-start | bytes 98308
  3.5 32.7 %all-to-all-start = ((bf16[128,16,128]{2,1,0:T(8,128)(2,1)}), bf16[128,16,128]{2,1,0:T(8,128)(2,1)S(1)}, u32[]{:S(2)}, u32[]{:S(2)}) async-start(bf16[128,16,128]{2,1,0:T(8,128)(2,1)} %get-tuple-element.25), calls=%async_computation | async-start | bytes 1048576 | tf_op jit(solution)/shard_map/all_to_all | solution.py:244
  36.9 3.8 %collective-permute-start = (bf16[768,256]{1,0:T(8,128)(2,1)S(1)}, bf16[768,256]{1,0:T(8,128)(2,1)S(1)}, u32[]{:S(2)}, u32[]{:S(2)}) collective-permute-start(bf16[768,256]{1,0:T(8,128)(2,1)S(1)} %get-tuple-element.28), channel_id=1, source_target_pairs={{0,1},{1,0},{2,3},{3,2},{4,5},{5,4},{6,7},{7,6},{8,9},{9,8},{10,11... | collective-permute-start | bytes 1179656 | tf_op jit(solution)/shard_map/ppermute | solution.py:269
  39.4 45.2 %copy-start.1 = (bf16[128,512]{1,0:T(8,128)(2,1)S(1)}, bf16[128,512]{1,0:T(8,128)(2,1)}, u32[]{:S(2)}) copy-start(bf16[128,512]{1,0:T(8,128)(2,1)} %refs_1_.3) | copy-start | bytes 393220
  41.8 19.5 %all-to-all-start.1 = ((bf16[128,8,128]{2,1,0:T(8,128)(2,1)}), bf16[128,8,128]{2,1,0:T(8,128)(2,1)S(1)}, u32[]{:S(2)}, u32[]{:S(2)}) async-start(bf16[128,8,128]{2,1,0:T(8,128)(2,1)} %bitcast.3), calls=%async_computation.1 | async-start | bytes 524288 | tf_op jit(solution)/shard_map/all_to_all | solution.py:244
  81.1 4.6 %collective-permute-start.1 = (bf16[2,16,4,8,128]{4,3,2,1,0:T(8,128)(2,1)S(1)}, bf16[2,16,4,8,128]{4,3,2,1,0:T(8,128)(2,1)S(1)}, u32[]{:S(2)}, u32[]{:S(2)}) collective-permute-start(bf16[2,16,4,8,128]{4,3,2,1,0:T(8,128)(2,1)S(1)} %bitcast.14), channel_id=1, source_target_pairs={{0,1},{1,0},{2,3},{3,2},{4,5},{5,4},{6,7},{7,6},{8,9},{9,8},{10,11... | collective-permute-start | bytes 786440 | tf_op jit(solution)/shard_map/ppermute | solution.py:278
  87.2 32.6 %copy-start.3 = (bf16[32,32,128]{2,1,0:T(8,128)(2,1)S(1)}, bf16[32,32,128]{2,1,0:T(8,128)(2,1)}, u32[]{:S(2)}) copy-start(bf16[32,32,128]{2,1,0:T(8,128)(2,1)} %param.5) | copy-start | bytes 786436
  112.3 15.5 %all-to-all-start.4 = ((bf16[32,24,128]{2,1,0:T(8,128)(2,1)}), bf16[32,24,128]{2,1,0:T(8,128)(2,1)S(1)}, u32[]{:S(2)}, u32[]{:S(2)}) async-start(bf16[32,24,128]{2,1,0:T(8,128)(2,1)} %bitcast.10), calls=%async_computation.4 | async-start | bytes 393216 | tf_op jit(solution)/shard_map/all_to_all | solution.py:244

commit v8 on v7

--- a/solution.py
+++ b/solution.py
@@ -59,7 +59,10 @@
         copy.wait()
     w = w_ref[...]
     pair = jnp.concatenate([pair_ref[:, s].astype(F32).reshape(128, 128) for s in range(8)], axis=0)
-    normed = layer_norm(pair)[0].astype(BF)
+    ones = jnp.full((128, 128), 1.0, BF)
+    center = pair - dot(pair.astype(BF), ones) * (1.0 / 128)
+    scale = lax.rsqrt(jnp.mean(center * center, axis=-1, keepdims=True) + EPS)
+    normed = (center * scale).astype(BF)
     norm_ref[...] = normed.reshape(8, 128, 128)
     for n in range(2):
         val = dot(w[:, 256 * n : 256 * n + 128], normed, ((0,), (1,)))

time: 152 us -> 152 us (level)
  no operation moved by 1% of the time
where the time goes in v8:
time: 152 us
  blocking collectives  65.9 us (43%)
  starting transfers between devices  38 us (25%)
  waiting for transfers between devices  33.4 us (22%)
  Pallas kernels  13.3 us (9%)
    all_to_all x4, blocking collectives, exchange(): return lax.all_to_all(values, axes, 0, 0, tiled=True)  65.9 us
    all_to_all x3, starting transfers between devices, exchange(): return lax.all_to_all(values, axes, 0, 0, tiled=True)  32.2 us
    all_to_all x3, waiting for transfers between devices, exchange(): return lax.all_to_all(values, axes, 0, 0, tiled=True)  32.1 us
    pallas_call x13, Pallas kernels, run(): pl.pallas_call(lambda *refs: kernel(*refs[skip:]), out_shape=outs, in_spe...  13.3 us
    ppermute x1, starting transfers between devices, per_device(): other = lax.ppermute(dx, 'core', SWAP)  3.39 us
  transfers between devices with their start and end apart: 5, of which 5 were waited for; matrix products, arithmetic and copies ran while one was open for 0% of the time, Pallas kernels for 3%

profile of v8, /device:TPU:1, one launch (start us, length us, event | category | flops | bytes accessed | tf_op | source)
XLA Modules:
  0.0 151.5 jit_solution(11799291843032397516)
XLA Ops:
  0.6 2.7 %shard_map.84 = (bf16[128,16,128]{2,1,0:T(8,128)(2,1)}, bf16[8,128,128]{2,1,0:T(8,128)(2,1)}) custom-call(bf16[4,8,32,128]{3,2,1,0:T(8,128)(2,1)} %bitcast.20, bf16[128,512]{1,0:T(8,128)(2,1)} %refs_1_.3), custom_call_target="tpu_custom_call" | custom-call | flops 134000000 | bytes 1179648 | tf_op jit(solution)/shard_map/pallas_call | solution.py:234
  3.4 16.5 %all-to-all-start = ((bf16[128,16,128]{2,1,0:T(8,128)(2,1)}), bf16[128,16,128]{2,1,0:T(8,128)(2,1)S(1)}, u32[]{:S(2)}, u32[]{:S(2)}) async-start(bf16[128,16,128]{2,1,0:T(8,128)(2,1)} %get-tuple-element.25), calls=%async_computation | async-start | bytes 1048576 | tf_op jit(solution)/shard_map/all_to_all | solution.py:247
  19.9 16.2 %all-to-all-done = bf16[128,16,128]{2,1,0:T(8,128)(2,1)S(1)} async-done(((bf16[128,16,128]{2,1,0:T(8,128)(2,1)}), bf16[128,16,128]{2,1,0:T(8,128)(2,1)S(1)}, u32[]{:S(2)}, u32[]{:S(2)}) %all-to-all-start) | async-done | bytes 524320 | tf_op jit(solution)/shard_map/all_to_all | solution.py:247
  36.1 0.7 shard_map.85
  36.8 2.5 %collective-permute-start = (bf16[768,256]{1,0:T(8,128)(2,1)S(1)}, bf16[768,256]{1,0:T(8,128)(2,1)S(1)}, u32[]{:S(2)}, u32[]{:S(2)}) collective-permute-start(bf16[768,256]{1,0:T(8,128)(2,1)S(1)} %get-tuple-element.28), channel_id=1, source_target_pairs={{0,1},{1,0},{2,3},{3,2},{4,5},{5,4},{6,7},{7,6},{8,9},{9,8},{10,11... | collective-permute-start | bytes 1179656 | tf_op jit(solution)/shard_map/ppermute | solution.py:272
  39.6 1.1 collective-permute-done.refs_1_
  40.7 1.1 shard_map.87
  41.8 8.3 %all-to-all-start.1 = ((bf16[128,8,128]{2,1,0:T(8,128)(2,1)}), bf16[128,8,128]{2,1,0:T(8,128)(2,1)S(1)}, u32[]{:S(2)}, u32[]{:S(2)}) async-start(bf16[128,8,128]{2,1,0:T(8,128)(2,1)} %bitcast.3), calls=%async_computation.1 | async-start | bytes 524288 | tf_op jit(solution)/shard_map/all_to_all | solution.py:247
  50.1 0.9 shard_map.88
  51.0 10.3 %all-to-all-done.1.refs_0_ = bf16[128,8,128]{2,1,0:T(8,128)(2,1)S(1)} async-done(((bf16[128,8,128]{2,1,0:T(8,128)(2,1)}), bf16[128,8,128]{2,1,0:T(8,128)(2,1)S(1)}, u32[]{:S(2)}, u32[]{:S(2)}) %all-to-all-start.1) | async-done | bytes 262176 | tf_op jit(solution)/shard_map/all_to_all | solution.py:247
  61.3 0.5 shard_map.89
  61.8 19.3 %all_to_all.35 = bf16[128,8,128]{2,1,0:T(8,128)(2,1)S(1)} all-to-all(bf16[128,8,128]{2,1,0:T(8,128)(2,1)S(1)} %get-tuple-element.31), channel_id=1, replica_groups=mesh['y'=4,'zh'=4,'zl'=2,'x'=4,'core'=2] {'zl','y','zh','x'}, dimensions={0} | all-to-all | bytes 524288 | tf_op jit(solution)/shard_map/all_to_all | solution.py:247
  81.1 3.4 %collective-permute-start.1 = (bf16[2,16,4,8,128]{4,3,2,1,0:T(8,128)(2,1)S(1)}, bf16[2,16,4,8,128]{4,3,2,1,0:T(8,128)(2,1)S(1)}, u32[]{:S(2)}, u32[]{:S(2)}) collective-permute-start(bf16[2,16,4,8,128]{4,3,2,1,0:T(8,128)(2,1)S(1)} %bitcast.14), channel_id=1, source_target_pairs={{0,1},{1,0},{2,3},{3,2},{4,5},{5,4},{6,7},{7,6},{8,9},{9,8},{10,11... | collective-permute-start | bytes 786440 | tf_op jit(solution)/shard_map/ppermute | solution.py:281
  84.5 0.9 shard_map.90
  85.4 0.3 collective-permute-done.1.refs_2_
  85.7 1.5 shard_map.91
  87.2 23.8 %all_to_all.36.refs_1_ = bf16[128,16,128]{2,1,0:T(8,128)(2,1)S(1)} all-to-all(bf16[128,16,128]{2,1,0:T(8,128)(2,1)S(1)} %bitcast.13), channel_id=1, replica_groups=mesh['y'=4,'zh'=4,'zl'=2,'x'=4,'core'=2] {'zl','y','zh','x'}, dimensions={0} | all-to-all | bytes 1048576 | tf_op jit(solution)/shard_map/all_to_all | solution.py:247
  111.0 1.3 shard_map.92
  112.3 7.4 %all-to-all-start.4 = ((bf16[32,24,128]{2,1,0:T(8,128)(2,1)}), bf16[32,24,128]{2,1,0:T(8,128)(2,1)S(1)}, u32[]{:S(2)}, u32[]{:S(2)}) async-start(bf16[32,24,128]{2,1,0:T(8,128)(2,1)} %bitcast.10), calls=%async_computation.4 | async-start | bytes 393216 | tf_op jit(solution)/shard_map/all_to_all | solution.py:247
  119.8 2.5 %shard_map.93 = (bf16[4,8,32,128]{3,2,1,0:T(8,128)(2,1)}, f32[8,128]{1,0:T(8,128)S(1)}) custom-call(bf16[8,512,128]{2,1,0:T(8,128)(2,1)S(1)} %get-tuple-element.38.refs_0_, bf16[128,512]{1,0:T(8,128)(2,1)S(1)} %copy-done.1, bf16[8,128,128]{2,1,0:T(8,128)(2,1)S(1)} %get-tuple-element.39.refs_2_, bf16[128,128]{1,0:T(8,128)(2,1)S(1)} %copy-done.5, ...), custom_call_target="tpu_custom_call" | custom-call | flops 134000000 | bytes 2002944 | tf_op jit(solution)/shard_map/pallas_call | solution.py:234
  122.3 5.5 %all-to-all-done.4.refs_1_ = bf16[32,24,128]{2,1,0:T(8,128)(2,1)S(1)} async-done(((bf16[32,24,128]{2,1,0:T(8,128)(2,1)}), bf16[32,24,128]{2,1,0:T(8,128)(2,1)S(1)}, u32[]{:S(2)}, u32[]{:S(2)}) %all-to-all-start.4) | async-done | bytes 196640 | tf_op jit(solution)/shard_map/all_to_all | solution.py:247
  127.9 9.7 %all_to_all.37.refs_0_ = bf16[8,24,128]{2,1,0:T(8,128)(2,1)S(1)} all-to-all(bf16[8,24,128]{2,1,0:T(8,128)(2,1)S(1)} %shard_map.94), channel_id=1, replica_groups=mesh['y'=4,'zh'=4,'zl'=2,'x'=4,'core'=2] {'zh','zl'}, dimensions={0} | all-to-all | bytes 98304 | tf_op jit(solution)/shard_map/all_to_all | solution.py:247
  137.6 13.1 %all_to_all.38 = bf16[32,24,128]{2,1,0:T(8,128)(2,1)S(1)} all-to-all(bf16[32,24,128]{2,1,0:T(8,128)(2,1)S(1)} %shard_map.95), channel_id=1, replica_groups=mesh['y'=4,'zh'=4,'zl'=2,'x'=4,'core'=2] {'core','y','x'}, dimensions={0} | all-to-all | bytes 393216 | tf_op jit(solution)/shard_map/all_to_all | solution.py:247
  150.7 0.8 shard_map.96
  (15 shorter events, 0.4 us)
Async XLA Ops:
  3.4 46.7 %copy-start = (bf16[8,128,128]{2,1,0:T(8,128)(2,1)S(1)}, bf16[8,128,128]{2,1,0:T(8,128)(2,1)}, u32[]{:S(2)}) copy-start(bf16[8,128,128]{2,1,0:T(8,128)(2,1)} %get-tuple-element.29.refs_0_.refs_2_.refs_3_) | copy-start | bytes 786436
  3.4 46.7 %copy-start.2 = (bf16[32,32,128]{2,1,0:T(8,128)(2,1)S(1)}, bf16[32,32,128]{2,1,0:T(8,128)(2,1)}, u32[]{:S(2)}) copy-start(bf16[32,32,128]{2,1,0:T(8,128)(2,1)} %param.6) | copy-start | bytes 786436
  3.4 46.7 %copy-start.4 = (bf16[128,128]{1,0:T(8,128)(2,1)S(1)}, bf16[128,128]{1,0:T(8,128)(2,1)}, u32[]{:S(2)}) copy-start(bf16[128,128]{1,0:T(8,128)(2,1)} %refs_6_.1) | copy-start | bytes 98308
  3.4 46.7 %copy-start.5 = (bf16[128,128]{1,0:T(8,128)(2,1)S(1)}, bf16[128,128]{1,0:T(8,128)(2,1)}, u32[]{:S(2)}) copy-start(bf16[128,128]{1,0:T(8,128)(2,1)} %refs_3_.3) | copy-start | bytes 98308
  3.4 32.7 %all-to-all-start = ((bf16[128,16,128]{2,1,0:T(8,128)(2,1)}), bf16[128,16,128]{2,1,0:T(8,128)(2,1)S(1)}, u32[]{:S(2)}, u32[]{:S(2)}) async-start(bf16[128,16,128]{2,1,0:T(8,128)(2,1)} %get-tuple-element.25), calls=%async_computation | async-start | bytes 1048576 | tf_op jit(solution)/shard_map/all_to_all | solution.py:247
  36.8 3.8 %collective-permute-start = (bf16[768,256]{1,0:T(8,128)(2,1)S(1)}, bf16[768,256]{1,0:T(8,128)(2,1)S(1)}, u32[]{:S(2)}, u32[]{:S(2)}) collective-permute-start(bf16[768,256]{1,0:T(8,128)(2,1)S(1)} %get-tuple-element.28), channel_id=1, source_target_pairs={{0,1},{1,0},{2,3},{3,2},{4,5},{5,4},{6,7},{7,6},{8,9},{9,8},{10,11... | collective-permute-start | bytes 1179656 | tf_op jit(solution)/shard_map/ppermute | solution.py:272
  39.3 45.2 %copy-start.1 = (bf16[128,512]{1,0:T(8,128)(2,1)S(1)}, bf16[128,512]{1,0:T(8,128)(2,1)}, u32[]{:S(2)}) copy-start(bf16[128,512]{1,0:T(8,128)(2,1)} %refs_1_.3) | copy-start | bytes 393220
  41.8 19.5 %all-to-all-start.1 = ((bf16[128,8,128]{2,1,0:T(8,128)(2,1)}), bf16[128,8,128]{2,1,0:T(8,128)(2,1)S(1)}, u32[]{:S(2)}, u32[]{:S(2)}) async-start(bf16[128,8,128]{2,1,0:T(8,128)(2,1)} %bitcast.3), calls=%async_computation.1 | async-start | bytes 524288 | tf_op jit(solution)/shard_map/all_to_all | solution.py:247
  81.1 4.6 %collective-permute-start.1 = (bf16[2,16,4,8,128]{4,3,2,1,0:T(8,128)(2,1)S(1)}, bf16[2,16,4,8,128]{4,3,2,1,0:T(8,128)(2,1)S(1)}, u32[]{:S(2)}, u32[]{:S(2)}) collective-permute-start(bf16[2,16,4,8,128]{4,3,2,1,0:T(8,128)(2,1)S(1)} %bitcast.14), channel_id=1, source_target_pairs={{0,1},{1,0},{2,3},{3,2},{4,5},{5,4},{6,7},{7,6},{8,9},{9,8},{10,11... | collective-permute-start | bytes 786440 | tf_op jit(solution)/shard_map/ppermute | solution.py:281
  87.1 32.6 %copy-start.3 = (bf16[32,32,128]{2,1,0:T(8,128)(2,1)S(1)}, bf16[32,32,128]{2,1,0:T(8,128)(2,1)}, u32[]{:S(2)}) copy-start(bf16[32,32,128]{2,1,0:T(8,128)(2,1)} %param.5) | copy-start | bytes 786436
  112.3 15.5 %all-to-all-start.4 = ((bf16[32,24,128]{2,1,0:T(8,128)(2,1)}), bf16[32,24,128]{2,1,0:T(8,128)(2,1)S(1)}, u32[]{:S(2)}, u32[]{:S(2)}) async-start(bf16[32,24,128]{2,1,0:T(8,128)(2,1)} %bitcast.10), calls=%async_computation.4 | async-start | bytes 393216 | tf_op jit(solution)/shard_map/all_to_all | solution.py:247
